TPU v7x, 32 devices: a whole 2x2x4 slice. The times are simulated.
32 devices in a mesh: groups: 2 (over x), shot: 16 (over z, y, core).
Axes of the slice: x: 2, y: 2, z: 4, core: 2. Of those that a mesh axis runs over, the one named last changes fastest.
Arguments:
- spectra: bfloat16 [1024, 2, 64, 512], P(('groups', 'shot')), parts along dimension 0, may hold values from -1.1953125 to 1.1953125
- fold_counts: int32 [1024], P('groups'), parts along dimension 0, may hold values from 1 to 512
- inverse_wavelet: float32 [2, 64], replicated, may hold values from -4 to 4
Outputs:
- multiples: bfloat16 [1024, 2, 64, 512], P(('groups', 'shot')), parts along dimension 0
There are 2 independent parts, one for each index of `groups`. A program takes and returns all parts, laid end to end along the dimension named above; an argument that names none is the same for every part. Nothing has to cross between parts.
All inputs are finite; a program needn't handle non-finite values.
Results may differ from a plain program's by a relative error of at most 0.001.
Values may be sent and summed in bfloat16 or wider, within the bound.
No kernel may reach another device: no remote copies, remote signals or barrier semaphores. Data moves between devices by JAX's collectives and lax.ppermute only.
A program may use at most 64 MiB of HBM per device.

v0:
```python
import jax
import jax.numpy as jnp
from jax import lax
from jax.sharding import PartitionSpec as P


def batched_product(left_operand, right_operand):
    return jnp.einsum(
        "hwi,iwc->hwc", left_operand, right_operand, preferred_element_type=jnp.float32
    )


def shards(spectra, fold_counts, inverse_wavelet):
    points = spectra.shape[3]
    everyone = jnp.arange(points, dtype=jnp.int32)
    regrouped = lax.all_to_all(spectra, "shot", split_axis=2, concat_axis=0, tiled=True)
    recorded = jnp.abs(everyone[None, :] - everyone[:, None]) < fold_counts[:, None]
    flipped = regrouped.transpose(3, 1, 2, 0)
    regrouped = jnp.where(
        recorded[:, None, None, :],
        regrouped,
        jnp.where(recorded.T[:, None, None, :], flipped, jnp.zeros_like(regrouped)),
    )
    local_bins = regrouped.shape[2]
    real_component = regrouped[:, 0]
    imaginary_component = regrouped[:, 1]
    prod_real = batched_product(real_component, real_component) - batched_product(
        imaginary_component, imaginary_component
    )
    prod_imag = batched_product(real_component, imaginary_component) + batched_product(
        imaginary_component, real_component
    )
    first_bin = lax.axis_index("shot") * local_bins
    wave = lax.dynamic_slice_in_dim(inverse_wavelet, first_bin, local_bins, 1)
    wavelet_real = wave[0][None, :, None]
    wave_imag = wave[1][None, :, None]
    output_real = -(wavelet_real * prod_real - wave_imag * prod_imag)
    out_imag = -(wavelet_real * prod_imag + wave_imag * prod_real)
    result = jnp.stack([output_real, out_imag], axis=1).astype(jnp.bfloat16)
    return lax.all_to_all(result, "shot", split_axis=0, concat_axis=2, tiled=True)


def solution(mesh):
    in_specs = (P(("groups", "shot"), None, None, None), P("groups"), P())
    out_specs = P(("groups", "shot"), None, None, None)
    return jax.shard_map(shards, mesh=mesh, in_specs=in_specs, out_specs=out_specs, check_vma=False)
```

profile of v0, /device:TPU:0, one launch (start us, length us, event | category | flops | bytes accessed | tf_op | source)
XLA Modules:
  0.0 245.2 jit_solution(15204879253858754187)
XLA Ops:
  0.0 0.0 copy-start
  0.0 6.6 %copy.27 = bf16[32,2,64,512]{3,0,1,2:T(8,128)(2,1)} copy(bf16[32,2,64,512]{3,2,1,0:T(8,128)(2,1)} %param.3) | data formatting | bytes 8388608 | tf_op args[0]
  6.6 0.0 copy-start.2
  6.6 7.6 %all-to-all-start = ((bf16[32,2,64,512]{3,0,1,2:T(8,128)(2,1)}), bf16[32,2,64,512]{3,0,1,2:T(8,128)(2,1)}, u32[]{:S(2)}, u32[]{:S(2)}) async-start(bf16[32,2,64,512]{3,0,1,2:T(8,128)(2,1)} %copy.27), calls=%async_computation | async-start | bytes 8388608 | tf_op jit(solution)/shard_map/all_to_all | solution.py:16
  14.2 0.0 copy-done
  14.2 0.1 constant_dynamic-slice_fusion
  14.2 0.0 copy-done.2
  14.2 0.5 abs_compare_fusion.1
  14.7 77.1 %all-to-all-done = bf16[32,2,64,512]{3,0,1,2:T(8,128)(2,1)} async-done(((bf16[32,2,64,512]{3,0,1,2:T(8,128)(2,1)}), bf16[32,2,64,512]{3,0,1,2:T(8,128)(2,1)}, u32[]{:S(2)}, u32[]{:S(2)}) %all-to-all-start) | async-done | bytes 4194336 | tf_op jit(solution)/shard_map/all_to_all | solution.py:16
  91.8 4.8 %copy.29 = bf16[16,32,2,4,512]{4,1,0,3,2:T(8,128)(2,1)} copy(bf16[16,32,2,4,512]{4,1,2,3,0:T(8,128)(2,1)} %bitcast.3) | data formatting | bytes 8388608 | tf_op jit(solution)/shard_map/all_to_all | solution.py:16
  96.6 7.3 %copy.30 = bf16[512,2,4,512]{0,3,2,1:T(8,128)(2,1)} copy(bf16[512,2,4,512]{3,0,2,1:T(8,128)(2,1)} %bitcast.37) | data formatting | bytes 8388608 | tf_op jit(solution)/shard_map/all_to_all | solution.py:16
  103.9 5.1 %fusion = bf16[512,2,4,512]{3,0,2,1:T(8,128)(2,1)S(1)} fusion(bf16[512,2,4,512]{0,3,2,1:T(8,128)(2,1)} %copy.30, pred[512,512]{1,0:T(8,128)(4,1)S(1)} %get-tuple-element.8, pred[512,512]{1,0:T(8,128)(4,1)S(1)} %get-tuple-element.7, bf16[16,32,2,4,512]{4,1,0,3,2:T(8,128)(2,1)} %copy.29), kind=kLoop, calls=%fused_computation.2 | loop fusion | flops 4194304 | bytes 13107200 | tf_op jit(solution)/shard_map/jit(_where)/select_n | solution.py:19
  109.0 1.5 fusion.3
  110.5 1.5 fusion.4
  112.1 1.6 convolution_add_fusion
  113.6 2.9 %fusion.1 = (bf16[512,1,4,512]{0,3,2,1:T(8,128)(2,1)S(1)}, bf16[512,1,4,512]{0,3,2,1:T(8,128)(2,1)S(1)}) fusion(f32[4,512,512]{2,1,0:T(8,128)S(1)} %convolution_add_fusion, f32[4]{0:T(128)S(1)} %get-tuple-element.10, f32[4]{0:T(128)S(1)} %get-tuple-element.9, f32[4,512,512]{2,1,0:T(8,128)S(1)} %fusion.4, bf16[512,2,4,512]{3,0,2,1:T(8,128)(2,1)S(1)} %fusion), kind=kOutput, calls=%fused_computation.7 | convolution fusion | flops 1085276160 | bytes 14681088 | tf_op jit(solution)/shard_map/hwi,iwc->hwc/dot_general | solution.py:8
  116.6 2.4 pad_maximum_fusion
  119.0 7.9 %copy.35 = bf16[512,2,4,512]{3,2,1,0:T(4,128)(2,1)} copy(bf16[512,2,4,512]{0,3,2,1:T(8,128)(2,1)} %pad_maximum_fusion) | data formatting | bytes 8388608 | tf_op jit(solution)/shard_map/stack | solution.py:39
  126.8 111.9 %all_to_all.36 = bf16[512,2,4,512]{3,2,1,0:T(4,128)(2,1)S(1)} all-to-all(bf16[512,2,4,512]{3,2,1,0:T(4,128)(2,1)} %copy.35), channel_id=1, replica_groups=mesh['groups'=2,'shot'=16] {'shot'}, dimensions={0} | all-to-all | bytes 8388608 | tf_op jit(solution)/shard_map/all_to_all | solution.py:40
  238.7 1.5 copy.36
  240.3 0.6 copy.37
  240.8 0.0 copy-start.1
  240.9 4.4 %copy.38 = bf16[32,2,64,512]{3,2,1,0:T(8,128)(2,1)} copy(bf16[32,2,64,512]{3,0,2,1:T(8,128)(2,1)S(1)} %bitcast.39) | data formatting | bytes 8388608 | tf_op jit(solution)/shard_map/all_to_all | solution.py:40
  245.2 0.0 copy-done.1
  (1 shorter events, 0.0 us)
Async XLA Ops:
  0.0 14.2 %copy-start = (f32[2,64]{1,0:T(2,128)S(1)}, f32[2,64]{1,0:T(2,128)}, u32[]{:S(2)}) copy-start(f32[2,64]{1,0:T(2,128)} %param.5) | copy-start | bytes 1540
  6.6 7.7 %copy-start.2 = (s32[512]{0:T(512)S(1)}, s32[512]{0:T(512)}, u32[]{:S(2)}) copy-start(s32[512]{0:T(512)} %param.4) | copy-start | bytes 6148
  6.6 85.3 %all-to-all-start = ((bf16[32,2,64,512]{3,0,1,2:T(8,128)(2,1)}), bf16[32,2,64,512]{3,0,1,2:T(8,128)(2,1)}, u32[]{:S(2)}, u32[]{:S(2)}) async-start(bf16[32,2,64,512]{3,0,1,2:T(8,128)(2,1)} %copy.27), calls=%async_computation | async-start | bytes 8388608 | tf_op jit(solution)/shard_map/all_to_all | solution.py:16
  240.8 4.4 %copy-start.1 = (f32[2,64]{1,0:T(2,128)S(1)}, f32[2,64]{1,0:T(2,128)}, u32[]{:S(2)}) copy-start(f32[2,64]{1,0:T(2,128)} %param.5) | copy-start | bytes 1540
where the time goes:
time: 246 us; the launch traced here: 245 us
  blocking collectives  112 us (46%)
  waiting for transfers between devices  77.1 us (31%)
  local copies, waits for them, and re-layouts  33.1 us (13%)
  other arithmetic  8 us (3%)
  starting transfers between devices  7.58 us (3%)
  matrix products  7.55 us (3%)
    all_to_all x1, blocking collectives, shards(): lax.all_to_all(result, 'shot', split_axis=0, concat_axis=2, tiled=True)  112 us
    all_to_all x1, waiting for transfers between devices, shards(): lax.all_to_all(spectra, 'shot', split_axis=2, concat_axis=0, tiled=True)  77.1 us
    all_to_all x2, local copies, waits for them, and re-layouts, shards(): lax.all_to_all(spectra, 'shot', split_axis=2, concat_axis=0, tiled=True)  12.1 us
    another operation x1, local copies, waits for them, and re-layouts, shards(): result = jnp.stack([output_real, out_imag], axis=1).astype(jnp.bfloat16)  7.87 us
    all_to_all x1, starting transfers between devices, shards(): lax.all_to_all(spectra, 'shot', split_axis=2, concat_axis=0, tiled=True)  7.58 us
    dot_general x4, matrix products, batched_product(): jnp.einsum('hwi,iwc->hwc', left_operand, right_operand, preferred_element...  7.55 us
    unnamed x7, local copies, waits for them, and re-layouts  6.57 us
    all_to_all x3, local copies, waits for them, and re-layouts, shards(): lax.all_to_all(result, 'shot', split_axis=0, concat_axis=2, tiled=True)  6.48 us
  transfers between devices with their start and end apart: 1, of which 1 were waited for; matrix products, arithmetic and copies ran while one was open for 0% of the time, Pallas kernels for 0%

commit v1 on v0

--- a/solution.py
+++ b/solution.py
@@ -1,7 +1,14 @@
+import functools
+
 import jax
 import jax.numpy as jnp
 from jax import lax
+from jax.experimental import pallas as pl
+from jax.experimental.pallas import tpu as pltpu
 from jax.sharding import PartitionSpec as P
+
+PLANE = 4
+VMEM_LIMIT = 32 * 1024 * 1024
 
 
 def batched_product(left_operand, right_operand):
@@ -10,7 +17,7 @@
     )
 
 
-def shards(spectra, fold_counts, inverse_wavelet):
+def plain_shards(spectra, fold_counts, inverse_wavelet):
     points = spectra.shape[3]
     everyone = jnp.arange(points, dtype=jnp.int32)
     regrouped = lax.all_to_all(spectra, "shot", split_axis=2, concat_axis=0, tiled=True)
@@ -40,7 +47,225 @@
     return lax.all_to_all(result, "shot", split_axis=0, concat_axis=2, tiled=True)
 
 
+def any_spec():
+    return pl.BlockSpec(memory_space=pl.ANY)
+
+
+def vmem_spec():
+    return pl.BlockSpec(memory_space=pltpu.VMEM)
+
+
+def smem_spec():
+    return pl.BlockSpec(memory_space=pltpu.SMEM)
+
+
+def params():
+    return pltpu.CompilerParams(vmem_limit_bytes=VMEM_LIMIT)
+
+
+def cost(flops, bytes_accessed):
+    return pl.CostEstimate(
+        flops=flops, bytes_accessed=bytes_accessed, transcendentals=0
+    )
+
+
+def split_order(me, n, shots, transposed):
+    rows = n * shots
+    a = lax.broadcasted_iota(jnp.int32, (rows, rows), 1 if transposed else 0)
+    b = lax.broadcasted_iota(jnp.int32, (rows, rows), 0 if transposed else 1)
+    source = (a % shots) * n + ((a // shots) ^ me)
+    return jnp.where(source == b, 1.0, 0.0).astype(jnp.bfloat16)
+
+
+def relayout_kernel(n, shots, me_ref, x_ref, *refs):
+    outs = refs[-(n // PLANE) :]
+    me = me_ref[0]
+    order = split_order(me, n, shots, False)
+    points = x_ref.shape[3]
+    for c in range(2):
+        rows = x_ref[:, c].reshape(shots * n, points)
+        moved = jnp.dot(order, rows, preferred_element_type=jnp.float32)
+        moved = moved.astype(jnp.bfloat16).reshape(n // PLANE, PLANE, shots, points)
+        for j, out in enumerate(outs):
+            out[:, c] = moved[j]
+
+
+def relayout(me, spectra, k, n, after):
+    shots, _, _, points = spectra.shape
+    planes = n // PLANE
+    block = jax.ShapeDtypeStruct((PLANE, 2, shots, points), spectra.dtype)
+    size = 2 * n * shots * points * 2
+    return pl.pallas_call(
+        functools.partial(relayout_kernel, n, shots),
+        grid=(1,),
+        out_shape=[block] * planes,
+        in_specs=[
+            smem_spec(),
+            pl.BlockSpec((shots, 2, n, points), lambda _: (0, 0, k, 0)),
+        ]
+        + [any_spec()] * len(after),
+        out_specs=[pl.BlockSpec(block.shape, lambda _: (0, 0, 0, 0))] * planes,
+        compiler_params=params(),
+        cost_estimate=cost(4 * (n * shots) ** 2 * points, 2 * size),
+        name="relayout",
+    )(me, spectra, *after)
+
+
+def swap_kernel(count_in, *refs):
+    ins, outs = refs[:count_in], refs[count_in:]
+    for i, out in enumerate(outs):
+        for j, block in enumerate(ins):
+            out[j] = block[i]
+
+
+def swap(blocks):
+    count_in, count_out = len(blocks), blocks[0].shape[0]
+    shape = jax.ShapeDtypeStruct((count_in, *blocks[0].shape[1:]), blocks[0].dtype)
+    size = 2 * count_out * shape.size
+    return pl.pallas_call(
+        functools.partial(swap_kernel, count_in),
+        out_shape=[shape] * count_out,
+        in_specs=[vmem_spec()] * count_in,
+        out_specs=[vmem_spec()] * count_out,
+        compiler_params=params(),
+        cost_estimate=cost(0, 2 * size),
+        name="swap",
+    )(*blocks)
+
+
+def product_kernel(k, n, me_ref, wave_ref, fold_row_ref, fold_col_ref, *refs):
+    ins, outs = refs[:PLANE], refs[PLANE : 2 * PLANE]
+    a_ref, o_ref = refs[2 * PLANE :]
+    me = me_ref[0]
+    planes, _, shots, points = ins[0].shape
+
+    def rows_of(j, i):
+        start = ((PLANE * j + i) ^ me) * shots
+        return pl.ds(pl.multiple_of(start, shots), shots)
+
+    for j in range(planes):
+        for i in range(PLANE):
+            for c in range(2):
+                a_ref[c, rows_of(j, i), :] = ins[i][j, c]
+    s = lax.broadcasted_iota(jnp.int32, (points, points), 0)
+    x = lax.broadcasted_iota(jnp.int32, (points, points), 1)
+    apart = jnp.abs(x - s)
+    recorded = apart < fold_col_ref[...]
+    mirrored = apart < fold_row_ref[...]
+
+    def fill(c):
+        own = a_ref[c].astype(jnp.float32)
+        return jnp.where(
+            recorded, own, jnp.where(mirrored, own.T, 0.0)
+        ).astype(jnp.bfloat16)
+
+    re, im = fill(0), fill(1)
+
+    def dot(left, right):
+        return jnp.dot(left, right, preferred_element_type=jnp.float32)
+
+    prod_re = dot(re, re) - dot(im, im)
+    prod_im = dot(re, im) + dot(im, re)
+    which = k * n + me
+    wave_re, wave_im = wave_ref[0, which], wave_ref[1, which]
+    o_ref[0] = (-(wave_re * prod_re - wave_im * prod_im)).astype(jnp.bfloat16)
+    o_ref[1] = (-(wave_re * prod_im + wave_im * prod_re)).astype(jnp.bfloat16)
+    for j in range(planes):
+        for i in range(PLANE):
+            for c in range(2):
+                outs[i][j, c] = o_ref[c, rows_of(j, i), :]
+
+
+def product(me, wave, fold, blocks, k, n):
+    shape = jax.ShapeDtypeStruct(blocks[0].shape, blocks[0].dtype)
+    points = shape.shape[3]
+    size = 2 * len(blocks) * shape.size
+    return pl.pallas_call(
+        functools.partial(product_kernel, k, n),
+        out_shape=[shape] * PLANE,
+        in_specs=[smem_spec()] * 2 + [vmem_spec()] * (2 + PLANE),
+        out_specs=[vmem_spec()] * PLANE,
+        scratch_shapes=[pltpu.VMEM((2, points, points), jnp.bfloat16)] * 2,
+        compiler_params=params(),
+        cost_estimate=cost(8 * points**3, 2 * size),
+        name="product",
+    )(me, wave, fold.reshape(1, -1), fold.reshape(-1, 1), *blocks)
+
+
+def assemble_kernel(n, shots, planes, me_ref, *refs):
+    ins, out_ref = refs[:planes], refs[-1]
+    me = me_ref[0]
+    order = split_order(me, n, shots, True)
+    points = out_ref.shape[3]
+    for c in range(2):
+        rows = jnp.concatenate(
+            [block[:, c].reshape(PLANE * shots, points) for block in ins], axis=0
+        )
+        moved = jnp.dot(order, rows, preferred_element_type=jnp.float32)
+        out_ref[:, c] = moved.astype(jnp.bfloat16).reshape(shots, n, points)
+
+
+def assemble(me, blocks, result, k, n, bins):
+    planes = len(blocks)
+    _, _, shots, points = blocks[0].shape
+    size = 2 * n * shots * points * 2
+    extra = [] if result is None else [result]
+    return pl.pallas_call(
+        functools.partial(assemble_kernel, n, shots, planes),
+        grid=(1,),
+        out_shape=jax.ShapeDtypeStruct((shots, 2, bins, points), jnp.bfloat16),
+        in_specs=[smem_spec()]
+        + [pl.BlockSpec(blocks[0].shape, lambda _: (0, 0, 0, 0))] * planes
+        + [any_spec()] * len(extra),
+        out_specs=pl.BlockSpec((shots, 2, n, points), lambda _: (0, 0, k, 0)),
+        input_output_aliases={1 + planes: 0} if extra else {},
+        compiler_params=params(),
+        cost_estimate=cost(4 * (n * shots) ** 2 * points, 2 * size),
+        name="assemble",
+    )(me, *blocks, *extra)
+
+
+def exchange(blocks, n, stride):
+    received = {
+        m: lax.ppermute(
+            blocks[m], "shot", [(d, d ^ (m * stride)) for d in range(n)]
+        )
+        for m in reversed(range(1, len(blocks)))
+    }
+    return [blocks[0]] + [received[m] for m in range(1, len(blocks))]
+
+
+def chunked_shards(n, spectra, fold_counts, inverse_wavelet):
+    bins = spectra.shape[2]
+    chunks = bins // n
+    me = lax.axis_index("shot").astype(jnp.int32).reshape(1)
+    arrived = []
+    for k in range(chunks):
+        after = [arrived[k - 2][-1]] if k >= 2 else []
+        arrived.append(exchange(relayout(me, spectra, k, n, after), n, PLANE))
+    leaving = []
+    for k in range(chunks):
+        inside = exchange(swap(arrived[k]), n, 1)
+        made = product(me, inverse_wavelet, fold_counts, inside, k, n)
+        leaving.append(swap(exchange(made, n, 1)))
+    result = None
+    for k in range(chunks):
+        result = assemble(me, exchange(leaving[k], n, PLANE), result, k, n, bins)
+    return result
+
+
 def solution(mesh):
+    n = mesh.shape["shot"]
+
+    def shards(spectra, fold_counts, inverse_wavelet):
+        shots, _, bins, _ = spectra.shape
+        power = n & (n - 1) == 0
+        if power and n % 16 == 0 and bins % n == 0 and shots % 16 == 0:
+            return chunked_shards(n, spectra, fold_counts, inverse_wavelet)
+        return plain_shards(spectra, fold_counts, inverse_wavelet)
+
     in_specs = (P(("groups", "shot"), None, None, None), P("groups"), P())
     out_specs = P(("groups", "shot"), None, None, None)
-    return jax.shard_map(shards, mesh=mesh, in_specs=in_specs, out_specs=out_specs, check_vma=False)
+    return jax.shard_map(
+        shards, mesh=mesh, in_specs=in_specs, out_specs=out_specs, check_vma=False
+    )

time: 246 us -> 226 us (0.919)
  blocking collectives: 112 us -> 0 us
  starting transfers between devices: 7.58 us -> 93.9 us
  local copies, waits for them, and re-layouts: 33.1 us -> 5.69 us
  waiting for transfers between devices: 77.1 us -> 102 us
  Pallas kernels: 0 us -> 21.7 us
  other arithmetic: 8 us -> 0 us
  matrix products: 7.55 us -> 0 us
    all_to_all x1 -> x0, blocking collectives: 112 us -> none  [shards(): lax.all_to_all(result, 'shot', split_axis=0, concat_axis=2, tiled=True)]
    ppermute x0 -> x48, waiting for transfers between devices: none -> 102 us  [exchange(): lax.ppermute(blocks[m], 'shot', [(d, d ^ m * stride) for d in range(n)])]
    ppermute x0 -> x48, starting transfers between devices: none -> 93.9 us  [exchange(): lax.ppermute(blocks[m], 'shot', [(d, d ^ m * stride) for d in range(n)])]
    all_to_all x1 -> x0, waiting for transfers between devices: 77.1 us -> none  [shards(): lax.all_to_all(spectra, 'shot', split_axis=2, concat_axis=0, tiled=True)]
    pallas_call x0 -> x20, Pallas kernels: none -> 21.7 us  [the longest x4 9.99 us: product(): pl.pallas_call(functools.partial(product_kernel, k, n), out_shape=[shape]...]
    all_to_all x5 -> x0, local copies, waits for them, and re-layouts: 18.5 us -> none  [the longest x2 12.1 us: shards(): lax.all_to_all(spectra, 'shot', split_axis=2, concat_axis=0, tiled=True)]
    another operation x1 -> x0, local copies, waits for them, and re-layouts: 7.87 us -> none  [shards(): result = jnp.stack([output_real, out_imag], axis=1).astype(jnp.bfloat16)]
    all_to_all x1 -> x0, starting transfers between devices: 7.58 us -> none  [shards(): lax.all_to_all(spectra, 'shot', split_axis=2, concat_axis=0, tiled=True)]
  transfers between devices with their start and end apart: 1 -> 48, of which waited for: 1 -> 16; matrix products, arithmetic and copies ran while one was open for 0% -> 0% of each run, Pallas kernels for 0% -> 9%
where the time goes in v1:
time: 226 us; the launch traced here: 223 us
  waiting for transfers between devices  102 us (45%)
  starting transfers between devices  93.9 us (42%)
  Pallas kernels  21.7 us (10%)
  local copies, waits for them, and re-layouts  5.69 us (3%)
    ppermute x48, waiting for transfers between devices, exchange(): lax.ppermute(blocks[m], 'shot', [(d, d ^ m * stride) for d in range(n)])  102 us
    ppermute x48, starting transfers between devices, exchange(): lax.ppermute(blocks[m], 'shot', [(d, d ^ m * stride) for d in range(n)])  93.9 us
    pallas_call x4, Pallas kernels, product(): pl.pallas_call(functools.partial(product_kernel, k, n), out_shape=[shape]...  9.99 us
    pallas_call x4, Pallas kernels, assemble(): pl.pallas_call(functools.partial(assemble_kernel, n, shots, planes), grid...  6.7 us
    unnamed x24, local copies, waits for them, and re-layouts  5.54 us
  transfers between devices with their start and end apart: 48, of which 16 were waited for; matrix products, arithmetic and copies ran while one was open for 0% of the time, Pallas kernels for 9%

profile of v1, /device:TPU:0, one launch (start us, length us, event | category | flops | bytes accessed | tf_op | source)
XLA Modules:
  0.0 223.4 jit_solution(261145887781709801)
XLA Ops:
  0.0 2.2 copy-done
  2.9 5.1 %collective-permute-start.13 = (bf16[4,2,32,512]{3,2,1,0:T(8,128)(2,1)S(1)}, bf16[4,2,32,512]{3,2,1,0:T(8,128)(2,1)S(1)}, u32[]{:S(2)}, u32[]{:S(2)}) collective-permute-start(bf16[4,2,32,512]{3,2,1,0:T(8,128)(2,1)S(1)} %get-tuple-element.86), channel_id=1, source_target_pairs={{0,12},{1,13},{2,14},{3,15},{4,8},{5,9},{6,10},{7,11},{8,4},{9,5},... | collective-permute-start | bytes 786440 | tf_op jit(solution)/shard_map/ppermute | solution.py:230
  9.4 3.8 %collective-permute-start = (bf16[4,2,32,512]{3,2,1,0:T(8,128)(2,1)S(1)}, bf16[4,2,32,512]{3,2,1,0:T(8,128)(2,1)S(1)}, u32[]{:S(2)}, u32[]{:S(2)}) collective-permute-start(bf16[4,2,32,512]{3,2,1,0:T(8,128)(2,1)S(1)} %get-tuple-element.69), channel_id=1, source_target_pairs={{0,12},{1,13},{2,14},{3,15},{4,8},{5,9},{6,10},{7,11},{8,4},{9,5},... | collective-permute-start | bytes 786440 | tf_op jit(solution)/shard_map/ppermute | solution.py:230
  13.2 2.1 collective-permute-done.13.refs_0_.refs_3_
  15.3 6.8 %collective-permute-start.27 = (bf16[4,2,32,512]{3,2,1,0:T(8,128)(2,1)S(1)}, bf16[4,2,32,512]{3,2,1,0:T(8,128)(2,1)S(1)}, u32[]{:S(2)}, u32[]{:S(2)}) collective-permute-start(bf16[4,2,32,512]{3,2,1,0:T(8,128)(2,1)S(1)} %get-tuple-element.105), channel_id=1, source_target_pairs={{0,8},{1,9},{2,10},{3,11},{4,12},{5,13},{6,14},{7,15},{8,0},{9,1},... | collective-permute-start | bytes 786440 | tf_op jit(solution)/shard_map/ppermute | solution.py:230
  22.1 15.7 %collective-permute-done.38.refs_2_ = bf16[4,2,32,512]{3,2,1,0:T(8,128)(2,1)S(1)} collective-permute-done((bf16[4,2,32,512]{3,2,1,0:T(8,128)(2,1)S(1)}, bf16[4,2,32,512]{3,2,1,0:T(8,128)(2,1)S(1)}, u32[]{:S(2)}, u32[]{:S(2)}) %collective-permute-start.38) | collective-permute-done | bytes 262176 | tf_op jit(solution)/shard_map/ppermute | solution.py:230
  39.8 13.0 %collective-permute-done.27.refs_2_ = bf16[4,2,32,512]{3,2,1,0:T(8,128)(2,1)S(1)} collective-permute-done((bf16[4,2,32,512]{3,2,1,0:T(8,128)(2,1)S(1)}, bf16[4,2,32,512]{3,2,1,0:T(8,128)(2,1)S(1)}, u32[]{:S(2)}, u32[]{:S(2)}) %collective-permute-start.27) | collective-permute-done | bytes 262176 | tf_op jit(solution)/shard_map/ppermute | solution.py:230
  56.4 3.1 %collective-permute-start.15 = (bf16[4,2,32,512]{3,2,1,0:T(8,128)(2,1)}, bf16[4,2,32,512]{3,2,1,0:T(8,128)(2,1)S(1)}, u32[]{:S(2)}, u32[]{:S(2)}) collective-permute-start(bf16[4,2,32,512]{3,2,1,0:T(8,128)(2,1)} %get-tuple-element.89), channel_id=1, source_target_pairs={{0,8},{1,9},{2,10},{3,11},{4,12},{5,13},{6,14},{7,15},{8,0},{9,1},... | collective-permute-start | bytes 786440 | tf_op jit(solution)/shard_map/ppermute | solution.py:230
  63.8 3.1 %collective-permute-done.30.refs_3_ = bf16[4,2,32,512]{3,2,1,0:T(8,128)(2,1)S(1)} collective-permute-done((bf16[4,2,32,512]{3,2,1,0:T(8,128)(2,1)S(1)}, bf16[4,2,32,512]{3,2,1,0:T(8,128)(2,1)S(1)}, u32[]{:S(2)}, u32[]{:S(2)}) %collective-permute-start.30) | collective-permute-done | bytes 262176 | tf_op jit(solution)/shard_map/ppermute | solution.py:230
  67.6 2.9 %collective-permute-start.2 = (bf16[4,2,32,512]{3,2,1,0:T(8,128)(2,1)}, bf16[4,2,32,512]{3,2,1,0:T(8,128)(2,1)S(1)}, u32[]{:S(2)}, u32[]{:S(2)}) collective-permute-start(bf16[4,2,32,512]{3,2,1,0:T(8,128)(2,1)} %get-tuple-element.72), channel_id=1, source_target_pairs={{0,8},{1,9},{2,10},{3,11},{4,12},{5,13},{6,14},{7,15},{8,0},{9,1},... | collective-permute-start | bytes 786440 | tf_op jit(solution)/shard_map/ppermute | solution.py:230
  74.2 2.5 %product.7 = (bf16[4,2,32,512]{3,2,1,0:T(8,128)(2,1)S(1)}, bf16[4,2,32,512]{3,2,1,0:T(8,128)(2,1)S(1)}, bf16[4,2,32,512]{3,2,1,0:T(8,128)(2,1)S(1)}, bf16[4,2,32,512]{3,2,1,0:T(8,128)(2,1)S(1)}) custom-call(s32[1]{0:T(128)} %bitcast.me_ref, f32[2,64]{1,0:T(2,128)S(1)} %copy-done.11, s32[1,512]{1,0:T(1,128)S(1)} %bitcast.4, s32[512,1]{1,0:T(8,128)S(1)} %copy.7.fold_col_ref, ...), custom_call_target="tpu_custom_call" | custom-call | flops 1073741824 | bytes 2097152 | tf_op jit(solution)/shard_map/product/pallas_call | solution.py:183
  79.7 2.5 %product.6 = (bf16[4,2,32,512]{3,2,1,0:T(8,128)(2,1)S(1)}, bf16[4,2,32,512]{3,2,1,0:T(8,128)(2,1)S(1)}, bf16[4,2,32,512]{3,2,1,0:T(8,128)(2,1)S(1)}, bf16[4,2,32,512]{3,2,1,0:T(8,128)(2,1)S(1)}) custom-call(s32[1]{0:T(128)} %bitcast.me_ref, f32[2,64]{1,0:T(2,128)S(1)} %copy-done.11, s32[1,512]{1,0:T(1,128)S(1)} %bitcast.5, s32[512,1]{1,0:T(8,128)S(1)} %copy.7.fold_col_ref, ...), custom_call_target="tpu_custom_call" | custom-call | flops 1073741824 | bytes 2097152 | tf_op jit(solution)/shard_map/product/pallas_call | solution.py:183
  82.6 18.0 %collective-permute-done.2.refs_2_ = bf16[4,2,32,512]{3,2,1,0:T(8,128)(2,1)S(1)} collective-permute-done((bf16[4,2,32,512]{3,2,1,0:T(8,128)(2,1)}, bf16[4,2,32,512]{3,2,1,0:T(8,128)(2,1)S(1)}, u32[]{:S(2)}, u32[]{:S(2)}) %collective-permute-start.2) | collective-permute-done | bytes 262176 | tf_op jit(solution)/shard_map/ppermute | solution.py:230
  104.9 5.4 %collective-permute-done.18.refs_2_ = bf16[4,2,32,512]{3,2,1,0:T(8,128)(2,1)S(1)} collective-permute-done((bf16[4,2,32,512]{3,2,1,0:T(8,128)(2,1)S(1)}, bf16[4,2,32,512]{3,2,1,0:T(8,128)(2,1)S(1)}, u32[]{:S(2)}, u32[]{:S(2)}) %collective-permute-start.18) | collective-permute-done | bytes 262176 | tf_op jit(solution)/shard_map/ppermute | solution.py:230
  111.7 3.1 %collective-permute-done.19.refs_3_ = bf16[4,2,32,512]{3,2,1,0:T(8,128)(2,1)S(1)} collective-permute-done((bf16[4,2,32,512]{3,2,1,0:T(8,128)(2,1)S(1)}, bf16[4,2,32,512]{3,2,1,0:T(8,128)(2,1)S(1)}, u32[]{:S(2)}, u32[]{:S(2)}) %collective-permute-start.19) | collective-permute-done | bytes 262176 | tf_op jit(solution)/shard_map/ppermute | solution.py:230
  114.9 1.9 collective-permute-start.6
  116.9 2.5 %product.5 = (bf16[4,2,32,512]{3,2,1,0:T(8,128)(2,1)S(1)}, bf16[4,2,32,512]{3,2,1,0:T(8,128)(2,1)S(1)}, bf16[4,2,32,512]{3,2,1,0:T(8,128)(2,1)S(1)}, bf16[4,2,32,512]{3,2,1,0:T(8,128)(2,1)S(1)}) custom-call(s32[1]{0:T(128)} %bitcast.me_ref, f32[2,64]{1,0:T(2,128)S(1)} %copy-done.11, s32[1,512]{1,0:T(1,128)S(1)} %bitcast.6, s32[512,1]{1,0:T(8,128)S(1)} %copy.7.fold_col_ref, ...), custom_call_target="tpu_custom_call" | custom-call | flops 1073741824 | bytes 2097152 | tf_op jit(solution)/shard_map/product/pallas_call | solution.py:183
  119.3 2.2 collective-permute-done.32.refs_2_
  121.5 5.0 %collective-permute-start.45 = (bf16[4,2,32,512]{3,2,1,0:T(8,128)(2,1)S(1)}, bf16[4,2,32,512]{3,2,1,0:T(8,128)(2,1)S(1)}, u32[]{:S(2)}, u32[]{:S(2)}) collective-permute-start(bf16[4,2,32,512]{3,2,1,0:T(8,128)(2,1)S(1)} %get-tuple-element.130), channel_id=1, source_target_pairs={{0,4},{1,5},{2,6},{3,7},{4,0},{5,1},{6,2},{7,3},{8,12},{9,13},{10,... | collective-permute-start | bytes 786440 | tf_op jit(solution)/shard_map/ppermute | solution.py:230
  126.5 5.8 %collective-permute-start.46 = (bf16[4,2,32,512]{3,2,1,0:T(8,128)(2,1)S(1)}, bf16[4,2,32,512]{3,2,1,0:T(8,128)(2,1)S(1)}, u32[]{:S(2)}, u32[]{:S(2)}) collective-permute-start(bf16[4,2,32,512]{3,2,1,0:T(8,128)(2,1)S(1)} %get-tuple-element.131), channel_id=1, source_target_pairs={{0,8},{1,9},{2,10},{3,11},{4,12},{5,13},{6,14},{7,15},{8,0},{9,1},... | collective-permute-start | bytes 786440 | tf_op jit(solution)/shard_map/ppermute | solution.py:230
  134.5 2.9 %collective-permute-done.6.refs_3_ = bf16[4,2,32,512]{3,2,1,0:T(8,128)(2,1)S(1)} collective-permute-done((bf16[4,2,32,512]{3,2,1,0:T(8,128)(2,1)S(1)}, bf16[4,2,32,512]{3,2,1,0:T(8,128)(2,1)S(1)}, u32[]{:S(2)}, u32[]{:S(2)}) %collective-permute-start.6) | collective-permute-done | bytes 262176 | tf_op jit(solution)/shard_map/ppermute | solution.py:230
  137.3 2.2 collective-permute-start.22
  139.5 2.6 %product.4 = (bf16[4,2,32,512]{3,2,1,0:T(8,128)(2,1)S(1)}, bf16[4,2,32,512]{3,2,1,0:T(8,128)(2,1)S(1)}, bf16[4,2,32,512]{3,2,1,0:T(8,128)(2,1)S(1)}, bf16[4,2,32,512]{3,2,1,0:T(8,128)(2,1)S(1)}) custom-call(s32[1]{0:T(128)} %bitcast.me_ref, f32[2,64]{1,0:T(2,128)S(1)} %copy-done.11, s32[1,512]{1,0:T(1,128)S(1)} %bitcast.7, s32[512,1]{1,0:T(8,128)S(1)} %copy.7.fold_col_ref, ...), custom_call_target="tpu_custom_call" | custom-call | flops 1073741824 | bytes 2097152 | tf_op jit(solution)/shard_map/product/pallas_call | solution.py:183
  142.3 2.5 %collective-permute-start.47 = (bf16[4,2,32,512]{3,2,1,0:T(8,128)(2,1)S(1)}, bf16[4,2,32,512]{3,2,1,0:T(8,128)(2,1)S(1)}, u32[]{:S(2)}, u32[]{:S(2)}) collective-permute-start(bf16[4,2,32,512]{3,2,1,0:T(8,128)(2,1)S(1)} %get-tuple-element.132), channel_id=1, source_target_pairs={{0,12},{1,13},{2,14},{3,15},{4,8},{5,9},{6,10},{7,11},{8,4},{9,5},... | collective-permute-start | bytes 786440 | tf_op jit(solution)/shard_map/ppermute | solution.py:230
  144.9 3.7 %collective-permute-start.34 = (bf16[4,2,32,512]{3,2,1,0:T(8,128)(2,1)S(1)}, bf16[4,2,32,512]{3,2,1,0:T(8,128)(2,1)S(1)}, u32[]{:S(2)}, u32[]{:S(2)}) collective-permute-start(bf16[4,2,32,512]{3,2,1,0:T(8,128)(2,1)S(1)} %get-tuple-element.115), channel_id=1, source_target_pairs={{0,4},{1,5},{2,6},{3,7},{4,0},{5,1},{6,2},{7,3},{8,12},{9,13},{10,... | collective-permute-start | bytes 786440 | tf_op jit(solution)/shard_map/ppermute | solution.py:230
  152.2 6.2 %collective-permute-start.35 = (bf16[4,2,32,512]{3,2,1,0:T(8,128)(2,1)S(1)}, bf16[4,2,32,512]{3,2,1,0:T(8,128)(2,1)S(1)}, u32[]{:S(2)}, u32[]{:S(2)}) collective-permute-start(bf16[4,2,32,512]{3,2,1,0:T(8,128)(2,1)S(1)} %get-tuple-element.116), channel_id=1, source_target_pairs={{0,8},{1,9},{2,10},{3,11},{4,12},{5,13},{6,14},{7,15},{8,0},{9,1},... | collective-permute-start | bytes 786440 | tf_op jit(solution)/shard_map/ppermute | solution.py:230
  159.8 3.0 %collective-permute-start.24 = (bf16[4,2,32,512]{3,2,1,0:T(8,128)(2,1)S(1)}, bf16[4,2,32,512]{3,2,1,0:T(8,128)(2,1)S(1)}, u32[]{:S(2)}, u32[]{:S(2)}) collective-permute-start(bf16[4,2,32,512]{3,2,1,0:T(8,128)(2,1)S(1)} %get-tuple-element.101), channel_id=1, source_target_pairs={{0,8},{1,9},{2,10},{3,11},{4,12},{5,13},{6,14},{7,15},{8,0},{9,1},... | collective-permute-start | bytes 786440 | tf_op jit(solution)/shard_map/ppermute | solution.py:230
  164.3 12.9 %collective-permute-done.35.refs_2_ = bf16[4,2,32,512]{3,2,1,0:T(8,128)(2,1)S(1)} collective-permute-done((bf16[4,2,32,512]{3,2,1,0:T(8,128)(2,1)S(1)}, bf16[4,2,32,512]{3,2,1,0:T(8,128)(2,1)S(1)}, u32[]{:S(2)}, u32[]{:S(2)}) %collective-permute-start.35) | collective-permute-done | bytes 262176 | tf_op jit(solution)/shard_map/ppermute | solution.py:230
  177.2 16.9 %collective-permute-start.11 = (bf16[4,2,32,512]{3,2,1,0:T(8,128)(2,1)S(1)}, bf16[4,2,32,512]{3,2,1,0:T(8,128)(2,1)S(1)}, u32[]{:S(2)}, u32[]{:S(2)}) collective-permute-start(bf16[4,2,32,512]{3,2,1,0:T(8,128)(2,1)S(1)} %get-tuple-element.84), channel_id=1, source_target_pairs={{0,8},{1,9},{2,10},{3,11},{4,12},{5,13},{6,14},{7,15},{8,0},{9,1},... | collective-permute-start | bytes 786440 | tf_op jit(solution)/shard_map/ppermute | solution.py:230
  194.1 2.4 %collective-permute-start.12 = (bf16[4,2,32,512]{3,2,1,0:T(8,128)(2,1)S(1)}, bf16[4,2,32,512]{3,2,1,0:T(8,128)(2,1)S(1)}, u32[]{:S(2)}, u32[]{:S(2)}) collective-permute-start(bf16[4,2,32,512]{3,2,1,0:T(8,128)(2,1)S(1)} %get-tuple-element.85), channel_id=1, source_target_pairs={{0,12},{1,13},{2,14},{3,15},{4,8},{5,9},{6,10},{7,11},{8,4},{9,5},... | collective-permute-start | bytes 786440 | tf_op jit(solution)/shard_map/ppermute | solution.py:230
  199.9 10.6 %collective-permute-done.24.refs_2_ = bf16[4,2,32,512]{3,2,1,0:T(8,128)(2,1)S(1)} collective-permute-done((bf16[4,2,32,512]{3,2,1,0:T(8,128)(2,1)S(1)}, bf16[4,2,32,512]{3,2,1,0:T(8,128)(2,1)S(1)}, u32[]{:S(2)}, u32[]{:S(2)}) %collective-permute-start.24) | collective-permute-done | bytes 262176 | tf_op jit(solution)/shard_map/ppermute | solution.py:230
  212.2 9.6 %collective-permute-done.11.refs_2_ = bf16[4,2,32,512]{3,2,1,0:T(8,128)(2,1)S(1)} collective-permute-done((bf16[4,2,32,512]{3,2,1,0:T(8,128)(2,1)S(1)}, bf16[4,2,32,512]{3,2,1,0:T(8,128)(2,1)S(1)}, u32[]{:S(2)}, u32[]{:S(2)}) %collective-permute-start.11) | collective-permute-done | bytes 262176 | tf_op jit(solution)/shard_map/ppermute | solution.py:230
  (109 shorter events, 41.1 us)
Async XLA Ops:
  8.1 29.7 %collective-permute-start.38 = (bf16[4,2,32,512]{3,2,1,0:T(8,128)(2,1)S(1)}, bf16[4,2,32,512]{3,2,1,0:T(8,128)(2,1)S(1)}, u32[]{:S(2)}, u32[]{:S(2)}) collective-permute-start(bf16[4,2,32,512]{3,2,1,0:T(8,128)(2,1)S(1)} %get-tuple-element.120), channel_id=1, source_target_pairs={{0,8},{1,9},{2,10},{3,11},{4,12},{5,13},{6,14},{7,15},{8,0},{9,1},... | collective-permute-start | bytes 786440 | tf_op jit(solution)/shard_map/ppermute | solution.py:230
  9.4 30.3 %collective-permute-start = (bf16[4,2,32,512]{3,2,1,0:T(8,128)(2,1)S(1)}, bf16[4,2,32,512]{3,2,1,0:T(8,128)(2,1)S(1)}, u32[]{:S(2)}, u32[]{:S(2)}) collective-permute-start(bf16[4,2,32,512]{3,2,1,0:T(8,128)(2,1)S(1)} %get-tuple-element.69), channel_id=1, source_target_pairs={{0,12},{1,13},{2,14},{3,15},{4,8},{5,9},{6,10},{7,11},{8,4},{9,5},... | collective-permute-start | bytes 786440 | tf_op jit(solution)/shard_map/ppermute | solution.py:230
  13.2 26.6 %collective-permute-start.26 = (bf16[4,2,32,512]{3,2,1,0:T(8,128)(2,1)S(1)}, bf16[4,2,32,512]{3,2,1,0:T(8,128)(2,1)S(1)}, u32[]{:S(2)}, u32[]{:S(2)}) collective-permute-start(bf16[4,2,32,512]{3,2,1,0:T(8,128)(2,1)S(1)} %get-tuple-element.104), channel_id=1, source_target_pairs={{0,4},{1,5},{2,6},{3,7},{4,0},{5,1},{6,2},{7,3},{8,12},{9,13},{10,... | collective-permute-start | bytes 786440 | tf_op jit(solution)/shard_map/ppermute | solution.py:230
  15.3 37.6 %collective-permute-start.27 = (bf16[4,2,32,512]{3,2,1,0:T(8,128)(2,1)S(1)}, bf16[4,2,32,512]{3,2,1,0:T(8,128)(2,1)S(1)}, u32[]{:S(2)}, u32[]{:S(2)}) collective-permute-start(bf16[4,2,32,512]{3,2,1,0:T(8,128)(2,1)S(1)} %get-tuple-element.105), channel_id=1, source_target_pairs={{0,8},{1,9},{2,10},{3,11},{4,12},{5,13},{6,14},{7,15},{8,0},{9,1},... | collective-permute-start | bytes 786440 | tf_op jit(solution)/shard_map/ppermute | solution.py:230
  37.9 18.2 %collective-permute-start.39 = (bf16[4,2,32,512]{3,2,1,0:T(8,128)(2,1)S(1)}, bf16[4,2,32,512]{3,2,1,0:T(8,128)(2,1)S(1)}, u32[]{:S(2)}, u32[]{:S(2)}) collective-permute-start(bf16[4,2,32,512]{3,2,1,0:T(8,128)(2,1)S(1)} %get-tuple-element.122), channel_id=1, source_target_pairs={{0,1},{1,0},{2,3},{3,2},{4,5},{5,4},{6,7},{7,6},{8,9},{9,8},{10,11... | collective-permute-start | bytes 786440 | tf_op jit(solution)/shard_map/ppermute | solution.py:230
  37.9 18.4 %collective-permute-start.40 = (bf16[4,2,32,512]{3,2,1,0:T(8,128)(2,1)S(1)}, bf16[4,2,32,512]{3,2,1,0:T(8,128)(2,1)S(1)}, u32[]{:S(2)}, u32[]{:S(2)}) collective-permute-start(bf16[4,2,32,512]{3,2,1,0:T(8,128)(2,1)S(1)} %get-tuple-element.123), channel_id=1, source_target_pairs={{0,2},{1,3},{2,0},{3,1},{4,6},{5,7},{6,4},{7,5},{8,10},{9,11},{10,... | collective-permute-start | bytes 786440 | tf_op jit(solution)/shard_map/ppermute | solution.py:230
  39.7 16.7 %collective-permute-start.41 = (bf16[4,2,32,512]{3,2,1,0:T(8,128)(2,1)S(1)}, bf16[4,2,32,512]{3,2,1,0:T(8,128)(2,1)S(1)}, u32[]{:S(2)}, u32[]{:S(2)}) collective-permute-start(bf16[4,2,32,512]{3,2,1,0:T(8,128)(2,1)S(1)} %get-tuple-element.124), channel_id=1, source_target_pairs={{0,3},{1,2},{2,1},{3,0},{4,7},{5,6},{6,5},{7,4},{8,11},{9,10},{10,... | collective-permute-start | bytes 786440 | tf_op jit(solution)/shard_map/ppermute | solution.py:230
  56.4 21.7 %collective-permute-start.15 = (bf16[4,2,32,512]{3,2,1,0:T(8,128)(2,1)}, bf16[4,2,32,512]{3,2,1,0:T(8,128)(2,1)S(1)}, u32[]{:S(2)}, u32[]{:S(2)}) collective-permute-start(bf16[4,2,32,512]{3,2,1,0:T(8,128)(2,1)} %get-tuple-element.89), channel_id=1, source_target_pairs={{0,8},{1,9},{2,10},{3,11},{4,12},{5,13},{6,14},{7,15},{8,0},{9,1},... | collective-permute-start | bytes 786440 | tf_op jit(solution)/shard_map/ppermute | solution.py:230
  59.4 18.6 %collective-permute-start.16 = (bf16[4,2,32,512]{3,2,1,0:T(8,128)(2,1)}, bf16[4,2,32,512]{3,2,1,0:T(8,128)(2,1)S(1)}, u32[]{:S(2)}, u32[]{:S(2)}) collective-permute-start(bf16[4,2,32,512]{3,2,1,0:T(8,128)(2,1)} %get-tuple-element.90), channel_id=1, source_target_pairs={{0,12},{1,13},{2,14},{3,15},{4,8},{5,9},{6,10},{7,11},{8,4},{9,5},... | collective-permute-start | bytes 786440 | tf_op jit(solution)/shard_map/ppermute | solution.py:230
  63.0 19.2 %collective-permute-start.1 = (bf16[4,2,32,512]{3,2,1,0:T(8,128)(2,1)}, bf16[4,2,32,512]{3,2,1,0:T(8,128)(2,1)S(1)}, u32[]{:S(2)}, u32[]{:S(2)}) collective-permute-start(bf16[4,2,32,512]{3,2,1,0:T(8,128)(2,1)} %get-tuple-element.71), channel_id=1, source_target_pairs={{0,4},{1,5},{2,6},{3,7},{4,0},{5,1},{6,2},{7,3},{8,12},{9,13},{10,... | collective-permute-start | bytes 786440 | tf_op jit(solution)/shard_map/ppermute | solution.py:230
  67.6 33.0 %collective-permute-start.2 = (bf16[4,2,32,512]{3,2,1,0:T(8,128)(2,1)}, bf16[4,2,32,512]{3,2,1,0:T(8,128)(2,1)S(1)}, u32[]{:S(2)}, u32[]{:S(2)}) collective-permute-start(bf16[4,2,32,512]{3,2,1,0:T(8,128)(2,1)} %get-tuple-element.72), channel_id=1, source_target_pairs={{0,8},{1,9},{2,10},{3,11},{4,12},{5,13},{6,14},{7,15},{8,0},{9,1},... | collective-permute-start | bytes 786440 | tf_op jit(solution)/shard_map/ppermute | solution.py:230
  70.6 29.9 %collective-permute-start.3 = (bf16[4,2,32,512]{3,2,1,0:T(8,128)(2,1)}, bf16[4,2,32,512]{3,2,1,0:T(8,128)(2,1)S(1)}, u32[]{:S(2)}, u32[]{:S(2)}) collective-permute-start(bf16[4,2,32,512]{3,2,1,0:T(8,128)(2,1)} %get-tuple-element.73), channel_id=1, source_target_pairs={{0,12},{1,13},{2,14},{3,15},{4,8},{5,9},{6,10},{7,11},{8,4},{9,5},... | collective-permute-start | bytes 786440 | tf_op jit(solution)/shard_map/ppermute | solution.py:230
  78.1 23.0 %collective-permute-start.42 = (bf16[4,2,32,512]{3,2,1,0:T(8,128)(2,1)S(1)}, bf16[4,2,32,512]{3,2,1,0:T(8,128)(2,1)S(1)}, u32[]{:S(2)}, u32[]{:S(2)}) collective-permute-start(bf16[4,2,32,512]{3,2,1,0:T(8,128)(2,1)S(1)} %get-tuple-element.126), channel_id=1, source_target_pairs={{0,1},{1,0},{2,3},{3,2},{4,5},{5,4},{6,7},{7,6},{8,9},{9,8},{10,11... | collective-permute-start | bytes 786440 | tf_op jit(solution)/shard_map/ppermute | solution.py:230
  78.1 24.5 %collective-permute-start.43 = (bf16[4,2,32,512]{3,2,1,0:T(8,128)(2,1)S(1)}, bf16[4,2,32,512]{3,2,1,0:T(8,128)(2,1)S(1)}, u32[]{:S(2)}, u32[]{:S(2)}) collective-permute-start(bf16[4,2,32,512]{3,2,1,0:T(8,128)(2,1)S(1)} %get-tuple-element.127), channel_id=1, source_target_pairs={{0,2},{1,3},{2,0},{3,1},{4,6},{5,7},{6,4},{7,5},{8,10},{9,11},{10,... | collective-permute-start | bytes 786440 | tf_op jit(solution)/shard_map/ppermute | solution.py:230
  82.2 20.5 %collective-permute-start.44 = (bf16[4,2,32,512]{3,2,1,0:T(8,128)(2,1)S(1)}, bf16[4,2,32,512]{3,2,1,0:T(8,128)(2,1)S(1)}, u32[]{:S(2)}, u32[]{:S(2)}) collective-permute-start(bf16[4,2,32,512]{3,2,1,0:T(8,128)(2,1)S(1)} %get-tuple-element.128), channel_id=1, source_target_pairs={{0,3},{1,2},{2,1},{3,0},{4,7},{5,6},{6,5},{7,4},{8,11},{9,10},{10,... | collective-permute-start | bytes 786440 | tf_op jit(solution)/shard_map/ppermute | solution.py:230
  102.7 18.8 %collective-permute-start.32 = (bf16[4,2,32,512]{3,2,1,0:T(8,128)(2,1)S(1)}, bf16[4,2,32,512]{3,2,1,0:T(8,128)(2,1)S(1)}, u32[]{:S(2)}, u32[]{:S(2)}) collective-permute-start(bf16[4,2,32,512]{3,2,1,0:T(8,128)(2,1)S(1)} %get-tuple-element.112), channel_id=1, source_target_pairs={{0,2},{1,3},{2,0},{3,1},{4,6},{5,7},{6,4},{7,5},{8,10},{9,11},{10,... | collective-permute-start | bytes 786440 | tf_op jit(solution)/shard_map/ppermute | solution.py:230
  104.2 22.4 %collective-permute-start.33 = (bf16[4,2,32,512]{3,2,1,0:T(8,128)(2,1)S(1)}, bf16[4,2,32,512]{3,2,1,0:T(8,128)(2,1)S(1)}, u32[]{:S(2)}, u32[]{:S(2)}) collective-permute-start(bf16[4,2,32,512]{3,2,1,0:T(8,128)(2,1)S(1)} %get-tuple-element.113), channel_id=1, source_target_pairs={{0,3},{1,2},{2,1},{3,0},{4,7},{5,6},{6,5},{7,4},{8,11},{9,10},{10,... | collective-permute-start | bytes 786440 | tf_op jit(solution)/shard_map/ppermute | solution.py:230
  104.7 27.6 %collective-permute-start.4 = (bf16[4,2,32,512]{3,2,1,0:T(8,128)(2,1)S(1)}, bf16[4,2,32,512]{3,2,1,0:T(8,128)(2,1)S(1)}, u32[]{:S(2)}, u32[]{:S(2)}) collective-permute-start(bf16[4,2,32,512]{3,2,1,0:T(8,128)(2,1)S(1)} %get-tuple-element.75), channel_id=1, source_target_pairs={{0,1},{1,0},{2,3},{3,2},{4,5},{5,4},{6,7},{7,6},{8,9},{9,8},{10,11... | collective-permute-start | bytes 786440 | tf_op jit(solution)/shard_map/ppermute | solution.py:230
  110.2 22.7 %collective-permute-start.5 = (bf16[4,2,32,512]{3,2,1,0:T(8,128)(2,1)S(1)}, bf16[4,2,32,512]{3,2,1,0:T(8,128)(2,1)S(1)}, u32[]{:S(2)}, u32[]{:S(2)}) collective-permute-start(bf16[4,2,32,512]{3,2,1,0:T(8,128)(2,1)S(1)} %get-tuple-element.76), channel_id=1, source_target_pairs={{0,2},{1,3},{2,0},{3,1},{4,6},{5,7},{6,4},{7,5},{8,10},{9,11},{10,... | collective-permute-start | bytes 786440 | tf_op jit(solution)/shard_map/ppermute | solution.py:230
  114.9 22.5 %collective-permute-start.6 = (bf16[4,2,32,512]{3,2,1,0:T(8,128)(2,1)S(1)}, bf16[4,2,32,512]{3,2,1,0:T(8,128)(2,1)S(1)}, u32[]{:S(2)}, u32[]{:S(2)}) collective-permute-start(bf16[4,2,32,512]{3,2,1,0:T(8,128)(2,1)S(1)} %get-tuple-element.77), channel_id=1, source_target_pairs={{0,3},{1,2},{2,1},{3,0},{4,7},{5,6},{6,5},{7,4},{8,11},{9,10},{10,... | collective-permute-start | bytes 786440 | tf_op jit(solution)/shard_map/ppermute | solution.py:230
  121.5 20.8 %collective-permute-start.45 = (bf16[4,2,32,512]{3,2,1,0:T(8,128)(2,1)S(1)}, bf16[4,2,32,512]{3,2,1,0:T(8,128)(2,1)S(1)}, u32[]{:S(2)}, u32[]{:S(2)}) collective-permute-start(bf16[4,2,32,512]{3,2,1,0:T(8,128)(2,1)S(1)} %get-tuple-element.130), channel_id=1, source_target_pairs={{0,4},{1,5},{2,6},{3,7},{4,0},{5,1},{6,2},{7,3},{8,12},{9,13},{10,... | collective-permute-start | bytes 786440 | tf_op jit(solution)/shard_map/ppermute | solution.py:230
  126.5 18.4 %collective-permute-start.46 = (bf16[4,2,32,512]{3,2,1,0:T(8,128)(2,1)S(1)}, bf16[4,2,32,512]{3,2,1,0:T(8,128)(2,1)S(1)}, u32[]{:S(2)}, u32[]{:S(2)}) collective-permute-start(bf16[4,2,32,512]{3,2,1,0:T(8,128)(2,1)S(1)} %get-tuple-element.131), channel_id=1, source_target_pairs={{0,8},{1,9},{2,10},{3,11},{4,12},{5,13},{6,14},{7,15},{8,0},{9,1},... | collective-permute-start | bytes 786440 | tf_op jit(solution)/shard_map/ppermute | solution.py:230
  132.3 16.3 %collective-permute-start.20 = (bf16[4,2,32,512]{3,2,1,0:T(8,128)(2,1)S(1)}, bf16[4,2,32,512]{3,2,1,0:T(8,128)(2,1)S(1)}, u32[]{:S(2)}, u32[]{:S(2)}) collective-permute-start(bf16[4,2,32,512]{3,2,1,0:T(8,128)(2,1)S(1)} %get-tuple-element.96), channel_id=1, source_target_pairs={{0,1},{1,0},{2,3},{3,2},{4,5},{5,4},{6,7},{7,6},{8,9},{9,8},{10,11... | collective-permute-start | bytes 786440 | tf_op jit(solution)/shard_map/ppermute | solution.py:230
  133.0 15.7 %collective-permute-start.21 = (bf16[4,2,32,512]{3,2,1,0:T(8,128)(2,1)S(1)}, bf16[4,2,32,512]{3,2,1,0:T(8,128)(2,1)S(1)}, u32[]{:S(2)}, u32[]{:S(2)}) collective-permute-start(bf16[4,2,32,512]{3,2,1,0:T(8,128)(2,1)S(1)} %get-tuple-element.97), channel_id=1, source_target_pairs={{0,2},{1,3},{2,0},{3,1},{4,6},{5,7},{6,4},{7,5},{8,10},{9,11},{10,... | collective-permute-start | bytes 786440 | tf_op jit(solution)/shard_map/ppermute | solution.py:230
  152.2 25.0 %collective-permute-start.35 = (bf16[4,2,32,512]{3,2,1,0:T(8,128)(2,1)S(1)}, bf16[4,2,32,512]{3,2,1,0:T(8,128)(2,1)S(1)}, u32[]{:S(2)}, u32[]{:S(2)}) collective-permute-start(bf16[4,2,32,512]{3,2,1,0:T(8,128)(2,1)S(1)} %get-tuple-element.116), channel_id=1, source_target_pairs={{0,8},{1,9},{2,10},{3,11},{4,12},{5,13},{6,14},{7,15},{8,0},{9,1},... | collective-permute-start | bytes 786440 | tf_op jit(solution)/shard_map/ppermute | solution.py:230
  158.4 18.8 %collective-permute-start.36 = (bf16[4,2,32,512]{3,2,1,0:T(8,128)(2,1)S(1)}, bf16[4,2,32,512]{3,2,1,0:T(8,128)(2,1)S(1)}, u32[]{:S(2)}, u32[]{:S(2)}) collective-permute-start(bf16[4,2,32,512]{3,2,1,0:T(8,128)(2,1)S(1)} %get-tuple-element.117), channel_id=1, source_target_pairs={{0,12},{1,13},{2,14},{3,15},{4,8},{5,9},{6,10},{7,11},{8,4},{9,5},... | collective-permute-start | bytes 786440 | tf_op jit(solution)/shard_map/ppermute | solution.py:230
  159.8 34.3 %collective-permute-start.23 = (bf16[4,2,32,512]{3,2,1,0:T(8,128)(2,1)S(1)}, bf16[4,2,32,512]{3,2,1,0:T(8,128)(2,1)S(1)}, u32[]{:S(2)}, u32[]{:S(2)}) collective-permute-start(bf16[4,2,32,512]{3,2,1,0:T(8,128)(2,1)S(1)} %get-tuple-element.100), channel_id=1, source_target_pairs={{0,4},{1,5},{2,6},{3,7},{4,0},{5,1},{6,2},{7,3},{8,12},{9,13},{10,... | collective-permute-start | bytes 786440 | tf_op jit(solution)/shard_map/ppermute | solution.py:230
  159.8 50.7 %collective-permute-start.24 = (bf16[4,2,32,512]{3,2,1,0:T(8,128)(2,1)S(1)}, bf16[4,2,32,512]{3,2,1,0:T(8,128)(2,1)S(1)}, u32[]{:S(2)}, u32[]{:S(2)}) collective-permute-start(bf16[4,2,32,512]{3,2,1,0:T(8,128)(2,1)S(1)} %get-tuple-element.101), channel_id=1, source_target_pairs={{0,8},{1,9},{2,10},{3,11},{4,12},{5,13},{6,14},{7,15},{8,0},{9,1},... | collective-permute-start | bytes 786440 | tf_op jit(solution)/shard_map/ppermute | solution.py:230
  162.8 47.7 %collective-permute-start.25 = (bf16[4,2,32,512]{3,2,1,0:T(8,128)(2,1)S(1)}, bf16[4,2,32,512]{3,2,1,0:T(8,128)(2,1)S(1)}, u32[]{:S(2)}, u32[]{:S(2)}) collective-permute-start(bf16[4,2,32,512]{3,2,1,0:T(8,128)(2,1)S(1)} %get-tuple-element.102), channel_id=1, source_target_pairs={{0,12},{1,13},{2,14},{3,15},{4,8},{5,9},{6,10},{7,11},{8,4},{9,5},... | collective-permute-start | bytes 786440 | tf_op jit(solution)/shard_map/ppermute | solution.py:230
  177.2 35.0 %collective-permute-start.10 = (bf16[4,2,32,512]{3,2,1,0:T(8,128)(2,1)S(1)}, bf16[4,2,32,512]{3,2,1,0:T(8,128)(2,1)S(1)}, u32[]{:S(2)}, u32[]{:S(2)}) collective-permute-start(bf16[4,2,32,512]{3,2,1,0:T(8,128)(2,1)S(1)} %get-tuple-element.83), channel_id=1, source_target_pairs={{0,4},{1,5},{2,6},{3,7},{4,0},{5,1},{6,2},{7,3},{8,12},{9,13},{10,... | collective-permute-start | bytes 786440 | tf_op jit(solution)/shard_map/ppermute | solution.py:230
  177.2 44.5 %collective-permute-start.11 = (bf16[4,2,32,512]{3,2,1,0:T(8,128)(2,1)S(1)}, bf16[4,2,32,512]{3,2,1,0:T(8,128)(2,1)S(1)}, u32[]{:S(2)}, u32[]{:S(2)}) collective-permute-start(bf16[4,2,32,512]{3,2,1,0:T(8,128)(2,1)S(1)} %get-tuple-element.84), channel_id=1, source_target_pairs={{0,8},{1,9},{2,10},{3,11},{4,12},{5,13},{6,14},{7,15},{8,0},{9,1},... | collective-permute-start | bytes 786440 | tf_op jit(solution)/shard_map/ppermute | solution.py:230
  194.1 27.6 %collective-permute-start.12 = (bf16[4,2,32,512]{3,2,1,0:T(8,128)(2,1)S(1)}, bf16[4,2,32,512]{3,2,1,0:T(8,128)(2,1)S(1)}, u32[]{:S(2)}, u32[]{:S(2)}) collective-permute-start(bf16[4,2,32,512]{3,2,1,0:T(8,128)(2,1)S(1)} %get-tuple-element.85), channel_id=1, source_target_pairs={{0,12},{1,13},{2,14},{3,15},{4,8},{5,9},{6,10},{7,11},{8,4},{9,5},... | collective-permute-start | bytes 786440 | tf_op jit(solution)/shard_map/ppermute | solution.py:230
  (28 other events, 307.5 us)

commit v2 on v0

--- a/solution.py
+++ b/solution.py
@@ -1,7 +1,14 @@
+import functools
+
 import jax
 import jax.numpy as jnp
 from jax import lax
+from jax.experimental import pallas as pl
+from jax.experimental.pallas import tpu as pltpu
 from jax.sharding import PartitionSpec as P
+
+PLANE = 4
+VMEM_LIMIT = 32 * 1024 * 1024
 
 
 def batched_product(left_operand, right_operand):
@@ -10,7 +17,7 @@
     )
 
 
-def shards(spectra, fold_counts, inverse_wavelet):
+def plain_shards(spectra, fold_counts, inverse_wavelet):
     points = spectra.shape[3]
     everyone = jnp.arange(points, dtype=jnp.int32)
     regrouped = lax.all_to_all(spectra, "shot", split_axis=2, concat_axis=0, tiled=True)
@@ -40,7 +47,324 @@
     return lax.all_to_all(result, "shot", split_axis=0, concat_axis=2, tiled=True)
 
 
+def any_spec():
+    return pl.BlockSpec(memory_space=pl.ANY)
+
+
+def vmem_spec():
+    return pl.BlockSpec(memory_space=pltpu.VMEM)
+
+
+def smem_spec():
+    return pl.BlockSpec(memory_space=pltpu.SMEM)
+
+
+def params():
+    return pltpu.CompilerParams(vmem_limit_bytes=VMEM_LIMIT)
+
+
+COST = pl.CostEstimate(flops=0, bytes_accessed=0, transcendentals=0)
+PACE = pl.CostEstimate(flops=40_000_000_000, bytes_accessed=0, transcendentals=0)
+
+
+def split_order(me, n, shots, wanted):
+    rows, count = n * shots, PLANE * shots
+    source = lax.broadcasted_iota(jnp.int32, (count, rows), 1)
+    target = lax.broadcasted_iota(jnp.int32, (count, rows), 0)
+    parts = []
+    for j in wanted:
+        which = ((me // PLANE) ^ j) * PLANE + target // shots
+        parts.append((target % shots) * n + which == source)
+    return jnp.concatenate(
+        [jnp.where(part, 1.0, 0.0).astype(jnp.bfloat16) for part in parts], axis=0
+    )
+
+
+def merge_order(me, n, shots):
+    rows = n * shots
+    source = lax.broadcasted_iota(jnp.int32, (rows, rows), 1)
+    target = lax.broadcasted_iota(jnp.int32, (rows, rows), 0)
+    block = (target % n) ^ ((me // PLANE) * PLANE)
+    return jnp.where(block * shots + target // n == source, 1.0, 0.0).astype(
+        jnp.bfloat16
+    )
+
+
+def relayout_kernel(n, shots, wanted, me_ref, x_ref, *refs):
+    outs = refs[-len(wanted) :]
+    me = me_ref[0]
+    order = split_order(me, n, shots, wanted)
+    points = x_ref.shape[3]
+    for c in range(2):
+        rows = x_ref[:, c].reshape(shots * n, points)
+        moved = jnp.dot(order, rows, preferred_element_type=jnp.float32)
+        moved = moved.astype(jnp.bfloat16).reshape(-1, PLANE, shots, points)
+        for at, out in enumerate(outs):
+            out[:, c] = moved[at]
+
+
+def relayout(me, spectra, k, n, wanted, after):
+    shots, _, _, points = spectra.shape
+    block = jax.ShapeDtypeStruct((PLANE, 2, shots, points), spectra.dtype)
+    return pl.pallas_call(
+        functools.partial(relayout_kernel, n, shots, wanted),
+        grid=(1,),
+        out_shape=[block] * len(wanted),
+        in_specs=[
+            smem_spec(),
+            pl.BlockSpec((shots, 2, n, points), lambda _: (0, 0, k, 0)),
+        ]
+        + [any_spec()] * len(after),
+        out_specs=[pl.BlockSpec(block.shape, lambda _: (0, 0, 0, 0))] * len(wanted),
+        compiler_params=params(),
+        cost_estimate=PACE,
+        name="relayout",
+    )(me, spectra, *after)
+
+
+def join_kernel(count_in, *refs):
+    out = refs[-1]
+    for at in range(count_in):
+        out[at] = refs[at][...]
+
+
+def join(blocks, after):
+    block = blocks[0]
+    return pl.pallas_call(
+        functools.partial(join_kernel, len(blocks)),
+        out_shape=jax.ShapeDtypeStruct((len(blocks), *block.shape), block.dtype),
+        in_specs=[vmem_spec()] * len(blocks) + [any_spec()] * len(after),
+        out_specs=vmem_spec(),
+        compiler_params=params(),
+        cost_estimate=COST,
+        name="join",
+    )(*blocks, *after)
+
+
+def release_kernel(count, *refs):
+    for block, out in zip(refs[:count], refs[-count:]):
+        out[...] = block[...]
+
+
+def release(blocks, after):
+    return pl.pallas_call(
+        functools.partial(release_kernel, len(blocks)),
+        out_shape=[jax.ShapeDtypeStruct(block.shape, block.dtype) for block in blocks],
+        in_specs=[vmem_spec()] * len(blocks) + [any_spec()] * len(after),
+        out_specs=[vmem_spec()] * len(blocks),
+        compiler_params=params(),
+        cost_estimate=PACE,
+        name="release",
+    )(*blocks, *after)
+
+
+def product_kernel(k, n, planes, me_ref, wave_ref, fold_row_ref, fold_col_ref, *refs):
+    near_ref, far_ref, core_ref = refs[:3]
+    outs, raw_ref, full_ref = refs[-planes - 2 : -2], refs[-2], refs[-1]
+    me = me_ref[0]
+    shots, points = near_ref.shape[3:]
+
+    def rows_of(j, i):
+        start = ((PLANE * j + i) ^ me) * shots
+        return pl.ds(pl.multiple_of(start, shots), shots)
+
+    def block(j, i, b, c):
+        if i % 2:
+            return core_ref[i // 2, j, b, c]
+        return (far_ref if i // 2 else near_ref)[j, b, c]
+
+    s = lax.broadcasted_iota(jnp.int32, (points, points), 0)
+    x = lax.broadcasted_iota(jnp.int32, (points, points), 1)
+    apart = jnp.abs(x - s)
+    recorded = apart < fold_col_ref[...]
+    mirrored = apart < fold_row_ref[...]
+
+    def dot(left, right):
+        return jnp.dot(left, right, preferred_element_type=jnp.float32)
+
+    half = planes * shots
+    for b in range(PLANE):
+        for c in range(2):
+            for j in range(planes):
+                for i in range(PLANE):
+                    raw_ref[b, c, rows_of(j, i), :] = block(j, i, b, c)
+            own = raw_ref[b, c].astype(jnp.float32)
+            full_ref[b, c] = jnp.where(
+                recorded, own, jnp.where(mirrored, own.T, 0.0)
+            ).astype(jnp.bfloat16)
+        left = jnp.concatenate(
+            [full_ref[b, c, rows_of(j, 0), :] for c in range(2) for j in range(planes)],
+            axis=0,
+        )
+        by_re, by_im = dot(left, full_ref[b, 0]), dot(left, full_ref[b, 1])
+        prod_re = by_re[:half] - by_im[half:]
+        prod_im = by_im[:half] + by_re[half:]
+        which = k * n + (me // PLANE) * PLANE + b
+        wave_re, wave_im = wave_ref[0, which], wave_ref[1, which]
+        made_re = (-(wave_re * prod_re - wave_im * prod_im)).astype(jnp.bfloat16)
+        made_im = (-(wave_re * prod_im + wave_im * prod_re)).astype(jnp.bfloat16)
+        for j, out in enumerate(outs):
+            out[b, 0] = made_re[j * shots : (j + 1) * shots]
+            out[b, 1] = made_im[j * shots : (j + 1) * shots]
+
+
+def product(me, wave, fold, near, far, core, k, n, after):
+    planes, _, _, shots, points = near.shape
+    block = jax.ShapeDtypeStruct(near.shape[1:], near.dtype)
+    return pl.pallas_call(
+        functools.partial(product_kernel, k, n, planes),
+        out_shape=[block] * planes,
+        in_specs=[smem_spec()] * 2 + [vmem_spec()] * 5 + [any_spec()] * len(after),
+        out_specs=[vmem_spec()] * planes,
+        scratch_shapes=[pltpu.VMEM((PLANE, 2, points, points), jnp.bfloat16)] * 2,
+        compiler_params=params(),
+        cost_estimate=COST,
+        name="product",
+    )(me, wave, fold.reshape(1, -1), fold.reshape(-1, 1), near, far, core, *after)
+
+
+def assemble_kernel(n, shots, planes, me_ref, *refs):
+    ins, out_ref = refs[:planes], refs[-1]
+    me = me_ref[0]
+    order = merge_order(me, n, shots)
+    points = out_ref.shape[3]
+    for c in range(2):
+        rows = jnp.concatenate(
+            [block[:, c].reshape(PLANE * shots, points) for block in ins], axis=0
+        )
+        moved = jnp.dot(order, rows, preferred_element_type=jnp.float32)
+        out_ref[:, c] = moved.astype(jnp.bfloat16).reshape(shots, n, points)
+
+
+def assemble(me, blocks, result, k, n, bins, after):
+    planes = len(blocks)
+    _, _, shots, points = blocks[0].shape
+    extra = [] if result is None else [result]
+    return pl.pallas_call(
+        functools.partial(assemble_kernel, n, shots, planes),
+        grid=(1,),
+        out_shape=jax.ShapeDtypeStruct((shots, 2, bins, points), jnp.bfloat16),
+        in_specs=[smem_spec()]
+        + [pl.BlockSpec(blocks[0].shape, lambda _: (0, 0, 0, 0))] * planes
+        + [any_spec()] * len(extra + after),
+        out_specs=pl.BlockSpec((shots, 2, n, points), lambda _: (0, 0, k, 0)),
+        input_output_aliases={1 + planes: 0} if extra else {},
+        compiler_params=params(),
+        cost_estimate=COST,
+        name="assemble",
+    )(me, *blocks, *extra, *after)
+
+
+def send(block, n, offset, what):
+    with jax.named_scope(what):
+        return lax.ppermute(block, "shot", [(d, d ^ offset) for d in range(n)])
+
+
+def chunked_shards(n, spectra, fold_counts, inverse_wavelet):
+    bins = spectra.shape[2]
+    chunks, planes = bins // n, n // PLANE
+    cross = list(reversed(range(planes // 2, planes)))
+    rest = list(range(1, planes // 2))
+    me = lax.axis_index("shot").astype(jnp.int32).reshape(1)
+
+    last = []
+    crossed = []
+
+    def order():
+        return last[-1:] + crossed[-2:-1]
+
+    def depart(blocks, what):
+        for j, block in blocks.items():
+            if j:
+                blocks[j] = send(block, n, PLANE * j, f"{what}_z{j}")
+            if j in cross:
+                crossed.append(blocks[j])
+        return blocks
+
+    arrived = [{} for _ in range(chunks)]
+    beside = [{} for _ in range(chunks)]
+    made = [{} for _ in range(chunks)]
+    leaving = [{} for _ in range(chunks)]
+    result = [None]
+
+    def parts(at):
+        return [cross[at]] + (([0] + rest) if at == len(cross) - 1 else [])
+
+    def go_in(k, at):
+        if k >= chunks:
+            return
+        wanted = parts(at)
+        with jax.named_scope(f"in{k}_{at}"):
+            blocks = relayout(me, spectra, k, n, wanted, order())
+        last.append(blocks[0])
+        arrived[k].update(depart(dict(zip(wanted, blocks)), f"in{k}"))
+
+    def go_out(k, at):
+        if not 0 <= k < chunks:
+            return
+        wanted = parts(at)
+        with jax.named_scope(f"out{k}_{at}"):
+            blocks = release([made[k][j] for j in wanted], order())
+        last.append(blocks[0])
+        leaving[k].update(depart(dict(zip(wanted, blocks)), f"out{k}"))
+
+    def go_y(k):
+        if not 0 <= k < chunks:
+            return
+        with jax.named_scope(f"y{k}"):
+            near = join([arrived[k][j] for j in range(planes)], last[-1:])
+        last.append(near)
+        beside[k] = near, send(near, n, 2, f"in{k}_y")
+
+    def go_core(k):
+        if not 0 <= k < chunks:
+            return
+        with jax.named_scope(f"core{k}"):
+            both = join(beside[k], last[-1:])
+        last.append(both)
+        beside[k] += (send(both, n, 1, f"in{k}_core"),)
+
+    def multiply(k):
+        if not 0 <= k < chunks:
+            return
+        with jax.named_scope(f"chunk{k}"):
+            blocks = product(
+                me, inverse_wavelet, fold_counts, *beside[k], k, n, last[-1:]
+            )
+        last.append(blocks[0])
+        made[k] = dict(enumerate(blocks))
+
+    def finish(k):
+        if not 0 <= k < chunks:
+            return
+        blocks = [leaving[k][j] for j in range(planes)]
+        with jax.named_scope(f"chunk{k}"):
+            result[0] = assemble(me, blocks, result[0], k, n, bins, last[-1:])
+
+    for t in range(2 * chunks + 1):
+        for at in range(len(cross)):
+            go_in(t, at)
+            go_out(t - chunks, at)
+            if at == 0:
+                multiply(t - 3)
+        go_core(t - 2)
+        go_y(t - 1)
+        finish(t - chunks - 1)
+    return result[0]
+
+
 def solution(mesh):
+    n = mesh.shape["shot"]
+
+    def shards(spectra, fold_counts, inverse_wavelet):
+        shots, _, bins, _ = spectra.shape
+        power = n & (n - 1) == 0
+        if power and n % 16 == 0 and bins % n == 0 and shots % 16 == 0:
+            return chunked_shards(n, spectra, fold_counts, inverse_wavelet)
+        return plain_shards(spectra, fold_counts, inverse_wavelet)
+
     in_specs = (P(("groups", "shot"), None, None, None), P("groups"), P())
     out_specs = P(("groups", "shot"), None, None, None)
-    return jax.shard_map(shards, mesh=mesh, in_specs=in_specs, out_specs=out_specs, check_vma=False)
+    return jax.shard_map(
+        shards, mesh=mesh, in_specs=in_specs, out_specs=out_specs, check_vma=False
+    )

time: 246 us -> 191 us (0.78)
  blocking collectives: 112 us -> 0 us
  starting transfers between devices: 7.58 us -> 45.9 us
  Pallas kernels: 0 us -> 31.2 us
  waiting for transfers between devices: 77.1 us -> 108 us
  local copies, waits for them, and re-layouts: 33.1 us -> 5.23 us
  other arithmetic: 8 us -> 0 us
  matrix products: 7.55 us -> 0 us
    all_to_all x1 -> x0, blocking collectives: 112 us -> none  [shards(): lax.all_to_all(result, 'shot', split_axis=0, concat_axis=2, tiled=True)]
    ppermute x0 -> x32, waiting for transfers between devices: none -> 108 us  [send(): return lax.ppermute(block, 'shot', [(d, d ^ offset) for d in range(n)])]
    all_to_all x1 -> x0, waiting for transfers between devices: 77.1 us -> none  [shards(): lax.all_to_all(spectra, 'shot', split_axis=2, concat_axis=0, tiled=True)]
    ppermute x0 -> x32, starting transfers between devices: none -> 45.9 us  [send(): return lax.ppermute(block, 'shot', [(d, d ^ offset) for d in range(n)])]
    pallas_call x0 -> x32, Pallas kernels: none -> 31.2 us  [the longest x4 16.5 us: product(): pl.pallas_call(functools.partial(product_kernel, k, n, planes), out_shape...]
    all_to_all x5 -> x0, local copies, waits for them, and re-layouts: 18.5 us -> none  [the longest x2 12.1 us: shards(): lax.all_to_all(spectra, 'shot', split_axis=2, concat_axis=0, tiled=True)]
    another operation x1 -> x0, local copies, waits for them, and re-layouts: 7.87 us -> none  [shards(): result = jnp.stack([output_real, out_imag], axis=1).astype(jnp.bfloat16)]
    all_to_all x1 -> x0, starting transfers between devices: 7.58 us -> none  [shards(): lax.all_to_all(spectra, 'shot', split_axis=2, concat_axis=0, tiled=True)]
  transfers between devices with their start and end apart: 1 -> 32, of which waited for: 1 -> 16; matrix products, arithmetic and copies ran while one was open for 0% -> 0% of each run, Pallas kernels for 0% -> 15%
where the time goes in v2:
time: 191 us; the launch traced here: 190 us
  waiting for transfers between devices  108 us (57%)
  starting transfers between devices  45.9 us (24%)
  Pallas kernels  31.2 us (16%)
  local copies, waits for them, and re-layouts  5.23 us (3%)
    ppermute x32, waiting for transfers between devices, send(): return lax.ppermute(block, 'shot', [(d, d ^ offset) for d in range(n)])  108 us
    ppermute x32, starting transfers between devices, send(): return lax.ppermute(block, 'shot', [(d, d ^ offset) for d in range(n)])  45.9 us
    pallas_call x4, Pallas kernels, product(): pl.pallas_call(functools.partial(product_kernel, k, n, planes), out_shape...  16.5 us
    pallas_call x4, Pallas kernels, assemble(): pl.pallas_call(functools.partial(assemble_kernel, n, shots, planes), grid...  8.65 us
    unnamed x16, local copies, waits for them, and re-layouts  5.08 us
  transfers between devices with their start and end apart: 32, of which 16 were waited for; matrix products, arithmetic and copies ran while one was open for 0% of the time, Pallas kernels for 15%

profile of v2, /device:TPU:0, one launch (start us, length us, event | category | flops | bytes accessed | tf_op | source)
XLA Modules:
  0.0 190.5 jit_solution(17513970304883188342)
XLA Ops:
  0.0 2.2 %copy-done.6 = bf16[32,2,64,512]{3,2,1,0:T(8,128)(2,1)S(1)} copy-done((bf16[32,2,64,512]{3,2,1,0:T(8,128)(2,1)S(1)}, bf16[32,2,64,512]{3,2,1,0:T(8,128)(2,1)}, u32[]{:S(2)}) %copy-start.6) | copy-done | bytes 4194328
  2.5 5.1 %collective-permute-start.2 = (bf16[4,2,32,512]{3,2,1,0:T(8,128)(2,1)S(1)}, bf16[4,2,32,512]{3,2,1,0:T(8,128)(2,1)S(1)}, u32[]{:S(2)}, u32[]{:S(2)}) collective-permute-start(bf16[4,2,32,512]{3,2,1,0:T(8,128)(2,1)S(1)} %relayout.8.refs_0_), channel_id=1, source_target_pairs={{0,12},{1,13},{2,14},{3,15},{4,8},{5,9},{6,10},{7,11},{8,4},{9,5},... | collective-permute-start | bytes 786440 | tf_op jit(solution)/shard_map/in0_z3/ppermute | solution.py:260
  9.0 5.8 %collective-permute-done.2.refs_1_.refs_3_ = bf16[4,2,32,512]{3,2,1,0:T(8,128)(2,1)S(1)} collective-permute-done((bf16[4,2,32,512]{3,2,1,0:T(8,128)(2,1)S(1)}, bf16[4,2,32,512]{3,2,1,0:T(8,128)(2,1)S(1)}, u32[]{:S(2)}, u32[]{:S(2)}) %collective-permute-start.2) | collective-permute-done | bytes 262176 | tf_op jit(solution)/shard_map/in0_z3/ppermute | solution.py:260
  14.8 2.2 %copy-done.7 = bf16[32,2,64,512]{3,2,1,0:T(8,128)(2,1)S(1)} copy-done((bf16[32,2,64,512]{3,2,1,0:T(8,128)(2,1)S(1)}, bf16[32,2,64,512]{3,2,1,0:T(8,128)(2,1)}, u32[]{:S(2)}) %copy-start.7) | copy-done | bytes 4194328
  17.3 3.8 %collective-permute-start.4 = (bf16[4,2,32,512]{3,2,1,0:T(8,128)(2,1)S(1)}, bf16[4,2,32,512]{3,2,1,0:T(8,128)(2,1)S(1)}, u32[]{:S(2)}, u32[]{:S(2)}) collective-permute-start(bf16[4,2,32,512]{3,2,1,0:T(8,128)(2,1)S(1)} %relayout.10.refs_0_), channel_id=1, source_target_pairs={{0,12},{1,13},{2,14},{3,15},{4,8},{5,9},{6,10},{7,11},{8,4},{9,5},... | collective-permute-start | bytes 786440 | tf_op jit(solution)/shard_map/in1_z3/ppermute | solution.py:260
  21.2 15.3 %collective-permute-done.1.refs_1_.refs_2_ = bf16[4,2,32,512]{3,2,1,0:T(8,128)(2,1)S(1)} collective-permute-done((bf16[4,2,32,512]{3,2,1,0:T(8,128)(2,1)S(1)}, bf16[4,2,32,512]{3,2,1,0:T(8,128)(2,1)S(1)}, u32[]{:S(2)}, u32[]{:S(2)}) %collective-permute-start.1) | collective-permute-done | bytes 262176 | tf_op jit(solution)/shard_map/in0_z2/ppermute | solution.py:260
  37.2 3.2 %collective-permute-start.5 = (bf16[4,2,32,512]{3,2,1,0:T(8,128)(2,1)S(1)}, bf16[4,2,32,512]{3,2,1,0:T(8,128)(2,1)S(1)}, u32[]{:S(2)}, u32[]{:S(2)}) collective-permute-start(bf16[4,2,32,512]{3,2,1,0:T(8,128)(2,1)S(1)} %get-tuple-element.48.refs_4_), channel_id=1, source_target_pairs={{0,8},{1,9},{2,10},{3,11},{4,12},{5,13},{6,14},{7,15},{8,0},{9,1},... | collective-permute-start | bytes 786440 | tf_op jit(solution)/shard_map/in1_z2/ppermute | solution.py:260
  43.6 15.4 %collective-permute-done.5.refs_1_.refs_2_ = bf16[4,2,32,512]{3,2,1,0:T(8,128)(2,1)S(1)} collective-permute-done((bf16[4,2,32,512]{3,2,1,0:T(8,128)(2,1)S(1)}, bf16[4,2,32,512]{3,2,1,0:T(8,128)(2,1)S(1)}, u32[]{:S(2)}, u32[]{:S(2)}) %collective-permute-start.5) | collective-permute-done | bytes 262176 | tf_op jit(solution)/shard_map/in1_z2/ppermute | solution.py:260
  59.6 3.2 %collective-permute-start.9 = (bf16[4,2,32,512]{3,2,1,0:T(8,128)(2,1)S(1)}, bf16[4,2,32,512]{3,2,1,0:T(8,128)(2,1)S(1)}, u32[]{:S(2)}, u32[]{:S(2)}) collective-permute-start(bf16[4,2,32,512]{3,2,1,0:T(8,128)(2,1)S(1)} %get-tuple-element.49.refs_2_), channel_id=1, source_target_pairs={{0,8},{1,9},{2,10},{3,11},{4,12},{5,13},{6,14},{7,15},{8,0},{9,1},... | collective-permute-start | bytes 786440 | tf_op jit(solution)/shard_map/in2_z2/ppermute | solution.py:260
  65.1 1.6 collective-permute-start.12
  67.2 4.1 %product.4 = (bf16[4,2,32,512]{3,2,1,0:T(8,128)(2,1)S(1)}, bf16[4,2,32,512]{3,2,1,0:T(8,128)(2,1)S(1)}, bf16[4,2,32,512]{3,2,1,0:T(8,128)(2,1)S(1)}, bf16[4,2,32,512]{3,2,1,0:T(8,128)(2,1)S(1)}) custom-call(s32[1]{0:T(128)} %bitcast.me_ref, f32[2,64]{1,0:T(2,128)S(1)} %copy-done.5, s32[1,512]{1,0:T(1,128)S(1)} %bitcast.4, s32[512,1]{1,0:T(8,128)S(1)} %copy.10.fold_col_ref, ...), custom_call_target="tpu_custom_call" | custom-call | tf_op jit(solution)/shard_map/chunk0/product/pallas_call | solution.py:214
  71.3 10.1 %collective-permute-done.9.refs_1_.refs_2_ = bf16[4,2,32,512]{3,2,1,0:T(8,128)(2,1)S(1)} collective-permute-done((bf16[4,2,32,512]{3,2,1,0:T(8,128)(2,1)S(1)}, bf16[4,2,32,512]{3,2,1,0:T(8,128)(2,1)S(1)}, u32[]{:S(2)}, u32[]{:S(2)}) %collective-permute-start.9) | collective-permute-done | bytes 262176 | tf_op jit(solution)/shard_map/in2_z2/ppermute | solution.py:260
  82.1 3.2 %collective-permute-start.11 = (bf16[4,2,32,512]{3,2,1,0:T(8,128)(2,1)S(1)}, bf16[4,2,32,512]{3,2,1,0:T(8,128)(2,1)S(1)}, u32[]{:S(2)}, u32[]{:S(2)}) collective-permute-start(bf16[4,2,32,512]{3,2,1,0:T(8,128)(2,1)S(1)} %get-tuple-element.55.refs_2_), channel_id=1, source_target_pairs={{0,8},{1,9},{2,10},{3,11},{4,12},{5,13},{6,14},{7,15},{8,0},{9,1},... | collective-permute-start | bytes 786440 | tf_op jit(solution)/shard_map/in3_z2/ppermute | solution.py:260
  85.3 3.5 %collective-permute-done.14.refs_1_ = bf16[4,4,2,32,512]{4,3,2,1,0:T(8,128)(2,1)S(1)} collective-permute-done((bf16[4,4,2,32,512]{4,3,2,1,0:T(8,128)(2,1)S(1)}, bf16[4,4,2,32,512]{4,3,2,1,0:T(8,128)(2,1)S(1)}, u32[]{:S(2)}, u32[]{:S(2)}) %collective-permute-start.14) | collective-permute-done | bytes 1048608 | tf_op jit(solution)/shard_map/in1_y/ppermute | solution.py:260
  93.2 4.1 %product.5 = (bf16[4,2,32,512]{3,2,1,0:T(8,128)(2,1)S(1)}, bf16[4,2,32,512]{3,2,1,0:T(8,128)(2,1)S(1)}, bf16[4,2,32,512]{3,2,1,0:T(8,128)(2,1)S(1)}, bf16[4,2,32,512]{3,2,1,0:T(8,128)(2,1)S(1)}) custom-call(s32[1]{0:T(128)} %bitcast.me_ref, f32[2,64]{1,0:T(2,128)S(1)} %copy-done.5, s32[1,512]{1,0:T(1,128)S(1)} %bitcast.5, s32[512,1]{1,0:T(8,128)S(1)} %copy.10.fold_col_ref, ...), custom_call_target="tpu_custom_call" | custom-call | tf_op jit(solution)/shard_map/chunk1/product/pallas_call | solution.py:214
  97.3 6.7 %collective-permute-done.11.refs_4_.refs_2_ = bf16[4,2,32,512]{3,2,1,0:T(8,128)(2,1)S(1)} collective-permute-done((bf16[4,2,32,512]{3,2,1,0:T(8,128)(2,1)S(1)}, bf16[4,2,32,512]{3,2,1,0:T(8,128)(2,1)S(1)}, u32[]{:S(2)}, u32[]{:S(2)}) %collective-permute-start.11) | collective-permute-done | bytes 262176 | tf_op jit(solution)/shard_map/in3_z2/ppermute | solution.py:260
  104.7 3.2 %collective-permute-start.20 = (bf16[4,2,32,512]{3,2,1,0:T(8,128)(2,1)S(1)}, bf16[4,2,32,512]{3,2,1,0:T(8,128)(2,1)S(1)}, u32[]{:S(2)}, u32[]{:S(2)}) collective-permute-start(bf16[4,2,32,512]{3,2,1,0:T(8,128)(2,1)S(1)} %get-tuple-element.62.refs_2_), channel_id=1, source_target_pairs={{0,8},{1,9},{2,10},{3,11},{4,12},{5,13},{6,14},{7,15},{8,0},{9,1},... | collective-permute-start | bytes 786440 | tf_op jit(solution)/shard_map/out0_z2/ppermute | solution.py:260
  107.9 6.8 %collective-permute-done.15.refs_1_ = bf16[4,4,2,32,512]{4,3,2,1,0:T(8,128)(2,1)S(1)} collective-permute-done((bf16[4,4,2,32,512]{4,3,2,1,0:T(8,128)(2,1)S(1)}, bf16[4,4,2,32,512]{4,3,2,1,0:T(8,128)(2,1)S(1)}, u32[]{:S(2)}, u32[]{:S(2)}) %collective-permute-start.15) | collective-permute-done | bytes 1048608 | tf_op jit(solution)/shard_map/in2_y/ppermute | solution.py:260
  119.1 4.3 %product.6 = (bf16[4,2,32,512]{3,2,1,0:T(8,128)(2,1)S(1)}, bf16[4,2,32,512]{3,2,1,0:T(8,128)(2,1)S(1)}, bf16[4,2,32,512]{3,2,1,0:T(8,128)(2,1)S(1)}, bf16[4,2,32,512]{3,2,1,0:T(8,128)(2,1)S(1)}) custom-call(s32[1]{0:T(128)} %bitcast.me_ref, f32[2,64]{1,0:T(2,128)S(1)} %copy-done.5, s32[1,512]{1,0:T(1,128)S(1)} %bitcast.6, s32[512,1]{1,0:T(8,128)S(1)} %copy.10.fold_col_ref, ...), custom_call_target="tpu_custom_call" | custom-call | tf_op jit(solution)/shard_map/chunk2/product/pallas_call | solution.py:214
  124.5 2.3 %collective-permute-start.23 = (bf16[4,2,32,512]{3,2,1,0:T(8,128)(2,1)S(1)}, bf16[4,2,32,512]{3,2,1,0:T(8,128)(2,1)S(1)}, u32[]{:S(2)}, u32[]{:S(2)}) collective-permute-start(bf16[4,2,32,512]{3,2,1,0:T(8,128)(2,1)S(1)} %get-tuple-element.67.refs_2_), channel_id=1, source_target_pairs={{0,8},{1,9},{2,10},{3,11},{4,12},{5,13},{6,14},{7,15},{8,0},{9,1},... | collective-permute-start | bytes 786440 | tf_op jit(solution)/shard_map/out1_z2/ppermute | solution.py:260
  126.8 13.8 %collective-permute-done.17.refs_1_ = bf16[4,4,2,32,512]{4,3,2,1,0:T(8,128)(2,1)S(1)} collective-permute-done((bf16[4,4,2,32,512]{4,3,2,1,0:T(8,128)(2,1)S(1)}, bf16[4,4,2,32,512]{4,3,2,1,0:T(8,128)(2,1)S(1)}, u32[]{:S(2)}, u32[]{:S(2)}) %collective-permute-start.17) | collective-permute-done | bytes 1048608 | tf_op jit(solution)/shard_map/in3_y/ppermute | solution.py:260
  142.5 2.5 %collective-permute-done.21.refs_2_ = bf16[2,4,4,2,32,512]{5,4,3,2,1,0:T(8,128)(2,1)S(1)} collective-permute-done((bf16[2,4,4,2,32,512]{5,4,3,2,1,0:T(8,128)(2,1)S(1)}, bf16[2,4,4,2,32,512]{5,4,3,2,1,0:T(8,128)(2,1)S(1)}, u32[]{:S(2)}, u32[]{:S(2)}) %collective-permute-start.21) | collective-permute-done | bytes 2097184 | tf_op jit(solution)/shard_map/in3_core/ppermute | solution.py:260
  145.0 4.1 %product.7 = (bf16[4,2,32,512]{3,2,1,0:T(8,128)(2,1)S(1)}, bf16[4,2,32,512]{3,2,1,0:T(8,128)(2,1)S(1)}, bf16[4,2,32,512]{3,2,1,0:T(8,128)(2,1)S(1)}, bf16[4,2,32,512]{3,2,1,0:T(8,128)(2,1)S(1)}) custom-call(s32[1]{0:T(128)} %bitcast.me_ref, f32[2,64]{1,0:T(2,128)S(1)} %copy-done.5, s32[1,512]{1,0:T(1,128)S(1)} %bitcast.7, s32[512,1]{1,0:T(8,128)S(1)} %copy.10.fold_col_ref, ...), custom_call_target="tpu_custom_call" | custom-call | tf_op jit(solution)/shard_map/chunk3/product/pallas_call | solution.py:214
  149.5 1.7 collective-permute-start.25
  151.6 2.1 %collective-permute-start.28 = (bf16[4,2,32,512]{3,2,1,0:T(8,128)(2,1)S(1)}, bf16[4,2,32,512]{3,2,1,0:T(8,128)(2,1)S(1)}, u32[]{:S(2)}, u32[]{:S(2)}) collective-permute-start(bf16[4,2,32,512]{3,2,1,0:T(8,128)(2,1)S(1)} %release.14.refs_3_), channel_id=1, source_target_pairs={{0,12},{1,13},{2,14},{3,15},{4,8},{5,9},{6,10},{7,11},{8,4},{9,5},... | collective-permute-start | bytes 786440 | tf_op jit(solution)/shard_map/out3_z3/ppermute | solution.py:260
  153.7 18.7 %collective-permute-done.25.refs_4_.refs_2_ = bf16[4,2,32,512]{3,2,1,0:T(8,128)(2,1)S(1)} collective-permute-done((bf16[4,2,32,512]{3,2,1,0:T(8,128)(2,1)S(1)}, bf16[4,2,32,512]{3,2,1,0:T(8,128)(2,1)S(1)}, u32[]{:S(2)}, u32[]{:S(2)}) %collective-permute-start.25) | collective-permute-done | bytes 262176 | tf_op jit(solution)/shard_map/out2_z2/ppermute | solution.py:260
  172.5 2.1 %collective-permute-start.27 = (bf16[4,2,32,512]{3,2,1,0:T(8,128)(2,1)S(1)}, bf16[4,2,32,512]{3,2,1,0:T(8,128)(2,1)S(1)}, u32[]{:S(2)}, u32[]{:S(2)}) collective-permute-start(bf16[4,2,32,512]{3,2,1,0:T(8,128)(2,1)S(1)} %get-tuple-element.78.refs_5_), channel_id=1, source_target_pairs={{0,8},{1,9},{2,10},{3,11},{4,12},{5,13},{6,14},{7,15},{8,0},{9,1},... | collective-permute-start | bytes 786440 | tf_op jit(solution)/shard_map/out3_z2/ppermute | solution.py:260
  174.6 2.6 %assemble.4.refs_4_ = bf16[32,2,64,512]{3,2,1,0:T(8,128)(2,1)} custom-call(s32[1]{0:T(128)} %bitcast.me_ref, bf16[4,2,32,512]{3,2,1,0:T(8,128)(2,1)S(1)} %get-tuple-element.83.refs_0_, bf16[4,2,32,512]{3,2,1,0:T(8,128)(2,1)} %collective-permute-done.31.refs_1_, bf16[4,2,32,512]{3,2,1,0:T(8,128)(2,1)S(1)} %copy-done.3, bf16[4,2,32,512]{3,2,1,0:T(8,128)(2,1)S(1)} %copy-done.1, ...), custom_call_target="tpu_custom_call" | custom-call | tf_op jit(solution)/shard_map/chunk0/assemble/pallas_call | solution.py:243
  177.2 2.6 %assemble.5.refs_4_ = bf16[32,2,64,512]{3,2,1,0:T(8,128)(2,1)} custom-call(s32[1]{0:T(128)} %bitcast.me_ref, bf16[4,2,32,512]{3,2,1,0:T(8,128)(2,1)S(1)} %get-tuple-element.81.refs_0_, bf16[4,2,32,512]{3,2,1,0:T(8,128)(2,1)} %collective-permute-done.30.refs_1_, ...), custom_call_target="tpu_custom_call", output_to_operand_aliasing={{}: (5, {})} | custom-call | tf_op jit(solution)/shard_map/chunk1/assemble/pallas_call | solution.py:243
  179.9 1.7 assemble.6.refs_4_
  182.3 6.5 %collective-permute-done.27.refs_2_ = bf16[4,2,32,512]{3,2,1,0:T(8,128)(2,1)S(1)} collective-permute-done((bf16[4,2,32,512]{3,2,1,0:T(8,128)(2,1)S(1)}, bf16[4,2,32,512]{3,2,1,0:T(8,128)(2,1)S(1)}, u32[]{:S(2)}, u32[]{:S(2)}) %collective-permute-start.27) | collective-permute-done | bytes 262176 | tf_op jit(solution)/shard_map/out3_z2/ppermute | solution.py:260
  188.8 1.7 assemble.7
  (81 shorter events, 23.8 us)
Async XLA Ops:
  2.5 12.3 %collective-permute-start.2 = (bf16[4,2,32,512]{3,2,1,0:T(8,128)(2,1)S(1)}, bf16[4,2,32,512]{3,2,1,0:T(8,128)(2,1)S(1)}, u32[]{:S(2)}, u32[]{:S(2)}) collective-permute-start(bf16[4,2,32,512]{3,2,1,0:T(8,128)(2,1)S(1)} %relayout.8.refs_0_), channel_id=1, source_target_pairs={{0,12},{1,13},{2,14},{3,15},{4,8},{5,9},{6,10},{7,11},{8,4},{9,5},... | collective-permute-start | bytes 786440 | tf_op jit(solution)/shard_map/in0_z3/ppermute | solution.py:260
  8.2 32.2 %collective-permute-start = (bf16[4,2,32,512]{3,2,1,0:T(8,128)(2,1)S(1)}, bf16[4,2,32,512]{3,2,1,0:T(8,128)(2,1)S(1)}, u32[]{:S(2)}, u32[]{:S(2)}) collective-permute-start(bf16[4,2,32,512]{3,2,1,0:T(8,128)(2,1)S(1)} %get-tuple-element.46), channel_id=1, source_target_pairs={{0,4},{1,5},{2,6},{3,7},{4,0},{5,1},{6,2},{7,3},{8,12},{9,13},{10,... | collective-permute-start | bytes 786440 | tf_op jit(solution)/shard_map/in0_z1/ppermute | solution.py:260
  8.3 28.2 %collective-permute-start.1 = (bf16[4,2,32,512]{3,2,1,0:T(8,128)(2,1)S(1)}, bf16[4,2,32,512]{3,2,1,0:T(8,128)(2,1)S(1)}, u32[]{:S(2)}, u32[]{:S(2)}) collective-permute-start(bf16[4,2,32,512]{3,2,1,0:T(8,128)(2,1)S(1)} %get-tuple-element.47.refs_0_), channel_id=1, source_target_pairs={{0,8},{1,9},{2,10},{3,11},{4,12},{5,13},{6,14},{7,15},{8,0},{9,1},... | collective-permute-start | bytes 786440 | tf_op jit(solution)/shard_map/in0_z2/ppermute | solution.py:260
  17.3 24.7 %collective-permute-start.4 = (bf16[4,2,32,512]{3,2,1,0:T(8,128)(2,1)S(1)}, bf16[4,2,32,512]{3,2,1,0:T(8,128)(2,1)S(1)}, u32[]{:S(2)}, u32[]{:S(2)}) collective-permute-start(bf16[4,2,32,512]{3,2,1,0:T(8,128)(2,1)S(1)} %relayout.10.refs_0_), channel_id=1, source_target_pairs={{0,12},{1,13},{2,14},{3,15},{4,8},{5,9},{6,10},{7,11},{8,4},{9,5},... | collective-permute-start | bytes 786440 | tf_op jit(solution)/shard_map/in1_z3/ppermute | solution.py:260
  37.1 26.0 %collective-permute-start.7 = (bf16[4,2,32,512]{3,2,1,0:T(8,128)(2,1)S(1)}, bf16[4,2,32,512]{3,2,1,0:T(8,128)(2,1)S(1)}, u32[]{:S(2)}, u32[]{:S(2)}) collective-permute-start(bf16[4,2,32,512]{3,2,1,0:T(8,128)(2,1)S(1)} %get-tuple-element.51), channel_id=1, source_target_pairs={{0,4},{1,5},{2,6},{3,7},{4,0},{5,1},{6,2},{7,3},{8,12},{9,13},{10,... | collective-permute-start | bytes 786440 | tf_op jit(solution)/shard_map/in1_z1/ppermute | solution.py:260
  37.2 21.8 %collective-permute-start.5 = (bf16[4,2,32,512]{3,2,1,0:T(8,128)(2,1)S(1)}, bf16[4,2,32,512]{3,2,1,0:T(8,128)(2,1)S(1)}, u32[]{:S(2)}, u32[]{:S(2)}) collective-permute-start(bf16[4,2,32,512]{3,2,1,0:T(8,128)(2,1)S(1)} %get-tuple-element.48.refs_4_), channel_id=1, source_target_pairs={{0,8},{1,9},{2,10},{3,11},{4,12},{5,13},{6,14},{7,15},{8,0},{9,1},... | collective-permute-start | bytes 786440 | tf_op jit(solution)/shard_map/in1_z2/ppermute | solution.py:260
  40.5 22.4 %collective-permute-start.3 = (bf16[4,4,2,32,512]{4,3,2,1,0:T(8,128)(2,1)S(1)}, bf16[4,4,2,32,512]{4,3,2,1,0:T(8,128)(2,1)S(1)}, u32[]{:S(2)}, u32[]{:S(2)}) collective-permute-start(bf16[4,4,2,32,512]{4,3,2,1,0:T(8,128)(2,1)S(1)} %join.8.refs_0_), channel_id=1, source_target_pairs={{0,2},{1,3},{2,0},{3,1},{4,6},{5,7},{6,4},{7,5},{8,10},{9,11},{10,... | collective-permute-start | bytes 3145736 | tf_op jit(solution)/shard_map/in0_y/ppermute | solution.py:260
  42.4 22.4 %collective-permute-start.8 = (bf16[4,2,32,512]{3,2,1,0:T(8,128)(2,1)S(1)}, bf16[4,2,32,512]{3,2,1,0:T(8,128)(2,1)S(1)}, u32[]{:S(2)}, u32[]{:S(2)}) collective-permute-start(bf16[4,2,32,512]{3,2,1,0:T(8,128)(2,1)S(1)} %relayout.12.refs_0_), channel_id=1, source_target_pairs={{0,12},{1,13},{2,14},{3,15},{4,8},{5,9},{6,10},{7,11},{8,4},{9,5},... | collective-permute-start | bytes 786440 | tf_op jit(solution)/shard_map/in2_z3/ppermute | solution.py:260
  59.6 29.4 %collective-permute-start.13 = (bf16[4,2,32,512]{3,2,1,0:T(8,128)(2,1)S(1)}, bf16[4,2,32,512]{3,2,1,0:T(8,128)(2,1)S(1)}, u32[]{:S(2)}, u32[]{:S(2)}) collective-permute-start(bf16[4,2,32,512]{3,2,1,0:T(8,128)(2,1)S(1)} %get-tuple-element.57), channel_id=1, source_target_pairs={{0,4},{1,5},{2,6},{3,7},{4,0},{5,1},{6,2},{7,3},{8,12},{9,13},{10,... | collective-permute-start | bytes 786440 | tf_op jit(solution)/shard_map/in2_z1/ppermute | solution.py:260
  59.6 21.8 %collective-permute-start.9 = (bf16[4,2,32,512]{3,2,1,0:T(8,128)(2,1)S(1)}, bf16[4,2,32,512]{3,2,1,0:T(8,128)(2,1)S(1)}, u32[]{:S(2)}, u32[]{:S(2)}) collective-permute-start(bf16[4,2,32,512]{3,2,1,0:T(8,128)(2,1)S(1)} %get-tuple-element.49.refs_2_), channel_id=1, source_target_pairs={{0,8},{1,9},{2,10},{3,11},{4,12},{5,13},{6,14},{7,15},{8,0},{9,1},... | collective-permute-start | bytes 786440 | tf_op jit(solution)/shard_map/in2_z2/ppermute | solution.py:260
  63.0 4.2 %collective-permute-start.6 = (bf16[2,4,4,2,32,512]{5,4,3,2,1,0:T(8,128)(2,1)S(1)}, bf16[2,4,4,2,32,512]{5,4,3,2,1,0:T(8,128)(2,1)S(1)}, u32[]{:S(2)}, u32[]{:S(2)}) collective-permute-start(bf16[2,4,4,2,32,512]{5,4,3,2,1,0:T(8,128)(2,1)S(1)} %join.9.refs_4_), channel_id=1, source_target_pairs={{0,1},{1,0},{2,3},{3,2},{4,5},{5,4},{6,7},{7,6},{8,9},{9,8},{10,11... | collective-permute-start | bytes 6291464 | tf_op jit(solution)/shard_map/in0_core/ppermute | solution.py:260
  63.2 25.6 %collective-permute-start.14 = (bf16[4,4,2,32,512]{4,3,2,1,0:T(8,128)(2,1)S(1)}, bf16[4,4,2,32,512]{4,3,2,1,0:T(8,128)(2,1)S(1)}, u32[]{:S(2)}, u32[]{:S(2)}) collective-permute-start(bf16[4,4,2,32,512]{4,3,2,1,0:T(8,128)(2,1)S(1)} %join.10.refs_0_), channel_id=1, source_target_pairs={{0,2},{1,3},{2,0},{3,1},{4,6},{5,7},{6,4},{7,5},{8,10},{9,11},{10,... | collective-permute-start | bytes 3145736 | tf_op jit(solution)/shard_map/in1_y/ppermute | solution.py:260
  65.1 25.6 %collective-permute-start.12 = (bf16[4,2,32,512]{3,2,1,0:T(8,128)(2,1)S(1)}, bf16[4,2,32,512]{3,2,1,0:T(8,128)(2,1)S(1)}, u32[]{:S(2)}, u32[]{:S(2)}) collective-permute-start(bf16[4,2,32,512]{3,2,1,0:T(8,128)(2,1)S(1)} %relayout.14.refs_3_), channel_id=1, source_target_pairs={{0,12},{1,13},{2,14},{3,15},{4,8},{5,9},{6,10},{7,11},{8,4},{9,5},... | collective-permute-start | bytes 786440 | tf_op jit(solution)/shard_map/in3_z3/ppermute | solution.py:260
  82.0 32.9 %collective-permute-start.10 = (bf16[4,2,32,512]{3,2,1,0:T(8,128)(2,1)S(1)}, bf16[4,2,32,512]{3,2,1,0:T(8,128)(2,1)S(1)}, u32[]{:S(2)}, u32[]{:S(2)}) collective-permute-start(bf16[4,2,32,512]{3,2,1,0:T(8,128)(2,1)S(1)} %get-tuple-element.54), channel_id=1, source_target_pairs={{0,4},{1,5},{2,6},{3,7},{4,0},{5,1},{6,2},{7,3},{8,12},{9,13},{10,... | collective-permute-start | bytes 786440 | tf_op jit(solution)/shard_map/in3_z1/ppermute | solution.py:260
  82.1 21.8 %collective-permute-start.11 = (bf16[4,2,32,512]{3,2,1,0:T(8,128)(2,1)S(1)}, bf16[4,2,32,512]{3,2,1,0:T(8,128)(2,1)S(1)}, u32[]{:S(2)}, u32[]{:S(2)}) collective-permute-start(bf16[4,2,32,512]{3,2,1,0:T(8,128)(2,1)S(1)} %get-tuple-element.55.refs_2_), channel_id=1, source_target_pairs={{0,8},{1,9},{2,10},{3,11},{4,12},{5,13},{6,14},{7,15},{8,0},{9,1},... | collective-permute-start | bytes 786440 | tf_op jit(solution)/shard_map/in3_z2/ppermute | solution.py:260
  88.9 4.2 %collective-permute-start.16 = (bf16[2,4,4,2,32,512]{5,4,3,2,1,0:T(8,128)(2,1)S(1)}, bf16[2,4,4,2,32,512]{5,4,3,2,1,0:T(8,128)(2,1)S(1)}, u32[]{:S(2)}, u32[]{:S(2)}) collective-permute-start(bf16[2,4,4,2,32,512]{5,4,3,2,1,0:T(8,128)(2,1)S(1)} %join.11.refs_4_), channel_id=1, source_target_pairs={{0,1},{1,0},{2,3},{3,2},{4,5},{5,4},{6,7},{7,6},{8,9},{9,8},{10,11... | collective-permute-start | bytes 6291464 | tf_op jit(solution)/shard_map/in1_core/ppermute | solution.py:260
  89.1 25.6 %collective-permute-start.15 = (bf16[4,4,2,32,512]{4,3,2,1,0:T(8,128)(2,1)S(1)}, bf16[4,4,2,32,512]{4,3,2,1,0:T(8,128)(2,1)S(1)}, u32[]{:S(2)}, u32[]{:S(2)}) collective-permute-start(bf16[4,4,2,32,512]{4,3,2,1,0:T(8,128)(2,1)S(1)} %join.12.refs_1_.refs_0_), channel_id=1, source_target_pairs={{0,2},{1,3},{2,0},{3,1},{4,6},{5,7},{6,4},{7,5},{8,10},{9,11},{10,... | collective-permute-start | bytes 3145736 | tf_op jit(solution)/shard_map/in2_y/ppermute | solution.py:260
  90.7 25.9 %collective-permute-start.19 = (bf16[4,2,32,512]{3,2,1,0:T(8,128)(2,1)S(1)}, bf16[4,2,32,512]{3,2,1,0:T(8,128)(2,1)S(1)}, u32[]{:S(2)}, u32[]{:S(2)}) collective-permute-start(bf16[4,2,32,512]{3,2,1,0:T(8,128)(2,1)S(1)} %release.8.refs_3_), channel_id=1, source_target_pairs={{0,12},{1,13},{2,14},{3,15},{4,8},{5,9},{6,10},{7,11},{8,4},{9,5},... | collective-permute-start | bytes 786440 | tf_op jit(solution)/shard_map/out0_z3/ppermute | solution.py:260
  104.7 67.8 %collective-permute-start.31 = (bf16[4,2,32,512]{3,2,1,0:T(8,128)(2,1)}, bf16[4,2,32,512]{3,2,1,0:T(8,128)(2,1)}, u32[]{:S(2)}, u32[]{:S(2)}) collective-permute-start(bf16[4,2,32,512]{3,2,1,0:T(8,128)(2,1)} %get-tuple-element.84), channel_id=1, source_target_pairs={{0,4},{1,5},{2,6},{3,7},{4,0},{5,1},{6,2},{7,3},{8,12},{9,13},{10,... | collective-permute-start | bytes 786440 | tf_op jit(solution)/shard_map/out0_z1/ppermute | solution.py:260
  104.7 18.7 %collective-permute-start.20 = (bf16[4,2,32,512]{3,2,1,0:T(8,128)(2,1)S(1)}, bf16[4,2,32,512]{3,2,1,0:T(8,128)(2,1)S(1)}, u32[]{:S(2)}, u32[]{:S(2)}) collective-permute-start(bf16[4,2,32,512]{3,2,1,0:T(8,128)(2,1)S(1)} %get-tuple-element.62.refs_2_), channel_id=1, source_target_pairs={{0,8},{1,9},{2,10},{3,11},{4,12},{5,13},{6,14},{7,15},{8,0},{9,1},... | collective-permute-start | bytes 786440 | tf_op jit(solution)/shard_map/out0_z2/ppermute | solution.py:260
  114.8 4.2 %collective-permute-start.18 = (bf16[2,4,4,2,32,512]{5,4,3,2,1,0:T(8,128)(2,1)S(1)}, bf16[2,4,4,2,32,512]{5,4,3,2,1,0:T(8,128)(2,1)S(1)}, u32[]{:S(2)}, u32[]{:S(2)}) collective-permute-start(bf16[2,4,4,2,32,512]{5,4,3,2,1,0:T(8,128)(2,1)S(1)} %join.13.refs_4_), channel_id=1, source_target_pairs={{0,1},{1,0},{2,3},{3,2},{4,5},{5,4},{6,7},{7,6},{8,9},{9,8},{10,11... | collective-permute-start | bytes 6291464 | tf_op jit(solution)/shard_map/in2_core/ppermute | solution.py:260
  115.0 25.6 %collective-permute-start.17 = (bf16[4,4,2,32,512]{4,3,2,1,0:T(8,128)(2,1)S(1)}, bf16[4,4,2,32,512]{4,3,2,1,0:T(8,128)(2,1)S(1)}, u32[]{:S(2)}, u32[]{:S(2)}) collective-permute-start(bf16[4,4,2,32,512]{4,3,2,1,0:T(8,128)(2,1)S(1)} %join.14.refs_1_.refs_0_), channel_id=1, source_target_pairs={{0,2},{1,3},{2,0},{3,1},{4,6},{5,7},{6,4},{7,5},{8,10},{9,11},{10,... | collective-permute-start | bytes 3145736 | tf_op jit(solution)/shard_map/in3_y/ppermute | solution.py:260
  117.3 23.5 %collective-permute-start.22 = (bf16[4,2,32,512]{3,2,1,0:T(8,128)(2,1)S(1)}, bf16[4,2,32,512]{3,2,1,0:T(8,128)(2,1)S(1)}, u32[]{:S(2)}, u32[]{:S(2)}) collective-permute-start(bf16[4,2,32,512]{3,2,1,0:T(8,128)(2,1)S(1)} %release.10.refs_3_), channel_id=1, source_target_pairs={{0,12},{1,13},{2,14},{3,15},{4,8},{5,9},{6,10},{7,11},{8,4},{9,5},... | collective-permute-start | bytes 786440 | tf_op jit(solution)/shard_map/out1_z3/ppermute | solution.py:260
  124.2 53.0 %collective-permute-start.30 = (bf16[4,2,32,512]{3,2,1,0:T(8,128)(2,1)}, bf16[4,2,32,512]{3,2,1,0:T(8,128)(2,1)}, u32[]{:S(2)}, u32[]{:S(2)}) collective-permute-start(bf16[4,2,32,512]{3,2,1,0:T(8,128)(2,1)} %get-tuple-element.82), channel_id=1, source_target_pairs={{0,4},{1,5},{2,6},{3,7},{4,0},{5,1},{6,2},{7,3},{8,12},{9,13},{10,... | collective-permute-start | bytes 786440 | tf_op jit(solution)/shard_map/out1_z1/ppermute | solution.py:260
  124.5 24.5 %collective-permute-start.23 = (bf16[4,2,32,512]{3,2,1,0:T(8,128)(2,1)S(1)}, bf16[4,2,32,512]{3,2,1,0:T(8,128)(2,1)S(1)}, u32[]{:S(2)}, u32[]{:S(2)}) collective-permute-start(bf16[4,2,32,512]{3,2,1,0:T(8,128)(2,1)S(1)} %get-tuple-element.67.refs_2_), channel_id=1, source_target_pairs={{0,8},{1,9},{2,10},{3,11},{4,12},{5,13},{6,14},{7,15},{8,0},{9,1},... | collective-permute-start | bytes 786440 | tf_op jit(solution)/shard_map/out1_z2/ppermute | solution.py:260
  140.8 4.2 %collective-permute-start.21 = (bf16[2,4,4,2,32,512]{5,4,3,2,1,0:T(8,128)(2,1)S(1)}, bf16[2,4,4,2,32,512]{5,4,3,2,1,0:T(8,128)(2,1)S(1)}, u32[]{:S(2)}, u32[]{:S(2)}) collective-permute-start(bf16[2,4,4,2,32,512]{5,4,3,2,1,0:T(8,128)(2,1)S(1)} %join.15.refs_1_.refs_4_), channel_id=1, source_target_pairs={{0,1},{1,0},{2,3},{3,2},{4,5},{5,4},{6,7},{7,6},{8,9},{9,8},{10,11... | collective-permute-start | bytes 6291464 | tf_op jit(solution)/shard_map/in3_core/ppermute | solution.py:260
  140.9 10.7 %collective-permute-start.24 = (bf16[4,2,32,512]{3,2,1,0:T(8,128)(2,1)S(1)}, bf16[4,2,32,512]{3,2,1,0:T(8,128)(2,1)S(1)}, u32[]{:S(2)}, u32[]{:S(2)}) collective-permute-start(bf16[4,2,32,512]{3,2,1,0:T(8,128)(2,1)S(1)} %release.12.refs_3_), channel_id=1, source_target_pairs={{0,12},{1,13},{2,14},{3,15},{4,8},{5,9},{6,10},{7,11},{8,4},{9,5},... | collective-permute-start | bytes 786440 | tf_op jit(solution)/shard_map/out2_z3/ppermute | solution.py:260
  149.1 30.7 %collective-permute-start.29 = (bf16[4,2,32,512]{3,2,1,0:T(8,128)(2,1)S(1)}, bf16[4,2,32,512]{3,2,1,0:T(8,128)(2,1)S(1)}, u32[]{:S(2)}, u32[]{:S(2)}) collective-permute-start(bf16[4,2,32,512]{3,2,1,0:T(8,128)(2,1)S(1)} %get-tuple-element.80), channel_id=1, source_target_pairs={{0,4},{1,5},{2,6},{3,7},{4,0},{5,1},{6,2},{7,3},{8,12},{9,13},{10,... | collective-permute-start | bytes 786440 | tf_op jit(solution)/shard_map/out2_z1/ppermute | solution.py:260
  149.5 22.8 %collective-permute-start.25 = (bf16[4,2,32,512]{3,2,1,0:T(8,128)(2,1)S(1)}, bf16[4,2,32,512]{3,2,1,0:T(8,128)(2,1)S(1)}, u32[]{:S(2)}, u32[]{:S(2)}) collective-permute-start(bf16[4,2,32,512]{3,2,1,0:T(8,128)(2,1)S(1)} %get-tuple-element.75.refs_1_.refs_5_), channel_id=1, source_target_pairs={{0,8},{1,9},{2,10},{3,11},{4,12},{5,13},{6,14},{7,15},{8,0},{9,1},... | collective-permute-start | bytes 786440 | tf_op jit(solution)/shard_map/out2_z2/ppermute | solution.py:260
  151.6 30.0 %collective-permute-start.28 = (bf16[4,2,32,512]{3,2,1,0:T(8,128)(2,1)S(1)}, bf16[4,2,32,512]{3,2,1,0:T(8,128)(2,1)S(1)}, u32[]{:S(2)}, u32[]{:S(2)}) collective-permute-start(bf16[4,2,32,512]{3,2,1,0:T(8,128)(2,1)S(1)} %release.14.refs_3_), channel_id=1, source_target_pairs={{0,12},{1,13},{2,14},{3,15},{4,8},{5,9},{6,10},{7,11},{8,4},{9,5},... | collective-permute-start | bytes 786440 | tf_op jit(solution)/shard_map/out3_z3/ppermute | solution.py:260
  172.4 9.9 %collective-permute-start.26 = (bf16[4,2,32,512]{3,2,1,0:T(8,128)(2,1)S(1)}, bf16[4,2,32,512]{3,2,1,0:T(8,128)(2,1)S(1)}, u32[]{:S(2)}, u32[]{:S(2)}) collective-permute-start(bf16[4,2,32,512]{3,2,1,0:T(8,128)(2,1)S(1)} %get-tuple-element.77), channel_id=1, source_target_pairs={{0,4},{1,5},{2,6},{3,7},{4,0},{5,1},{6,2},{7,3},{8,12},{9,13},{10,... | collective-permute-start | bytes 786440 | tf_op jit(solution)/shard_map/out3_z1/ppermute | solution.py:260
  172.5 16.3 %collective-permute-start.27 = (bf16[4,2,32,512]{3,2,1,0:T(8,128)(2,1)S(1)}, bf16[4,2,32,512]{3,2,1,0:T(8,128)(2,1)S(1)}, u32[]{:S(2)}, u32[]{:S(2)}) collective-permute-start(bf16[4,2,32,512]{3,2,1,0:T(8,128)(2,1)S(1)} %get-tuple-element.78.refs_5_), channel_id=1, source_target_pairs={{0,8},{1,9},{2,10},{3,11},{4,12},{5,13},{6,14},{7,15},{8,0},{9,1},... | collective-permute-start | bytes 786440 | tf_op jit(solution)/shard_map/out3_z2/ppermute | solution.py:260
  (8 other events, 20.8 us)

commit v3 on v2

--- a/solution.py
+++ b/solution.py
@@ -55,6 +55,10 @@
     return pl.BlockSpec(memory_space=pltpu.VMEM)
 
 
+def hbm_spec():
+    return pl.BlockSpec(memory_space=pltpu.HBM)
+
+
 def smem_spec():
     return pl.BlockSpec(memory_space=pltpu.SMEM)
 
@@ -80,14 +84,96 @@
     )
 
 
-def merge_order(me, n, shots):
-    rows = n * shots
-    source = lax.broadcasted_iota(jnp.int32, (rows, rows), 1)
-    target = lax.broadcasted_iota(jnp.int32, (rows, rows), 0)
-    block = (target % n) ^ ((me // PLANE) * PLANE)
-    return jnp.where(block * shots + target // n == source, 1.0, 0.0).astype(
-        jnp.bfloat16
-    )
+def merge_order_kernel(n, shots, me_ref, *refs):
+    out = refs[-1]
+    planes, rows, count = out.shape
+    source = lax.broadcasted_iota(jnp.int32, (rows, count), 1)
+    target = lax.broadcasted_iota(jnp.int32, (rows, count), 0)
+    for j in range(planes):
+        first = ((me_ref[0] // PLANE) ^ j) * PLANE
+        hit = (target % n - first) * shots + target // n == source
+        out[j] = jnp.where(hit, 1.0, 0.0).astype(jnp.bfloat16)
+
+
+def merge_order(me, n, shots, after):
+    return pl.pallas_call(
+        functools.partial(merge_order_kernel, n, shots),
+        out_shape=jax.ShapeDtypeStruct(
+            (n // PLANE, n * shots, PLANE * shots), jnp.bfloat16
+        ),
+        in_specs=[smem_spec()] + [any_spec()] * len(after),
+        out_specs=vmem_spec(),
+        compiler_params=params(),
+        cost_estimate=COST,
+        name="merge_order",
+    )(me, *after)
+
+
+def merged(order_ref, blocks, c):
+    total = None
+    for j, block in blocks:
+        rows = block[:, c].reshape(-1, block.shape[3])
+        part = jnp.dot(order_ref[j], rows, preferred_element_type=jnp.float32)
+        total = part if total is None else total + part
+    return total
+
+
+def early_kernel(which, order_ref, *refs):
+    ins, out = refs[: len(which)], refs[-1]
+    for c in range(2):
+        out[c] = merged(order_ref, list(zip(which, ins)), c).astype(jnp.bfloat16)
+
+
+def early(order, blocks, after, cost):
+    _, _, shots, points = next(iter(blocks.values())).shape
+    return pl.pallas_call(
+        functools.partial(early_kernel, list(blocks)),
+        out_shape=jax.ShapeDtypeStruct((2, order.shape[1], points), jnp.bfloat16),
+        in_specs=[vmem_spec()] * (1 + len(blocks)) + [any_spec()] * len(after),
+        out_specs=vmem_spec(),
+        compiler_params=params(),
+        cost_estimate=cost,
+        name="early",
+    )(order, *blocks.values(), *after)
+
+
+def assemble_kernel(n, shots, k, which, order_ref, begun_ref, *refs):
+    ins = refs[: len(which)]
+    out, held, sems = refs[-3:]
+    copies = []
+    for c in range(2):
+        total = merged(order_ref, list(zip(which, ins)), c)
+        total = total + begun_ref[c].astype(jnp.float32)
+        held[c] = total.astype(jnp.bfloat16).reshape(shots, n, -1)
+        copies.append(
+            pltpu.make_async_copy(
+                held.at[c], out.at[:, c, pl.ds(k * n, n), :], sems.at[c]
+            )
+        )
+        copies[c].start()
+    for copy in copies:
+        copy.wait()
+
+
+def assemble(order, begun, blocks, result, k, n, bins, after):
+    _, _, shots, points = next(iter(blocks.values())).shape
+    extra = [] if result is None else [result]
+    return pl.pallas_call(
+        functools.partial(assemble_kernel, n, shots, k, list(blocks)),
+        out_shape=jax.ShapeDtypeStruct((shots, 2, bins, points), jnp.bfloat16),
+        in_specs=[vmem_spec()] * (2 + len(blocks))
+        + [hbm_spec()] * len(extra)
+        + [any_spec()] * len(after),
+        out_specs=hbm_spec(),
+        scratch_shapes=[
+            pltpu.VMEM((2, shots, n, points), jnp.bfloat16),
+            pltpu.SemaphoreType.DMA((2,)),
+        ],
+        input_output_aliases={2 + len(blocks): 0} if extra else {},
+        compiler_params=params(),
+        cost_estimate=COST,
+        name="assemble",
+    )(order, begun, *blocks.values(), *extra, *after)
 
 
 def relayout_kernel(n, shots, wanted, me_ref, x_ref, *refs):
@@ -223,38 +309,6 @@
     )(me, wave, fold.reshape(1, -1), fold.reshape(-1, 1), near, far, core, *after)
 
 
-def assemble_kernel(n, shots, planes, me_ref, *refs):
-    ins, out_ref = refs[:planes], refs[-1]
-    me = me_ref[0]
-    order = merge_order(me, n, shots)
-    points = out_ref.shape[3]
-    for c in range(2):
-        rows = jnp.concatenate(
-            [block[:, c].reshape(PLANE * shots, points) for block in ins], axis=0
-        )
-        moved = jnp.dot(order, rows, preferred_element_type=jnp.float32)
-        out_ref[:, c] = moved.astype(jnp.bfloat16).reshape(shots, n, points)
-
-
-def assemble(me, blocks, result, k, n, bins, after):
-    planes = len(blocks)
-    _, _, shots, points = blocks[0].shape
-    extra = [] if result is None else [result]
-    return pl.pallas_call(
-        functools.partial(assemble_kernel, n, shots, planes),
-        grid=(1,),
-        out_shape=jax.ShapeDtypeStruct((shots, 2, bins, points), jnp.bfloat16),
-        in_specs=[smem_spec()]
-        + [pl.BlockSpec(blocks[0].shape, lambda _: (0, 0, 0, 0))] * planes
-        + [any_spec()] * len(extra + after),
-        out_specs=pl.BlockSpec((shots, 2, n, points), lambda _: (0, 0, k, 0)),
-        input_output_aliases={1 + planes: 0} if extra else {},
-        compiler_params=params(),
-        cost_estimate=COST,
-        name="assemble",
-    )(me, *blocks, *extra, *after)
-
-
 def send(block, n, offset, what):
     with jax.named_scope(what):
         return lax.ppermute(block, "shot", [(d, d ^ offset) for d in range(n)])
@@ -285,7 +339,7 @@
     beside = [{} for _ in range(chunks)]
     made = [{} for _ in range(chunks)]
     leaving = [{} for _ in range(chunks)]
-    result = [None]
+    result, merge = [None], []
 
     def parts(at):
         return [cross[at]] + (([0] + rest) if at == len(cross) - 1 else [])
@@ -334,22 +388,49 @@
         last.append(blocks[0])
         made[k] = dict(enumerate(blocks))
 
+    begun = {}
+
+    def begin_finish(k):
+        if not 0 <= k < chunks:
+            return
+        blocks = {j: leaving[k][j] for j in range(planes) if j != cross[-1]}
+        with jax.named_scope(f"chunk{k}"):
+            begun[k] = early(
+                merge[0], blocks, last[-1:], PACE if k == chunks - 2 else COST
+            )
+        last.append(begun[k])
+
     def finish(k):
         if not 0 <= k < chunks:
             return
-        blocks = [leaving[k][j] for j in range(planes)]
+        blocks = {cross[-1]: leaving[k][cross[-1]]}
         with jax.named_scope(f"chunk{k}"):
-            result[0] = assemble(me, blocks, result[0], k, n, bins, last[-1:])
-
-    for t in range(2 * chunks + 1):
+            result[0] = assemble(merge[0], begun[k], blocks, result[0], k, n, bins, [])
+
+    for t in range(chunks):
         for at in range(len(cross)):
             go_in(t, at)
-            go_out(t - chunks, at)
             if at == 0:
                 multiply(t - 3)
         go_core(t - 2)
+        if t == 1:
+            merge.append(merge_order(me, n, spectra.shape[0], last[-1:]))
+            last.append(merge[0])
         go_y(t - 1)
-        finish(t - chunks - 1)
+    for t in range(chunks):
+        go_out(t, 0)
+        if t == 0:
+            multiply(chunks - 3)
+        else:
+            go_core(chunks - 3 + t)
+            go_y(chunks - 2 + t)
+        go_out(t, 1)
+        if t:
+            multiply(chunks - 3 + t)
+        begin_finish(t - 1)
+        finish(t - 1)
+    begin_finish(chunks - 1)
+    finish(chunks - 1)
     return result[0]
 
 

time: 191 us -> 189 us (0.990)
  waiting for transfers between devices: 108 us -> 105 us
  starting transfers between devices: 45.9 us -> 47.9 us
    ppermute x32, waiting for transfers between devices: 108 us -> 105 us  [send(): return lax.ppermute(block, 'shot', [(d, d ^ offset) for d in range(n)])]
    ppermute x32, starting transfers between devices: 45.9 us -> 47.9 us  [send(): return lax.ppermute(block, 'shot', [(d, d ^ offset) for d in range(n)])]
    pallas_call x4 -> x9, Pallas kernels: 8.65 us -> 9.14 us  [the longest x4 5.08 us: assemble(): pl.pallas_call(functools.partial(assemble_kernel, n, shots, k, list(block...]
    unnamed x16 -> x14, local copies, waits for them, and re-layouts: 5.08 us -> 5.19 us
where the time goes in v3:
time: 189 us
  waiting for transfers between devices  105 us (56%)
  starting transfers between devices  47.9 us (25%)
  Pallas kernels  30.1 us (16%)
  local copies, waits for them, and re-layouts  5.33 us (3%)
    ppermute x32, waiting for transfers between devices, send(): return lax.ppermute(block, 'shot', [(d, d ^ offset) for d in range(n)])  105 us
    ppermute x32, starting transfers between devices, send(): return lax.ppermute(block, 'shot', [(d, d ^ offset) for d in range(n)])  47.9 us
    pallas_call x4, Pallas kernels, product(): pl.pallas_call(functools.partial(product_kernel, k, n, planes), out_shape...  16.4 us
    unnamed x14, local copies, waits for them, and re-layouts  5.19 us
    pallas_call x4, Pallas kernels, assemble(): pl.pallas_call(functools.partial(assemble_kernel, n, shots, k, list(block...  5.08 us
    pallas_call x4, Pallas kernels, early(): pl.pallas_call(functools.partial(early_kernel, list(blocks)), out_shape=j...  3.84 us
  transfers between devices with their start and end apart: 32, of which 16 were waited for; matrix products, arithmetic and copies ran while one was open for 0% of the time, Pallas kernels for 15%

profile of v3, /device:TPU:0, one launch (start us, length us, event | category | flops | bytes accessed | tf_op | source)
XLA Modules:
  0.0 188.7 jit_solution(15843720251646907205)
XLA Ops:
  0.0 2.2 %copy-done.4 = bf16[32,2,64,512]{3,2,1,0:T(8,128)(2,1)S(1)} copy-done((bf16[32,2,64,512]{3,2,1,0:T(8,128)(2,1)S(1)}, bf16[32,2,64,512]{3,2,1,0:T(8,128)(2,1)}, u32[]{:S(2)}) %copy-start.4) | copy-done | bytes 4194328
  2.5 5.1 %collective-permute-start = (bf16[4,2,32,512]{3,2,1,0:T(8,128)(2,1)S(1)}, bf16[4,2,32,512]{3,2,1,0:T(8,128)(2,1)S(1)}, u32[]{:S(2)}, u32[]{:S(2)}) collective-permute-start(bf16[4,2,32,512]{3,2,1,0:T(8,128)(2,1)S(1)} %relayout.8.refs_0_), channel_id=1, source_target_pairs={{0,12},{1,13},{2,14},{3,15},{4,8},{5,9},{6,10},{7,11},{8,4},{9,5},... | collective-permute-start | bytes 786440 | tf_op jit(solution)/shard_map/in0_z3/ppermute | solution.py:314
  9.0 5.8 %collective-permute-done.refs_1_.refs_3_ = bf16[4,2,32,512]{3,2,1,0:T(8,128)(2,1)S(1)} collective-permute-done((bf16[4,2,32,512]{3,2,1,0:T(8,128)(2,1)S(1)}, bf16[4,2,32,512]{3,2,1,0:T(8,128)(2,1)S(1)}, u32[]{:S(2)}, u32[]{:S(2)}) %collective-permute-start) | collective-permute-done | bytes 262176 | tf_op jit(solution)/shard_map/in0_z3/ppermute | solution.py:314
  14.8 2.2 %copy-done.5 = bf16[32,2,64,512]{3,2,1,0:T(8,128)(2,1)S(1)} copy-done((bf16[32,2,64,512]{3,2,1,0:T(8,128)(2,1)S(1)}, bf16[32,2,64,512]{3,2,1,0:T(8,128)(2,1)}, u32[]{:S(2)}) %copy-start.5) | copy-done | bytes 4194328
  17.3 3.8 %collective-permute-start.4 = (bf16[4,2,32,512]{3,2,1,0:T(8,128)(2,1)S(1)}, bf16[4,2,32,512]{3,2,1,0:T(8,128)(2,1)S(1)}, u32[]{:S(2)}, u32[]{:S(2)}) collective-permute-start(bf16[4,2,32,512]{3,2,1,0:T(8,128)(2,1)S(1)} %relayout.10.refs_0_), channel_id=1, source_target_pairs={{0,12},{1,13},{2,14},{3,15},{4,8},{5,9},{6,10},{7,11},{8,4},{9,5},... | collective-permute-start | bytes 786440 | tf_op jit(solution)/shard_map/in1_z3/ppermute | solution.py:314
  21.2 15.3 %collective-permute-done.1.refs_1_.refs_2_ = bf16[4,2,32,512]{3,2,1,0:T(8,128)(2,1)S(1)} collective-permute-done((bf16[4,2,32,512]{3,2,1,0:T(8,128)(2,1)S(1)}, bf16[4,2,32,512]{3,2,1,0:T(8,128)(2,1)S(1)}, u32[]{:S(2)}, u32[]{:S(2)}) %collective-permute-start.1) | collective-permute-done | bytes 262176 | tf_op jit(solution)/shard_map/in0_z2/ppermute | solution.py:314
  37.4 3.3 %collective-permute-start.7 = (bf16[4,2,32,512]{3,2,1,0:T(8,128)(2,1)S(1)}, bf16[4,2,32,512]{3,2,1,0:T(8,128)(2,1)S(1)}, u32[]{:S(2)}, u32[]{:S(2)}) collective-permute-start(bf16[4,2,32,512]{3,2,1,0:T(8,128)(2,1)S(1)} %get-tuple-element.51), channel_id=1, source_target_pairs={{0,4},{1,5},{2,6},{3,7},{4,0},{5,1},{6,2},{7,3},{8,12},{9,13},{10,... | collective-permute-start | bytes 786440 | tf_op jit(solution)/shard_map/in1_z1/ppermute | solution.py:314
  44.6 14.4 %collective-permute-done.5.refs_1_.refs_2_ = bf16[4,2,32,512]{3,2,1,0:T(8,128)(2,1)S(1)} collective-permute-done((bf16[4,2,32,512]{3,2,1,0:T(8,128)(2,1)S(1)}, bf16[4,2,32,512]{3,2,1,0:T(8,128)(2,1)S(1)}, u32[]{:S(2)}, u32[]{:S(2)}) %collective-permute-start.5) | collective-permute-done | bytes 262176 | tf_op jit(solution)/shard_map/in1_z2/ppermute | solution.py:314
  59.6 3.2 %collective-permute-start.9 = (bf16[4,2,32,512]{3,2,1,0:T(8,128)(2,1)S(1)}, bf16[4,2,32,512]{3,2,1,0:T(8,128)(2,1)S(1)}, u32[]{:S(2)}, u32[]{:S(2)}) collective-permute-start(bf16[4,2,32,512]{3,2,1,0:T(8,128)(2,1)S(1)} %get-tuple-element.49.refs_2_), channel_id=1, source_target_pairs={{0,8},{1,9},{2,10},{3,11},{4,12},{5,13},{6,14},{7,15},{8,0},{9,1},... | collective-permute-start | bytes 786440 | tf_op jit(solution)/shard_map/in2_z2/ppermute | solution.py:314
  64.2 1.6 collective-permute-start.14
  66.1 1.6 collective-permute-start.12
  68.2 4.1 %product.4 = (bf16[4,2,32,512]{3,2,1,0:T(8,128)(2,1)S(1)}, bf16[4,2,32,512]{3,2,1,0:T(8,128)(2,1)S(1)}, bf16[4,2,32,512]{3,2,1,0:T(8,128)(2,1)S(1)}, bf16[4,2,32,512]{3,2,1,0:T(8,128)(2,1)S(1)}) custom-call(s32[1]{0:T(128)} %bitcast.me_ref, f32[2,64]{1,0:T(2,128)S(1)} %copy-done.3, s32[1,512]{1,0:T(1,128)S(1)} %bitcast.4, s32[512,1]{1,0:T(8,128)S(1)} %copy.10.fold_col_ref, ...), custom_call_target="tpu_custom_call" | custom-call | tf_op jit(solution)/shard_map/chunk0/product/pallas_call | solution.py:300
  72.3 9.1 %collective-permute-done.9.refs_1_.refs_2_ = bf16[4,2,32,512]{3,2,1,0:T(8,128)(2,1)S(1)} collective-permute-done((bf16[4,2,32,512]{3,2,1,0:T(8,128)(2,1)S(1)}, bf16[4,2,32,512]{3,2,1,0:T(8,128)(2,1)S(1)}, u32[]{:S(2)}, u32[]{:S(2)}) %collective-permute-start.9) | collective-permute-done | bytes 262176 | tf_op jit(solution)/shard_map/in2_z2/ppermute | solution.py:314
  82.1 3.2 %collective-permute-start.11 = (bf16[4,2,32,512]{3,2,1,0:T(8,128)(2,1)S(1)}, bf16[4,2,32,512]{3,2,1,0:T(8,128)(2,1)S(1)}, u32[]{:S(2)}, u32[]{:S(2)}) collective-permute-start(bf16[4,2,32,512]{3,2,1,0:T(8,128)(2,1)S(1)} %get-tuple-element.55.refs_2_), channel_id=1, source_target_pairs={{0,8},{1,9},{2,10},{3,11},{4,12},{5,13},{6,14},{7,15},{8,0},{9,1},... | collective-permute-start | bytes 786440 | tf_op jit(solution)/shard_map/in3_z2/ppermute | solution.py:314
  85.3 4.5 %collective-permute-done.14.refs_1_ = bf16[4,4,2,32,512]{4,3,2,1,0:T(8,128)(2,1)S(1)} collective-permute-done((bf16[4,4,2,32,512]{4,3,2,1,0:T(8,128)(2,1)S(1)}, bf16[4,4,2,32,512]{4,3,2,1,0:T(8,128)(2,1)S(1)}, u32[]{:S(2)}, u32[]{:S(2)}) %collective-permute-start.14) | collective-permute-done | bytes 1048608 | tf_op jit(solution)/shard_map/in1_y/ppermute | solution.py:314
  90.1 1.6 collective-permute-start.15
  91.7 1.6 collective-permute-start.17
  94.2 4.1 %product.5 = (bf16[4,2,32,512]{3,2,1,0:T(8,128)(2,1)S(1)}, bf16[4,2,32,512]{3,2,1,0:T(8,128)(2,1)S(1)}, bf16[4,2,32,512]{3,2,1,0:T(8,128)(2,1)S(1)}, bf16[4,2,32,512]{3,2,1,0:T(8,128)(2,1)S(1)}) custom-call(s32[1]{0:T(128)} %bitcast.me_ref, f32[2,64]{1,0:T(2,128)S(1)} %copy-done.3, s32[1,512]{1,0:T(1,128)S(1)} %bitcast.5, s32[512,1]{1,0:T(8,128)S(1)} %copy.10.fold_col_ref, ...), custom_call_target="tpu_custom_call" | custom-call | tf_op jit(solution)/shard_map/chunk1/product/pallas_call | solution.py:300
  98.3 5.7 %collective-permute-done.11.refs_4_.refs_2_ = bf16[4,2,32,512]{3,2,1,0:T(8,128)(2,1)S(1)} collective-permute-done((bf16[4,2,32,512]{3,2,1,0:T(8,128)(2,1)S(1)}, bf16[4,2,32,512]{3,2,1,0:T(8,128)(2,1)S(1)}, u32[]{:S(2)}, u32[]{:S(2)}) %collective-permute-start.11) | collective-permute-done | bytes 262176 | tf_op jit(solution)/shard_map/in3_z2/ppermute | solution.py:314
  104.1 3.2 %collective-permute-start.20 = (bf16[4,2,32,512]{3,2,1,0:T(8,128)(2,1)S(1)}, bf16[4,2,32,512]{3,2,1,0:T(8,128)(2,1)S(1)}, u32[]{:S(2)}, u32[]{:S(2)}) collective-permute-start(bf16[4,2,32,512]{3,2,1,0:T(8,128)(2,1)S(1)} %get-tuple-element.63.refs_1_), channel_id=1, source_target_pairs={{0,8},{1,9},{2,10},{3,11},{4,12},{5,13},{6,14},{7,15},{8,0},{9,1},... | collective-permute-start | bytes 786440 | tf_op jit(solution)/shard_map/out0_z2/ppermute | solution.py:314
  108.5 7.2 %collective-permute-done.15.refs_1_ = bf16[4,4,2,32,512]{4,3,2,1,0:T(8,128)(2,1)S(1)} collective-permute-done((bf16[4,4,2,32,512]{4,3,2,1,0:T(8,128)(2,1)S(1)}, bf16[4,4,2,32,512]{4,3,2,1,0:T(8,128)(2,1)S(1)}, u32[]{:S(2)}, u32[]{:S(2)}) %collective-permute-start.15) | collective-permute-done | bytes 1048608 | tf_op jit(solution)/shard_map/in2_y/ppermute | solution.py:314
  117.6 8.8 %collective-permute-done.20.refs_4_.refs_0_ = bf16[4,2,32,512]{3,2,1,0:T(8,128)(2,1)S(1)} collective-permute-done((bf16[4,2,32,512]{3,2,1,0:T(8,128)(2,1)S(1)}, bf16[4,2,32,512]{3,2,1,0:T(8,128)(2,1)S(1)}, u32[]{:S(2)}, u32[]{:S(2)}) %collective-permute-start.20) | collective-permute-done | bytes 262176 | tf_op jit(solution)/shard_map/out0_z2/ppermute | solution.py:314
  126.6 3.2 %collective-permute-start.24 = (bf16[4,2,32,512]{3,2,1,0:T(8,128)(2,1)S(1)}, bf16[4,2,32,512]{3,2,1,0:T(8,128)(2,1)S(1)}, u32[]{:S(2)}, u32[]{:S(2)}) collective-permute-start(bf16[4,2,32,512]{3,2,1,0:T(8,128)(2,1)S(1)} %get-tuple-element.66.refs_3_), channel_id=1, source_target_pairs={{0,8},{1,9},{2,10},{3,11},{4,12},{5,13},{6,14},{7,15},{8,0},{9,1},... | collective-permute-start | bytes 786440 | tf_op jit(solution)/shard_map/out1_z2/ppermute | solution.py:314
  129.7 4.1 %product.6 = (bf16[4,2,32,512]{3,2,1,0:T(8,128)(2,1)S(1)}, bf16[4,2,32,512]{3,2,1,0:T(8,128)(2,1)S(1)}, bf16[4,2,32,512]{3,2,1,0:T(8,128)(2,1)S(1)}, bf16[4,2,32,512]{3,2,1,0:T(8,128)(2,1)S(1)}) custom-call(s32[1]{0:T(128)} %bitcast.me_ref, f32[2,64]{1,0:T(2,128)S(1)} %copy-done.3, s32[1,512]{1,0:T(1,128)S(1)} %bitcast.6, s32[512,1]{1,0:T(8,128)S(1)} %copy.10.fold_col_ref, ...), custom_call_target="tpu_custom_call" | custom-call | tf_op jit(solution)/shard_map/chunk2/product/pallas_call | solution.py:300
  136.1 5.5 %collective-permute-done.18.refs_1_ = bf16[4,4,2,32,512]{4,3,2,1,0:T(8,128)(2,1)S(1)} collective-permute-done((bf16[4,4,2,32,512]{4,3,2,1,0:T(8,128)(2,1)S(1)}, bf16[4,4,2,32,512]{4,3,2,1,0:T(8,128)(2,1)S(1)}, u32[]{:S(2)}, u32[]{:S(2)}) %collective-permute-start.18) | collective-permute-done | bytes 1048608 | tf_op jit(solution)/shard_map/in3_y/ppermute | solution.py:314
  141.9 7.0 %collective-permute-done.24.refs_4_.refs_0_ = bf16[4,2,32,512]{3,2,1,0:T(8,128)(2,1)S(1)} collective-permute-done((bf16[4,2,32,512]{3,2,1,0:T(8,128)(2,1)S(1)}, bf16[4,2,32,512]{3,2,1,0:T(8,128)(2,1)S(1)}, u32[]{:S(2)}, u32[]{:S(2)}) %collective-permute-start.24) | collective-permute-done | bytes 262176 | tf_op jit(solution)/shard_map/out1_z2/ppermute | solution.py:314
  149.5 2.7 %collective-permute-start.27 = (bf16[4,2,32,512]{3,2,1,0:T(8,128)(2,1)S(1)}, bf16[4,2,32,512]{3,2,1,0:T(8,128)(2,1)S(1)}, u32[]{:S(2)}, u32[]{:S(2)}) collective-permute-start(bf16[4,2,32,512]{3,2,1,0:T(8,128)(2,1)S(1)} %get-tuple-element.73.refs_3_), channel_id=1, source_target_pairs={{0,8},{1,9},{2,10},{3,11},{4,12},{5,13},{6,14},{7,15},{8,0},{9,1},... | collective-permute-start | bytes 786440 | tf_op jit(solution)/shard_map/out2_z2/ppermute | solution.py:314
  153.5 4.1 %product.7 = (bf16[4,2,32,512]{3,2,1,0:T(8,128)(2,1)S(1)}, bf16[4,2,32,512]{3,2,1,0:T(8,128)(2,1)S(1)}, bf16[4,2,32,512]{3,2,1,0:T(8,128)(2,1)S(1)}, bf16[4,2,32,512]{3,2,1,0:T(8,128)(2,1)S(1)}) custom-call(s32[1]{0:T(128)} %bitcast.me_ref, f32[2,64]{1,0:T(2,128)S(1)} %copy-done.3, s32[1,512]{1,0:T(1,128)S(1)} %bitcast.7, s32[512,1]{1,0:T(8,128)S(1)} %copy.10.fold_col_ref, ...), custom_call_target="tpu_custom_call" | custom-call | tf_op jit(solution)/shard_map/chunk3/product/pallas_call | solution.py:300
  159.8 10.9 %collective-permute-done.27.refs_4_.refs_0_ = bf16[4,2,32,512]{3,2,1,0:T(8,128)(2,1)S(1)} collective-permute-done((bf16[4,2,32,512]{3,2,1,0:T(8,128)(2,1)S(1)}, bf16[4,2,32,512]{3,2,1,0:T(8,128)(2,1)S(1)}, u32[]{:S(2)}, u32[]{:S(2)}) %collective-permute-start.27) | collective-permute-done | bytes 262176 | tf_op jit(solution)/shard_map/out2_z2/ppermute | solution.py:314
  171.3 3.4 %collective-permute-start.31 = (bf16[4,2,32,512]{3,2,1,0:T(8,128)(2,1)S(1)}, bf16[4,2,32,512]{3,2,1,0:T(8,128)(2,1)S(1)}, u32[]{:S(2)}, u32[]{:S(2)}) collective-permute-start(bf16[4,2,32,512]{3,2,1,0:T(8,128)(2,1)S(1)} %get-tuple-element.84.refs_3_), channel_id=1, source_target_pairs={{0,8},{1,9},{2,10},{3,11},{4,12},{5,13},{6,14},{7,15},{8,0},{9,1},... | collective-permute-start | bytes 786440 | tf_op jit(solution)/shard_map/out3_z2/ppermute | solution.py:314
  178.3 2.1 %collective-permute-done.28.refs_1_ = bf16[4,2,32,512]{3,2,1,0:T(8,128)(2,1)S(1)} collective-permute-done((bf16[4,2,32,512]{3,2,1,0:T(8,128)(2,1)S(1)}, bf16[4,2,32,512]{3,2,1,0:T(8,128)(2,1)S(1)}, u32[]{:S(2)}, u32[]{:S(2)}) %collective-permute-start.28) | collective-permute-done | bytes 262176 | tf_op jit(solution)/shard_map/out3_z1/ppermute | solution.py:314
  181.4 5.9 %collective-permute-done.31.refs_0_ = bf16[4,2,32,512]{3,2,1,0:T(8,128)(2,1)S(1)} collective-permute-done((bf16[4,2,32,512]{3,2,1,0:T(8,128)(2,1)S(1)}, bf16[4,2,32,512]{3,2,1,0:T(8,128)(2,1)S(1)}, u32[]{:S(2)}, u32[]{:S(2)}) %collective-permute-start.31) | collective-permute-done | bytes 262176 | tf_op jit(solution)/shard_map/out3_z2/ppermute | solution.py:314
  (84 shorter events, 27.4 us)
Async XLA Ops:
  2.5 12.3 %collective-permute-start = (bf16[4,2,32,512]{3,2,1,0:T(8,128)(2,1)S(1)}, bf16[4,2,32,512]{3,2,1,0:T(8,128)(2,1)S(1)}, u32[]{:S(2)}, u32[]{:S(2)}) collective-permute-start(bf16[4,2,32,512]{3,2,1,0:T(8,128)(2,1)S(1)} %relayout.8.refs_0_), channel_id=1, source_target_pairs={{0,12},{1,13},{2,14},{3,15},{4,8},{5,9},{6,10},{7,11},{8,4},{9,5},... | collective-permute-start | bytes 786440 | tf_op jit(solution)/shard_map/in0_z3/ppermute | solution.py:314
  8.2 32.5 %collective-permute-start.2 = (bf16[4,2,32,512]{3,2,1,0:T(8,128)(2,1)S(1)}, bf16[4,2,32,512]{3,2,1,0:T(8,128)(2,1)S(1)}, u32[]{:S(2)}, u32[]{:S(2)}) collective-permute-start(bf16[4,2,32,512]{3,2,1,0:T(8,128)(2,1)S(1)} %get-tuple-element.48), channel_id=1, source_target_pairs={{0,4},{1,5},{2,6},{3,7},{4,0},{5,1},{6,2},{7,3},{8,12},{9,13},{10,... | collective-permute-start | bytes 786440 | tf_op jit(solution)/shard_map/in0_z1/ppermute | solution.py:314
  8.3 28.2 %collective-permute-start.1 = (bf16[4,2,32,512]{3,2,1,0:T(8,128)(2,1)S(1)}, bf16[4,2,32,512]{3,2,1,0:T(8,128)(2,1)S(1)}, u32[]{:S(2)}, u32[]{:S(2)}) collective-permute-start(bf16[4,2,32,512]{3,2,1,0:T(8,128)(2,1)S(1)} %get-tuple-element.45.refs_0_), channel_id=1, source_target_pairs={{0,8},{1,9},{2,10},{3,11},{4,12},{5,13},{6,14},{7,15},{8,0},{9,1},... | collective-permute-start | bytes 786440 | tf_op jit(solution)/shard_map/in0_z2/ppermute | solution.py:314
  17.3 25.7 %collective-permute-start.4 = (bf16[4,2,32,512]{3,2,1,0:T(8,128)(2,1)S(1)}, bf16[4,2,32,512]{3,2,1,0:T(8,128)(2,1)S(1)}, u32[]{:S(2)}, u32[]{:S(2)}) collective-permute-start(bf16[4,2,32,512]{3,2,1,0:T(8,128)(2,1)S(1)} %relayout.10.refs_0_), channel_id=1, source_target_pairs={{0,12},{1,13},{2,14},{3,15},{4,8},{5,9},{6,10},{7,11},{8,4},{9,5},... | collective-permute-start | bytes 786440 | tf_op jit(solution)/shard_map/in1_z3/ppermute | solution.py:314
  37.1 21.9 %collective-permute-start.5 = (bf16[4,2,32,512]{3,2,1,0:T(8,128)(2,1)S(1)}, bf16[4,2,32,512]{3,2,1,0:T(8,128)(2,1)S(1)}, u32[]{:S(2)}, u32[]{:S(2)}) collective-permute-start(bf16[4,2,32,512]{3,2,1,0:T(8,128)(2,1)S(1)} %get-tuple-element.46.refs_0_), channel_id=1, source_target_pairs={{0,8},{1,9},{2,10},{3,11},{4,12},{5,13},{6,14},{7,15},{8,0},{9,1},... | collective-permute-start | bytes 786440 | tf_op jit(solution)/shard_map/in1_z2/ppermute | solution.py:314
  37.4 26.7 %collective-permute-start.7 = (bf16[4,2,32,512]{3,2,1,0:T(8,128)(2,1)S(1)}, bf16[4,2,32,512]{3,2,1,0:T(8,128)(2,1)S(1)}, u32[]{:S(2)}, u32[]{:S(2)}) collective-permute-start(bf16[4,2,32,512]{3,2,1,0:T(8,128)(2,1)S(1)} %get-tuple-element.51), channel_id=1, source_target_pairs={{0,4},{1,5},{2,6},{3,7},{4,0},{5,1},{6,2},{7,3},{8,12},{9,13},{10,... | collective-permute-start | bytes 786440 | tf_op jit(solution)/shard_map/in1_z1/ppermute | solution.py:314
  41.5 22.3 %collective-permute-start.3 = (bf16[4,4,2,32,512]{4,3,2,1,0:T(8,128)(2,1)S(1)}, bf16[4,4,2,32,512]{4,3,2,1,0:T(8,128)(2,1)S(1)}, u32[]{:S(2)}, u32[]{:S(2)}) collective-permute-start(bf16[4,4,2,32,512]{4,3,2,1,0:T(8,128)(2,1)S(1)} %join.8.refs_0_), channel_id=1, source_target_pairs={{0,2},{1,3},{2,0},{3,1},{4,6},{5,7},{6,4},{7,5},{8,10},{9,11},{10,... | collective-permute-start | bytes 3145736 | tf_op jit(solution)/shard_map/in0_y/ppermute | solution.py:314
  43.4 22.4 %collective-permute-start.8 = (bf16[4,2,32,512]{3,2,1,0:T(8,128)(2,1)S(1)}, bf16[4,2,32,512]{3,2,1,0:T(8,128)(2,1)S(1)}, u32[]{:S(2)}, u32[]{:S(2)}) collective-permute-start(bf16[4,2,32,512]{3,2,1,0:T(8,128)(2,1)S(1)} %relayout.12.refs_0_), channel_id=1, source_target_pairs={{0,12},{1,13},{2,14},{3,15},{4,8},{5,9},{6,10},{7,11},{8,4},{9,5},... | collective-permute-start | bytes 786440 | tf_op jit(solution)/shard_map/in2_z3/ppermute | solution.py:314
  59.6 30.5 %collective-permute-start.13 = (bf16[4,2,32,512]{3,2,1,0:T(8,128)(2,1)S(1)}, bf16[4,2,32,512]{3,2,1,0:T(8,128)(2,1)S(1)}, u32[]{:S(2)}, u32[]{:S(2)}) collective-permute-start(bf16[4,2,32,512]{3,2,1,0:T(8,128)(2,1)S(1)} %get-tuple-element.57), channel_id=1, source_target_pairs={{0,4},{1,5},{2,6},{3,7},{4,0},{5,1},{6,2},{7,3},{8,12},{9,13},{10,... | collective-permute-start | bytes 786440 | tf_op jit(solution)/shard_map/in2_z1/ppermute | solution.py:314
  59.6 21.8 %collective-permute-start.9 = (bf16[4,2,32,512]{3,2,1,0:T(8,128)(2,1)S(1)}, bf16[4,2,32,512]{3,2,1,0:T(8,128)(2,1)S(1)}, u32[]{:S(2)}, u32[]{:S(2)}) collective-permute-start(bf16[4,2,32,512]{3,2,1,0:T(8,128)(2,1)S(1)} %get-tuple-element.49.refs_2_), channel_id=1, source_target_pairs={{0,8},{1,9},{2,10},{3,11},{4,12},{5,13},{6,14},{7,15},{8,0},{9,1},... | collective-permute-start | bytes 786440 | tf_op jit(solution)/shard_map/in2_z2/ppermute | solution.py:314
  64.0 4.2 %collective-permute-start.6 = (bf16[2,4,4,2,32,512]{5,4,3,2,1,0:T(8,128)(2,1)S(1)}, bf16[2,4,4,2,32,512]{5,4,3,2,1,0:T(8,128)(2,1)S(1)}, u32[]{:S(2)}, u32[]{:S(2)}) collective-permute-start(bf16[2,4,4,2,32,512]{5,4,3,2,1,0:T(8,128)(2,1)S(1)} %join.9.refs_4_), channel_id=1, source_target_pairs={{0,1},{1,0},{2,3},{3,2},{4,5},{5,4},{6,7},{7,6},{8,9},{9,8},{10,11... | collective-permute-start | bytes 6291464 | tf_op jit(solution)/shard_map/in0_core/ppermute | solution.py:314
  64.2 25.6 %collective-permute-start.14 = (bf16[4,4,2,32,512]{4,3,2,1,0:T(8,128)(2,1)S(1)}, bf16[4,4,2,32,512]{4,3,2,1,0:T(8,128)(2,1)S(1)}, u32[]{:S(2)}, u32[]{:S(2)}) collective-permute-start(bf16[4,4,2,32,512]{4,3,2,1,0:T(8,128)(2,1)S(1)} %join.10.refs_0_), channel_id=1, source_target_pairs={{0,2},{1,3},{2,0},{3,1},{4,6},{5,7},{6,4},{7,5},{8,10},{9,11},{10,... | collective-permute-start | bytes 3145736 | tf_op jit(solution)/shard_map/in1_y/ppermute | solution.py:314
  66.1 25.6 %collective-permute-start.12 = (bf16[4,2,32,512]{3,2,1,0:T(8,128)(2,1)S(1)}, bf16[4,2,32,512]{3,2,1,0:T(8,128)(2,1)S(1)}, u32[]{:S(2)}, u32[]{:S(2)}) collective-permute-start(bf16[4,2,32,512]{3,2,1,0:T(8,128)(2,1)S(1)} %relayout.14.refs_3_), channel_id=1, source_target_pairs={{0,12},{1,13},{2,14},{3,15},{4,8},{5,9},{6,10},{7,11},{8,4},{9,5},... | collective-permute-start | bytes 786440 | tf_op jit(solution)/shard_map/in3_z3/ppermute | solution.py:314
  82.0 33.9 %collective-permute-start.10 = (bf16[4,2,32,512]{3,2,1,0:T(8,128)(2,1)S(1)}, bf16[4,2,32,512]{3,2,1,0:T(8,128)(2,1)S(1)}, u32[]{:S(2)}, u32[]{:S(2)}) collective-permute-start(bf16[4,2,32,512]{3,2,1,0:T(8,128)(2,1)S(1)} %get-tuple-element.54), channel_id=1, source_target_pairs={{0,4},{1,5},{2,6},{3,7},{4,0},{5,1},{6,2},{7,3},{8,12},{9,13},{10,... | collective-permute-start | bytes 786440 | tf_op jit(solution)/shard_map/in3_z1/ppermute | solution.py:314
  82.1 21.8 %collective-permute-start.11 = (bf16[4,2,32,512]{3,2,1,0:T(8,128)(2,1)S(1)}, bf16[4,2,32,512]{3,2,1,0:T(8,128)(2,1)S(1)}, u32[]{:S(2)}, u32[]{:S(2)}) collective-permute-start(bf16[4,2,32,512]{3,2,1,0:T(8,128)(2,1)S(1)} %get-tuple-element.55.refs_2_), channel_id=1, source_target_pairs={{0,8},{1,9},{2,10},{3,11},{4,12},{5,13},{6,14},{7,15},{8,0},{9,1},... | collective-permute-start | bytes 786440 | tf_op jit(solution)/shard_map/in3_z2/ppermute | solution.py:314
  89.9 4.2 %collective-permute-start.16 = (bf16[2,4,4,2,32,512]{5,4,3,2,1,0:T(8,128)(2,1)S(1)}, bf16[2,4,4,2,32,512]{5,4,3,2,1,0:T(8,128)(2,1)S(1)}, u32[]{:S(2)}, u32[]{:S(2)}) collective-permute-start(bf16[2,4,4,2,32,512]{5,4,3,2,1,0:T(8,128)(2,1)S(1)} %join.11.refs_4_), channel_id=1, source_target_pairs={{0,1},{1,0},{2,3},{3,2},{4,5},{5,4},{6,7},{7,6},{8,9},{9,8},{10,11... | collective-permute-start | bytes 6291464 | tf_op jit(solution)/shard_map/in1_core/ppermute | solution.py:314
  90.1 25.6 %collective-permute-start.15 = (bf16[4,4,2,32,512]{4,3,2,1,0:T(8,128)(2,1)S(1)}, bf16[4,4,2,32,512]{4,3,2,1,0:T(8,128)(2,1)S(1)}, u32[]{:S(2)}, u32[]{:S(2)}) collective-permute-start(bf16[4,4,2,32,512]{4,3,2,1,0:T(8,128)(2,1)S(1)} %join.12.refs_1_.refs_0_), channel_id=1, source_target_pairs={{0,2},{1,3},{2,0},{3,1},{4,6},{5,7},{6,4},{7,5},{8,10},{9,11},{10,... | collective-permute-start | bytes 3145736 | tf_op jit(solution)/shard_map/in2_y/ppermute | solution.py:314
  91.7 15.6 %collective-permute-start.17 = (bf16[4,2,32,512]{3,2,1,0:T(8,128)(2,1)S(1)}, bf16[4,2,32,512]{3,2,1,0:T(8,128)(2,1)S(1)}, u32[]{:S(2)}, u32[]{:S(2)}) collective-permute-start(bf16[4,2,32,512]{3,2,1,0:T(8,128)(2,1)S(1)} %release.8.refs_3_), channel_id=1, source_target_pairs={{0,12},{1,13},{2,14},{3,15},{4,8},{5,9},{6,10},{7,11},{8,4},{9,5},... | collective-permute-start | bytes 786440 | tf_op jit(solution)/shard_map/out0_z3/ppermute | solution.py:314
  104.0 29.9 %collective-permute-start.21 = (bf16[4,2,32,512]{3,2,1,0:T(8,128)(2,1)S(1)}, bf16[4,2,32,512]{3,2,1,0:T(8,128)(2,1)S(1)}, u32[]{:S(2)}, u32[]{:S(2)}) collective-permute-start(bf16[4,2,32,512]{3,2,1,0:T(8,128)(2,1)S(1)} %get-tuple-element.69), channel_id=1, source_target_pairs={{0,4},{1,5},{2,6},{3,7},{4,0},{5,1},{6,2},{7,3},{8,12},{9,13},{10,... | collective-permute-start | bytes 786440 | tf_op jit(solution)/shard_map/out0_z1/ppermute | solution.py:314
  104.1 22.3 %collective-permute-start.20 = (bf16[4,2,32,512]{3,2,1,0:T(8,128)(2,1)S(1)}, bf16[4,2,32,512]{3,2,1,0:T(8,128)(2,1)S(1)}, u32[]{:S(2)}, u32[]{:S(2)}) collective-permute-start(bf16[4,2,32,512]{3,2,1,0:T(8,128)(2,1)S(1)} %get-tuple-element.63.refs_1_), channel_id=1, source_target_pairs={{0,8},{1,9},{2,10},{3,11},{4,12},{5,13},{6,14},{7,15},{8,0},{9,1},... | collective-permute-start | bytes 786440 | tf_op jit(solution)/shard_map/out0_z2/ppermute | solution.py:314
  107.3 27.5 %collective-permute-start.22 = (bf16[4,2,32,512]{3,2,1,0:T(8,128)(2,1)S(1)}, bf16[4,2,32,512]{3,2,1,0:T(8,128)(2,1)S(1)}, u32[]{:S(2)}, u32[]{:S(2)}) collective-permute-start(bf16[4,2,32,512]{3,2,1,0:T(8,128)(2,1)S(1)} %release.10.refs_2_), channel_id=1, source_target_pairs={{0,12},{1,13},{2,14},{3,15},{4,8},{5,9},{6,10},{7,11},{8,4},{9,5},... | collective-permute-start | bytes 786440 | tf_op jit(solution)/shard_map/out1_z3/ppermute | solution.py:314
  115.9 10.7 %collective-permute-start.19 = (bf16[2,4,4,2,32,512]{5,4,3,2,1,0:T(8,128)(2,1)S(1)}, bf16[2,4,4,2,32,512]{5,4,3,2,1,0:T(8,128)(2,1)S(1)}, u32[]{:S(2)}, u32[]{:S(2)}) collective-permute-start(bf16[2,4,4,2,32,512]{5,4,3,2,1,0:T(8,128)(2,1)S(1)} %join.13.refs_4_), channel_id=1, source_target_pairs={{0,1},{1,0},{2,3},{3,2},{4,5},{5,4},{6,7},{7,6},{8,9},{9,8},{10,11... | collective-permute-start | bytes 6291464 | tf_op jit(solution)/shard_map/in2_core/ppermute | solution.py:314
  116.0 25.6 %collective-permute-start.18 = (bf16[4,4,2,32,512]{4,3,2,1,0:T(8,128)(2,1)S(1)}, bf16[4,4,2,32,512]{4,3,2,1,0:T(8,128)(2,1)S(1)}, u32[]{:S(2)}, u32[]{:S(2)}) collective-permute-start(bf16[4,4,2,32,512]{4,3,2,1,0:T(8,128)(2,1)S(1)} %join.14.refs_3_.refs_0_), channel_id=1, source_target_pairs={{0,2},{1,3},{2,0},{3,1},{4,6},{5,7},{6,4},{7,5},{8,10},{9,11},{10,... | collective-permute-start | bytes 3145736 | tf_op jit(solution)/shard_map/in3_y/ppermute | solution.py:314
  126.5 31.2 %collective-permute-start.25 = (bf16[4,2,32,512]{3,2,1,0:T(8,128)(2,1)S(1)}, bf16[4,2,32,512]{3,2,1,0:T(8,128)(2,1)S(1)}, u32[]{:S(2)}, u32[]{:S(2)}) collective-permute-start(bf16[4,2,32,512]{3,2,1,0:T(8,128)(2,1)S(1)} %get-tuple-element.79), channel_id=1, source_target_pairs={{0,4},{1,5},{2,6},{3,7},{4,0},{5,1},{6,2},{7,3},{8,12},{9,13},{10,... | collective-permute-start | bytes 786440 | tf_op jit(solution)/shard_map/out1_z1/ppermute | solution.py:314
  126.6 22.3 %collective-permute-start.24 = (bf16[4,2,32,512]{3,2,1,0:T(8,128)(2,1)S(1)}, bf16[4,2,32,512]{3,2,1,0:T(8,128)(2,1)S(1)}, u32[]{:S(2)}, u32[]{:S(2)}) collective-permute-start(bf16[4,2,32,512]{3,2,1,0:T(8,128)(2,1)S(1)} %get-tuple-element.66.refs_3_), channel_id=1, source_target_pairs={{0,8},{1,9},{2,10},{3,11},{4,12},{5,13},{6,14},{7,15},{8,0},{9,1},... | collective-permute-start | bytes 786440 | tf_op jit(solution)/shard_map/out1_z2/ppermute | solution.py:314
  134.9 23.7 %collective-permute-start.26 = (bf16[4,2,32,512]{3,2,1,0:T(8,128)(2,1)S(1)}, bf16[4,2,32,512]{3,2,1,0:T(8,128)(2,1)S(1)}, u32[]{:S(2)}, u32[]{:S(2)}) collective-permute-start(bf16[4,2,32,512]{3,2,1,0:T(8,128)(2,1)S(1)} %release.12.refs_2_), channel_id=1, source_target_pairs={{0,12},{1,13},{2,14},{3,15},{4,8},{5,9},{6,10},{7,11},{8,4},{9,5},... | collective-permute-start | bytes 786440 | tf_op jit(solution)/shard_map/out2_z3/ppermute | solution.py:314
  141.8 11.7 %collective-permute-start.23 = (bf16[2,4,4,2,32,512]{5,4,3,2,1,0:T(8,128)(2,1)S(1)}, bf16[2,4,4,2,32,512]{5,4,3,2,1,0:T(8,128)(2,1)S(1)}, u32[]{:S(2)}, u32[]{:S(2)}) collective-permute-start(bf16[2,4,4,2,32,512]{5,4,3,2,1,0:T(8,128)(2,1)S(1)} %join.15.refs_3_), channel_id=1, source_target_pairs={{0,1},{1,0},{2,3},{3,2},{4,5},{5,4},{6,7},{7,6},{8,9},{9,8},{10,11... | collective-permute-start | bytes 6291464 | tf_op jit(solution)/shard_map/in3_core/ppermute | solution.py:314
  148.9 25.8 %collective-permute-start.30 = (bf16[4,2,32,512]{3,2,1,0:T(8,128)(2,1)S(1)}, bf16[4,2,32,512]{3,2,1,0:T(8,128)(2,1)S(1)}, u32[]{:S(2)}, u32[]{:S(2)}) collective-permute-start(bf16[4,2,32,512]{3,2,1,0:T(8,128)(2,1)S(1)} %get-tuple-element.83), channel_id=1, source_target_pairs={{0,4},{1,5},{2,6},{3,7},{4,0},{5,1},{6,2},{7,3},{8,12},{9,13},{10,... | collective-permute-start | bytes 786440 | tf_op jit(solution)/shard_map/out2_z1/ppermute | solution.py:314
  149.5 21.3 %collective-permute-start.27 = (bf16[4,2,32,512]{3,2,1,0:T(8,128)(2,1)S(1)}, bf16[4,2,32,512]{3,2,1,0:T(8,128)(2,1)S(1)}, u32[]{:S(2)}, u32[]{:S(2)}) collective-permute-start(bf16[4,2,32,512]{3,2,1,0:T(8,128)(2,1)S(1)} %get-tuple-element.73.refs_3_), channel_id=1, source_target_pairs={{0,8},{1,9},{2,10},{3,11},{4,12},{5,13},{6,14},{7,15},{8,0},{9,1},... | collective-permute-start | bytes 786440 | tf_op jit(solution)/shard_map/out2_z2/ppermute | solution.py:314
  158.6 21.8 %collective-permute-start.29 = (bf16[4,2,32,512]{3,2,1,0:T(8,128)(2,1)S(1)}, bf16[4,2,32,512]{3,2,1,0:T(8,128)(2,1)S(1)}, u32[]{:S(2)}, u32[]{:S(2)}) collective-permute-start(bf16[4,2,32,512]{3,2,1,0:T(8,128)(2,1)S(1)} %release.14.refs_3_), channel_id=1, source_target_pairs={{0,12},{1,13},{2,14},{3,15},{4,8},{5,9},{6,10},{7,11},{8,4},{9,5},... | collective-permute-start | bytes 786440 | tf_op jit(solution)/shard_map/out3_z3/ppermute | solution.py:314
  170.9 9.5 %collective-permute-start.28 = (bf16[4,2,32,512]{3,2,1,0:T(8,128)(2,1)S(1)}, bf16[4,2,32,512]{3,2,1,0:T(8,128)(2,1)S(1)}, u32[]{:S(2)}, u32[]{:S(2)}) collective-permute-start(bf16[4,2,32,512]{3,2,1,0:T(8,128)(2,1)S(1)} %get-tuple-element.81), channel_id=1, source_target_pairs={{0,4},{1,5},{2,6},{3,7},{4,0},{5,1},{6,2},{7,3},{8,12},{9,13},{10,... | collective-permute-start | bytes 786440 | tf_op jit(solution)/shard_map/out3_z1/ppermute | solution.py:314
  171.3 15.9 %collective-permute-start.31 = (bf16[4,2,32,512]{3,2,1,0:T(8,128)(2,1)S(1)}, bf16[4,2,32,512]{3,2,1,0:T(8,128)(2,1)S(1)}, u32[]{:S(2)}, u32[]{:S(2)}) collective-permute-start(bf16[4,2,32,512]{3,2,1,0:T(8,128)(2,1)S(1)} %get-tuple-element.84.refs_3_), channel_id=1, source_target_pairs={{0,8},{1,9},{2,10},{3,11},{4,12},{5,13},{6,14},{7,15},{8,0},{9,1},... | collective-permute-start | bytes 786440 | tf_op jit(solution)/shard_map/out3_z2/ppermute | solution.py:314
  (7 other events, 29.5 us)

commit v4 on v3

--- a/solution.py
+++ b/solution.py
@@ -439,8 +439,7 @@
 
     def shards(spectra, fold_counts, inverse_wavelet):
         shots, _, bins, _ = spectra.shape
-        power = n & (n - 1) == 0
-        if power and n % 16 == 0 and bins % n == 0 and shots % 16 == 0:
+        if n == 4 * PLANE and bins % n == 0 and bins // n >= 4 and shots % 16 == 0:
             return chunked_shards(n, spectra, fold_counts, inverse_wavelet)
         return plain_shards(spectra, fold_counts, inverse_wavelet)
 

time: 189 us -> 189 us (level)
  no operation moved by 1% of the time
where the time goes in v4:
time: 189 us
  waiting for transfers between devices  105 us (56%)
  starting transfers between devices  47.9 us (25%)
  Pallas kernels  30.1 us (16%)
  local copies, waits for them, and re-layouts  5.33 us (3%)
    ppermute x32, waiting for transfers between devices, send(): return lax.ppermute(block, 'shot', [(d, d ^ offset) for d in range(n)])  105 us
    ppermute x32, starting transfers between devices, send(): return lax.ppermute(block, 'shot', [(d, d ^ offset) for d in range(n)])  47.9 us
    pallas_call x4, Pallas kernels, product(): pl.pallas_call(functools.partial(product_kernel, k, n, planes), out_shape...  16.4 us
    unnamed x14, local copies, waits for them, and re-layouts  5.19 us
    pallas_call x4, Pallas kernels, assemble(): pl.pallas_call(functools.partial(assemble_kernel, n, shots, k, list(block...  5.08 us
    pallas_call x4, Pallas kernels, early(): pl.pallas_call(functools.partial(early_kernel, list(blocks)), out_shape=j...  3.84 us
  transfers between devices with their start and end apart: 32, of which 16 were waited for; matrix products, arithmetic and copies ran while one was open for 0% of the time, Pallas kernels for 15%

profile of v4, /device:TPU:0, one launch (start us, length us, event | category | flops | bytes accessed | tf_op | source)
XLA Modules:
  0.0 188.7 jit_solution(15843720251646907205)
XLA Ops:
  0.0 2.2 %copy-done.4 = bf16[32,2,64,512]{3,2,1,0:T(8,128)(2,1)S(1)} copy-done((bf16[32,2,64,512]{3,2,1,0:T(8,128)(2,1)S(1)}, bf16[32,2,64,512]{3,2,1,0:T(8,128)(2,1)}, u32[]{:S(2)}) %copy-start.4) | copy-done | bytes 4194328
  2.5 5.1 %collective-permute-start = (bf16[4,2,32,512]{3,2,1,0:T(8,128)(2,1)S(1)}, bf16[4,2,32,512]{3,2,1,0:T(8,128)(2,1)S(1)}, u32[]{:S(2)}, u32[]{:S(2)}) collective-permute-start(bf16[4,2,32,512]{3,2,1,0:T(8,128)(2,1)S(1)} %relayout.8.refs_0_), channel_id=1, source_target_pairs={{0,12},{1,13},{2,14},{3,15},{4,8},{5,9},{6,10},{7,11},{8,4},{9,5},... | collective-permute-start | bytes 786440 | tf_op jit(solution)/shard_map/in0_z3/ppermute | solution.py:314
  9.0 5.8 %collective-permute-done.refs_1_.refs_3_ = bf16[4,2,32,512]{3,2,1,0:T(8,128)(2,1)S(1)} collective-permute-done((bf16[4,2,32,512]{3,2,1,0:T(8,128)(2,1)S(1)}, bf16[4,2,32,512]{3,2,1,0:T(8,128)(2,1)S(1)}, u32[]{:S(2)}, u32[]{:S(2)}) %collective-permute-start) | collective-permute-done | bytes 262176 | tf_op jit(solution)/shard_map/in0_z3/ppermute | solution.py:314
  14.8 2.2 %copy-done.5 = bf16[32,2,64,512]{3,2,1,0:T(8,128)(2,1)S(1)} copy-done((bf16[32,2,64,512]{3,2,1,0:T(8,128)(2,1)S(1)}, bf16[32,2,64,512]{3,2,1,0:T(8,128)(2,1)}, u32[]{:S(2)}) %copy-start.5) | copy-done | bytes 4194328
  17.3 3.8 %collective-permute-start.4 = (bf16[4,2,32,512]{3,2,1,0:T(8,128)(2,1)S(1)}, bf16[4,2,32,512]{3,2,1,0:T(8,128)(2,1)S(1)}, u32[]{:S(2)}, u32[]{:S(2)}) collective-permute-start(bf16[4,2,32,512]{3,2,1,0:T(8,128)(2,1)S(1)} %relayout.10.refs_0_), channel_id=1, source_target_pairs={{0,12},{1,13},{2,14},{3,15},{4,8},{5,9},{6,10},{7,11},{8,4},{9,5},... | collective-permute-start | bytes 786440 | tf_op jit(solution)/shard_map/in1_z3/ppermute | solution.py:314
  21.2 15.3 %collective-permute-done.1.refs_1_.refs_2_ = bf16[4,2,32,512]{3,2,1,0:T(8,128)(2,1)S(1)} collective-permute-done((bf16[4,2,32,512]{3,2,1,0:T(8,128)(2,1)S(1)}, bf16[4,2,32,512]{3,2,1,0:T(8,128)(2,1)S(1)}, u32[]{:S(2)}, u32[]{:S(2)}) %collective-permute-start.1) | collective-permute-done | bytes 262176 | tf_op jit(solution)/shard_map/in0_z2/ppermute | solution.py:314
  37.4 3.3 %collective-permute-start.7 = (bf16[4,2,32,512]{3,2,1,0:T(8,128)(2,1)S(1)}, bf16[4,2,32,512]{3,2,1,0:T(8,128)(2,1)S(1)}, u32[]{:S(2)}, u32[]{:S(2)}) collective-permute-start(bf16[4,2,32,512]{3,2,1,0:T(8,128)(2,1)S(1)} %get-tuple-element.51), channel_id=1, source_target_pairs={{0,4},{1,5},{2,6},{3,7},{4,0},{5,1},{6,2},{7,3},{8,12},{9,13},{10,... | collective-permute-start | bytes 786440 | tf_op jit(solution)/shard_map/in1_z1/ppermute | solution.py:314
  44.6 14.4 %collective-permute-done.5.refs_1_.refs_2_ = bf16[4,2,32,512]{3,2,1,0:T(8,128)(2,1)S(1)} collective-permute-done((bf16[4,2,32,512]{3,2,1,0:T(8,128)(2,1)S(1)}, bf16[4,2,32,512]{3,2,1,0:T(8,128)(2,1)S(1)}, u32[]{:S(2)}, u32[]{:S(2)}) %collective-permute-start.5) | collective-permute-done | bytes 262176 | tf_op jit(solution)/shard_map/in1_z2/ppermute | solution.py:314
  59.6 3.2 %collective-permute-start.9 = (bf16[4,2,32,512]{3,2,1,0:T(8,128)(2,1)S(1)}, bf16[4,2,32,512]{3,2,1,0:T(8,128)(2,1)S(1)}, u32[]{:S(2)}, u32[]{:S(2)}) collective-permute-start(bf16[4,2,32,512]{3,2,1,0:T(8,128)(2,1)S(1)} %get-tuple-element.49.refs_2_), channel_id=1, source_target_pairs={{0,8},{1,9},{2,10},{3,11},{4,12},{5,13},{6,14},{7,15},{8,0},{9,1},... | collective-permute-start | bytes 786440 | tf_op jit(solution)/shard_map/in2_z2/ppermute | solution.py:314
  64.2 1.6 collective-permute-start.14
  66.1 1.6 collective-permute-start.12
  68.2 4.1 %product.4 = (bf16[4,2,32,512]{3,2,1,0:T(8,128)(2,1)S(1)}, bf16[4,2,32,512]{3,2,1,0:T(8,128)(2,1)S(1)}, bf16[4,2,32,512]{3,2,1,0:T(8,128)(2,1)S(1)}, bf16[4,2,32,512]{3,2,1,0:T(8,128)(2,1)S(1)}) custom-call(s32[1]{0:T(128)} %bitcast.me_ref, f32[2,64]{1,0:T(2,128)S(1)} %copy-done.3, s32[1,512]{1,0:T(1,128)S(1)} %bitcast.4, s32[512,1]{1,0:T(8,128)S(1)} %copy.10.fold_col_ref, ...), custom_call_target="tpu_custom_call" | custom-call | tf_op jit(solution)/shard_map/chunk0/product/pallas_call | solution.py:300
  72.3 9.1 %collective-permute-done.9.refs_1_.refs_2_ = bf16[4,2,32,512]{3,2,1,0:T(8,128)(2,1)S(1)} collective-permute-done((bf16[4,2,32,512]{3,2,1,0:T(8,128)(2,1)S(1)}, bf16[4,2,32,512]{3,2,1,0:T(8,128)(2,1)S(1)}, u32[]{:S(2)}, u32[]{:S(2)}) %collective-permute-start.9) | collective-permute-done | bytes 262176 | tf_op jit(solution)/shard_map/in2_z2/ppermute | solution.py:314
  82.1 3.2 %collective-permute-start.11 = (bf16[4,2,32,512]{3,2,1,0:T(8,128)(2,1)S(1)}, bf16[4,2,32,512]{3,2,1,0:T(8,128)(2,1)S(1)}, u32[]{:S(2)}, u32[]{:S(2)}) collective-permute-start(bf16[4,2,32,512]{3,2,1,0:T(8,128)(2,1)S(1)} %get-tuple-element.55.refs_2_), channel_id=1, source_target_pairs={{0,8},{1,9},{2,10},{3,11},{4,12},{5,13},{6,14},{7,15},{8,0},{9,1},... | collective-permute-start | bytes 786440 | tf_op jit(solution)/shard_map/in3_z2/ppermute | solution.py:314
  85.3 4.5 %collective-permute-done.14.refs_1_ = bf16[4,4,2,32,512]{4,3,2,1,0:T(8,128)(2,1)S(1)} collective-permute-done((bf16[4,4,2,32,512]{4,3,2,1,0:T(8,128)(2,1)S(1)}, bf16[4,4,2,32,512]{4,3,2,1,0:T(8,128)(2,1)S(1)}, u32[]{:S(2)}, u32[]{:S(2)}) %collective-permute-start.14) | collective-permute-done | bytes 1048608 | tf_op jit(solution)/shard_map/in1_y/ppermute | solution.py:314
  90.1 1.6 collective-permute-start.15
  91.7 1.6 collective-permute-start.17
  94.2 4.1 %product.5 = (bf16[4,2,32,512]{3,2,1,0:T(8,128)(2,1)S(1)}, bf16[4,2,32,512]{3,2,1,0:T(8,128)(2,1)S(1)}, bf16[4,2,32,512]{3,2,1,0:T(8,128)(2,1)S(1)}, bf16[4,2,32,512]{3,2,1,0:T(8,128)(2,1)S(1)}) custom-call(s32[1]{0:T(128)} %bitcast.me_ref, f32[2,64]{1,0:T(2,128)S(1)} %copy-done.3, s32[1,512]{1,0:T(1,128)S(1)} %bitcast.5, s32[512,1]{1,0:T(8,128)S(1)} %copy.10.fold_col_ref, ...), custom_call_target="tpu_custom_call" | custom-call | tf_op jit(solution)/shard_map/chunk1/product/pallas_call | solution.py:300
  98.3 5.7 %collective-permute-done.11.refs_4_.refs_2_ = bf16[4,2,32,512]{3,2,1,0:T(8,128)(2,1)S(1)} collective-permute-done((bf16[4,2,32,512]{3,2,1,0:T(8,128)(2,1)S(1)}, bf16[4,2,32,512]{3,2,1,0:T(8,128)(2,1)S(1)}, u32[]{:S(2)}, u32[]{:S(2)}) %collective-permute-start.11) | collective-permute-done | bytes 262176 | tf_op jit(solution)/shard_map/in3_z2/ppermute | solution.py:314
  104.1 3.2 %collective-permute-start.20 = (bf16[4,2,32,512]{3,2,1,0:T(8,128)(2,1)S(1)}, bf16[4,2,32,512]{3,2,1,0:T(8,128)(2,1)S(1)}, u32[]{:S(2)}, u32[]{:S(2)}) collective-permute-start(bf16[4,2,32,512]{3,2,1,0:T(8,128)(2,1)S(1)} %get-tuple-element.63.refs_1_), channel_id=1, source_target_pairs={{0,8},{1,9},{2,10},{3,11},{4,12},{5,13},{6,14},{7,15},{8,0},{9,1},... | collective-permute-start | bytes 786440 | tf_op jit(solution)/shard_map/out0_z2/ppermute | solution.py:314
  108.5 7.2 %collective-permute-done.15.refs_1_ = bf16[4,4,2,32,512]{4,3,2,1,0:T(8,128)(2,1)S(1)} collective-permute-done((bf16[4,4,2,32,512]{4,3,2,1,0:T(8,128)(2,1)S(1)}, bf16[4,4,2,32,512]{4,3,2,1,0:T(8,128)(2,1)S(1)}, u32[]{:S(2)}, u32[]{:S(2)}) %collective-permute-start.15) | collective-permute-done | bytes 1048608 | tf_op jit(solution)/shard_map/in2_y/ppermute | solution.py:314
  117.6 8.8 %collective-permute-done.20.refs_4_.refs_0_ = bf16[4,2,32,512]{3,2,1,0:T(8,128)(2,1)S(1)} collective-permute-done((bf16[4,2,32,512]{3,2,1,0:T(8,128)(2,1)S(1)}, bf16[4,2,32,512]{3,2,1,0:T(8,128)(2,1)S(1)}, u32[]{:S(2)}, u32[]{:S(2)}) %collective-permute-start.20) | collective-permute-done | bytes 262176 | tf_op jit(solution)/shard_map/out0_z2/ppermute | solution.py:314
  126.6 3.2 %collective-permute-start.24 = (bf16[4,2,32,512]{3,2,1,0:T(8,128)(2,1)S(1)}, bf16[4,2,32,512]{3,2,1,0:T(8,128)(2,1)S(1)}, u32[]{:S(2)}, u32[]{:S(2)}) collective-permute-start(bf16[4,2,32,512]{3,2,1,0:T(8,128)(2,1)S(1)} %get-tuple-element.66.refs_3_), channel_id=1, source_target_pairs={{0,8},{1,9},{2,10},{3,11},{4,12},{5,13},{6,14},{7,15},{8,0},{9,1},... | collective-permute-start | bytes 786440 | tf_op jit(solution)/shard_map/out1_z2/ppermute | solution.py:314
  129.7 4.1 %product.6 = (bf16[4,2,32,512]{3,2,1,0:T(8,128)(2,1)S(1)}, bf16[4,2,32,512]{3,2,1,0:T(8,128)(2,1)S(1)}, bf16[4,2,32,512]{3,2,1,0:T(8,128)(2,1)S(1)}, bf16[4,2,32,512]{3,2,1,0:T(8,128)(2,1)S(1)}) custom-call(s32[1]{0:T(128)} %bitcast.me_ref, f32[2,64]{1,0:T(2,128)S(1)} %copy-done.3, s32[1,512]{1,0:T(1,128)S(1)} %bitcast.6, s32[512,1]{1,0:T(8,128)S(1)} %copy.10.fold_col_ref, ...), custom_call_target="tpu_custom_call" | custom-call | tf_op jit(solution)/shard_map/chunk2/product/pallas_call | solution.py:300
  136.1 5.5 %collective-permute-done.18.refs_1_ = bf16[4,4,2,32,512]{4,3,2,1,0:T(8,128)(2,1)S(1)} collective-permute-done((bf16[4,4,2,32,512]{4,3,2,1,0:T(8,128)(2,1)S(1)}, bf16[4,4,2,32,512]{4,3,2,1,0:T(8,128)(2,1)S(1)}, u32[]{:S(2)}, u32[]{:S(2)}) %collective-permute-start.18) | collective-permute-done | bytes 1048608 | tf_op jit(solution)/shard_map/in3_y/ppermute | solution.py:314
  141.9 7.0 %collective-permute-done.24.refs_4_.refs_0_ = bf16[4,2,32,512]{3,2,1,0:T(8,128)(2,1)S(1)} collective-permute-done((bf16[4,2,32,512]{3,2,1,0:T(8,128)(2,1)S(1)}, bf16[4,2,32,512]{3,2,1,0:T(8,128)(2,1)S(1)}, u32[]{:S(2)}, u32[]{:S(2)}) %collective-permute-start.24) | collective-permute-done | bytes 262176 | tf_op jit(solution)/shard_map/out1_z2/ppermute | solution.py:314
  149.5 2.7 %collective-permute-start.27 = (bf16[4,2,32,512]{3,2,1,0:T(8,128)(2,1)S(1)}, bf16[4,2,32,512]{3,2,1,0:T(8,128)(2,1)S(1)}, u32[]{:S(2)}, u32[]{:S(2)}) collective-permute-start(bf16[4,2,32,512]{3,2,1,0:T(8,128)(2,1)S(1)} %get-tuple-element.73.refs_3_), channel_id=1, source_target_pairs={{0,8},{1,9},{2,10},{3,11},{4,12},{5,13},{6,14},{7,15},{8,0},{9,1},... | collective-permute-start | bytes 786440 | tf_op jit(solution)/shard_map/out2_z2/ppermute | solution.py:314
  153.5 4.1 %product.7 = (bf16[4,2,32,512]{3,2,1,0:T(8,128)(2,1)S(1)}, bf16[4,2,32,512]{3,2,1,0:T(8,128)(2,1)S(1)}, bf16[4,2,32,512]{3,2,1,0:T(8,128)(2,1)S(1)}, bf16[4,2,32,512]{3,2,1,0:T(8,128)(2,1)S(1)}) custom-call(s32[1]{0:T(128)} %bitcast.me_ref, f32[2,64]{1,0:T(2,128)S(1)} %copy-done.3, s32[1,512]{1,0:T(1,128)S(1)} %bitcast.7, s32[512,1]{1,0:T(8,128)S(1)} %copy.10.fold_col_ref, ...), custom_call_target="tpu_custom_call" | custom-call | tf_op jit(solution)/shard_map/chunk3/product/pallas_call | solution.py:300
  159.8 10.9 %collective-permute-done.27.refs_4_.refs_0_ = bf16[4,2,32,512]{3,2,1,0:T(8,128)(2,1)S(1)} collective-permute-done((bf16[4,2,32,512]{3,2,1,0:T(8,128)(2,1)S(1)}, bf16[4,2,32,512]{3,2,1,0:T(8,128)(2,1)S(1)}, u32[]{:S(2)}, u32[]{:S(2)}) %collective-permute-start.27) | collective-permute-done | bytes 262176 | tf_op jit(solution)/shard_map/out2_z2/ppermute | solution.py:314
  171.3 3.4 %collective-permute-start.31 = (bf16[4,2,32,512]{3,2,1,0:T(8,128)(2,1)S(1)}, bf16[4,2,32,512]{3,2,1,0:T(8,128)(2,1)S(1)}, u32[]{:S(2)}, u32[]{:S(2)}) collective-permute-start(bf16[4,2,32,512]{3,2,1,0:T(8,128)(2,1)S(1)} %get-tuple-element.84.refs_3_), channel_id=1, source_target_pairs={{0,8},{1,9},{2,10},{3,11},{4,12},{5,13},{6,14},{7,15},{8,0},{9,1},... | collective-permute-start | bytes 786440 | tf_op jit(solution)/shard_map/out3_z2/ppermute | solution.py:314
  178.3 2.1 %collective-permute-done.28.refs_1_ = bf16[4,2,32,512]{3,2,1,0:T(8,128)(2,1)S(1)} collective-permute-done((bf16[4,2,32,512]{3,2,1,0:T(8,128)(2,1)S(1)}, bf16[4,2,32,512]{3,2,1,0:T(8,128)(2,1)S(1)}, u32[]{:S(2)}, u32[]{:S(2)}) %collective-permute-start.28) | collective-permute-done | bytes 262176 | tf_op jit(solution)/shard_map/out3_z1/ppermute | solution.py:314
  181.4 5.9 %collective-permute-done.31.refs_0_ = bf16[4,2,32,512]{3,2,1,0:T(8,128)(2,1)S(1)} collective-permute-done((bf16[4,2,32,512]{3,2,1,0:T(8,128)(2,1)S(1)}, bf16[4,2,32,512]{3,2,1,0:T(8,128)(2,1)S(1)}, u32[]{:S(2)}, u32[]{:S(2)}) %collective-permute-start.31) | collective-permute-done | bytes 262176 | tf_op jit(solution)/shard_map/out3_z2/ppermute | solution.py:314
  (84 shorter events, 27.4 us)
Async XLA Ops:
  2.5 12.3 %collective-permute-start = (bf16[4,2,32,512]{3,2,1,0:T(8,128)(2,1)S(1)}, bf16[4,2,32,512]{3,2,1,0:T(8,128)(2,1)S(1)}, u32[]{:S(2)}, u32[]{:S(2)}) collective-permute-start(bf16[4,2,32,512]{3,2,1,0:T(8,128)(2,1)S(1)} %relayout.8.refs_0_), channel_id=1, source_target_pairs={{0,12},{1,13},{2,14},{3,15},{4,8},{5,9},{6,10},{7,11},{8,4},{9,5},... | collective-permute-start | bytes 786440 | tf_op jit(solution)/shard_map/in0_z3/ppermute | solution.py:314
  8.2 32.5 %collective-permute-start.2 = (bf16[4,2,32,512]{3,2,1,0:T(8,128)(2,1)S(1)}, bf16[4,2,32,512]{3,2,1,0:T(8,128)(2,1)S(1)}, u32[]{:S(2)}, u32[]{:S(2)}) collective-permute-start(bf16[4,2,32,512]{3,2,1,0:T(8,128)(2,1)S(1)} %get-tuple-element.48), channel_id=1, source_target_pairs={{0,4},{1,5},{2,6},{3,7},{4,0},{5,1},{6,2},{7,3},{8,12},{9,13},{10,... | collective-permute-start | bytes 786440 | tf_op jit(solution)/shard_map/in0_z1/ppermute | solution.py:314
  8.3 28.2 %collective-permute-start.1 = (bf16[4,2,32,512]{3,2,1,0:T(8,128)(2,1)S(1)}, bf16[4,2,32,512]{3,2,1,0:T(8,128)(2,1)S(1)}, u32[]{:S(2)}, u32[]{:S(2)}) collective-permute-start(bf16[4,2,32,512]{3,2,1,0:T(8,128)(2,1)S(1)} %get-tuple-element.45.refs_0_), channel_id=1, source_target_pairs={{0,8},{1,9},{2,10},{3,11},{4,12},{5,13},{6,14},{7,15},{8,0},{9,1},... | collective-permute-start | bytes 786440 | tf_op jit(solution)/shard_map/in0_z2/ppermute | solution.py:314
  17.3 25.7 %collective-permute-start.4 = (bf16[4,2,32,512]{3,2,1,0:T(8,128)(2,1)S(1)}, bf16[4,2,32,512]{3,2,1,0:T(8,128)(2,1)S(1)}, u32[]{:S(2)}, u32[]{:S(2)}) collective-permute-start(bf16[4,2,32,512]{3,2,1,0:T(8,128)(2,1)S(1)} %relayout.10.refs_0_), channel_id=1, source_target_pairs={{0,12},{1,13},{2,14},{3,15},{4,8},{5,9},{6,10},{7,11},{8,4},{9,5},... | collective-permute-start | bytes 786440 | tf_op jit(solution)/shard_map/in1_z3/ppermute | solution.py:314
  37.1 21.9 %collective-permute-start.5 = (bf16[4,2,32,512]{3,2,1,0:T(8,128)(2,1)S(1)}, bf16[4,2,32,512]{3,2,1,0:T(8,128)(2,1)S(1)}, u32[]{:S(2)}, u32[]{:S(2)}) collective-permute-start(bf16[4,2,32,512]{3,2,1,0:T(8,128)(2,1)S(1)} %get-tuple-element.46.refs_0_), channel_id=1, source_target_pairs={{0,8},{1,9},{2,10},{3,11},{4,12},{5,13},{6,14},{7,15},{8,0},{9,1},... | collective-permute-start | bytes 786440 | tf_op jit(solution)/shard_map/in1_z2/ppermute | solution.py:314
  37.4 26.7 %collective-permute-start.7 = (bf16[4,2,32,512]{3,2,1,0:T(8,128)(2,1)S(1)}, bf16[4,2,32,512]{3,2,1,0:T(8,128)(2,1)S(1)}, u32[]{:S(2)}, u32[]{:S(2)}) collective-permute-start(bf16[4,2,32,512]{3,2,1,0:T(8,128)(2,1)S(1)} %get-tuple-element.51), channel_id=1, source_target_pairs={{0,4},{1,5},{2,6},{3,7},{4,0},{5,1},{6,2},{7,3},{8,12},{9,13},{10,... | collective-permute-start | bytes 786440 | tf_op jit(solution)/shard_map/in1_z1/ppermute | solution.py:314
  41.5 22.3 %collective-permute-start.3 = (bf16[4,4,2,32,512]{4,3,2,1,0:T(8,128)(2,1)S(1)}, bf16[4,4,2,32,512]{4,3,2,1,0:T(8,128)(2,1)S(1)}, u32[]{:S(2)}, u32[]{:S(2)}) collective-permute-start(bf16[4,4,2,32,512]{4,3,2,1,0:T(8,128)(2,1)S(1)} %join.8.refs_0_), channel_id=1, source_target_pairs={{0,2},{1,3},{2,0},{3,1},{4,6},{5,7},{6,4},{7,5},{8,10},{9,11},{10,... | collective-permute-start | bytes 3145736 | tf_op jit(solution)/shard_map/in0_y/ppermute | solution.py:314
  43.4 22.4 %collective-permute-start.8 = (bf16[4,2,32,512]{3,2,1,0:T(8,128)(2,1)S(1)}, bf16[4,2,32,512]{3,2,1,0:T(8,128)(2,1)S(1)}, u32[]{:S(2)}, u32[]{:S(2)}) collective-permute-start(bf16[4,2,32,512]{3,2,1,0:T(8,128)(2,1)S(1)} %relayout.12.refs_0_), channel_id=1, source_target_pairs={{0,12},{1,13},{2,14},{3,15},{4,8},{5,9},{6,10},{7,11},{8,4},{9,5},... | collective-permute-start | bytes 786440 | tf_op jit(solution)/shard_map/in2_z3/ppermute | solution.py:314
  59.6 30.5 %collective-permute-start.13 = (bf16[4,2,32,512]{3,2,1,0:T(8,128)(2,1)S(1)}, bf16[4,2,32,512]{3,2,1,0:T(8,128)(2,1)S(1)}, u32[]{:S(2)}, u32[]{:S(2)}) collective-permute-start(bf16[4,2,32,512]{3,2,1,0:T(8,128)(2,1)S(1)} %get-tuple-element.57), channel_id=1, source_target_pairs={{0,4},{1,5},{2,6},{3,7},{4,0},{5,1},{6,2},{7,3},{8,12},{9,13},{10,... | collective-permute-start | bytes 786440 | tf_op jit(solution)/shard_map/in2_z1/ppermute | solution.py:314
  59.6 21.8 %collective-permute-start.9 = (bf16[4,2,32,512]{3,2,1,0:T(8,128)(2,1)S(1)}, bf16[4,2,32,512]{3,2,1,0:T(8,128)(2,1)S(1)}, u32[]{:S(2)}, u32[]{:S(2)}) collective-permute-start(bf16[4,2,32,512]{3,2,1,0:T(8,128)(2,1)S(1)} %get-tuple-element.49.refs_2_), channel_id=1, source_target_pairs={{0,8},{1,9},{2,10},{3,11},{4,12},{5,13},{6,14},{7,15},{8,0},{9,1},... | collective-permute-start | bytes 786440 | tf_op jit(solution)/shard_map/in2_z2/ppermute | solution.py:314
  64.0 4.2 %collective-permute-start.6 = (bf16[2,4,4,2,32,512]{5,4,3,2,1,0:T(8,128)(2,1)S(1)}, bf16[2,4,4,2,32,512]{5,4,3,2,1,0:T(8,128)(2,1)S(1)}, u32[]{:S(2)}, u32[]{:S(2)}) collective-permute-start(bf16[2,4,4,2,32,512]{5,4,3,2,1,0:T(8,128)(2,1)S(1)} %join.9.refs_4_), channel_id=1, source_target_pairs={{0,1},{1,0},{2,3},{3,2},{4,5},{5,4},{6,7},{7,6},{8,9},{9,8},{10,11... | collective-permute-start | bytes 6291464 | tf_op jit(solution)/shard_map/in0_core/ppermute | solution.py:314
  64.2 25.6 %collective-permute-start.14 = (bf16[4,4,2,32,512]{4,3,2,1,0:T(8,128)(2,1)S(1)}, bf16[4,4,2,32,512]{4,3,2,1,0:T(8,128)(2,1)S(1)}, u32[]{:S(2)}, u32[]{:S(2)}) collective-permute-start(bf16[4,4,2,32,512]{4,3,2,1,0:T(8,128)(2,1)S(1)} %join.10.refs_0_), channel_id=1, source_target_pairs={{0,2},{1,3},{2,0},{3,1},{4,6},{5,7},{6,4},{7,5},{8,10},{9,11},{10,... | collective-permute-start | bytes 3145736 | tf_op jit(solution)/shard_map/in1_y/ppermute | solution.py:314
  66.1 25.6 %collective-permute-start.12 = (bf16[4,2,32,512]{3,2,1,0:T(8,128)(2,1)S(1)}, bf16[4,2,32,512]{3,2,1,0:T(8,128)(2,1)S(1)}, u32[]{:S(2)}, u32[]{:S(2)}) collective-permute-start(bf16[4,2,32,512]{3,2,1,0:T(8,128)(2,1)S(1)} %relayout.14.refs_3_), channel_id=1, source_target_pairs={{0,12},{1,13},{2,14},{3,15},{4,8},{5,9},{6,10},{7,11},{8,4},{9,5},... | collective-permute-start | bytes 786440 | tf_op jit(solution)/shard_map/in3_z3/ppermute | solution.py:314
  82.0 33.9 %collective-permute-start.10 = (bf16[4,2,32,512]{3,2,1,0:T(8,128)(2,1)S(1)}, bf16[4,2,32,512]{3,2,1,0:T(8,128)(2,1)S(1)}, u32[]{:S(2)}, u32[]{:S(2)}) collective-permute-start(bf16[4,2,32,512]{3,2,1,0:T(8,128)(2,1)S(1)} %get-tuple-element.54), channel_id=1, source_target_pairs={{0,4},{1,5},{2,6},{3,7},{4,0},{5,1},{6,2},{7,3},{8,12},{9,13},{10,... | collective-permute-start | bytes 786440 | tf_op jit(solution)/shard_map/in3_z1/ppermute | solution.py:314
  82.1 21.8 %collective-permute-start.11 = (bf16[4,2,32,512]{3,2,1,0:T(8,128)(2,1)S(1)}, bf16[4,2,32,512]{3,2,1,0:T(8,128)(2,1)S(1)}, u32[]{:S(2)}, u32[]{:S(2)}) collective-permute-start(bf16[4,2,32,512]{3,2,1,0:T(8,128)(2,1)S(1)} %get-tuple-element.55.refs_2_), channel_id=1, source_target_pairs={{0,8},{1,9},{2,10},{3,11},{4,12},{5,13},{6,14},{7,15},{8,0},{9,1},... | collective-permute-start | bytes 786440 | tf_op jit(solution)/shard_map/in3_z2/ppermute | solution.py:314
  89.9 4.2 %collective-permute-start.16 = (bf16[2,4,4,2,32,512]{5,4,3,2,1,0:T(8,128)(2,1)S(1)}, bf16[2,4,4,2,32,512]{5,4,3,2,1,0:T(8,128)(2,1)S(1)}, u32[]{:S(2)}, u32[]{:S(2)}) collective-permute-start(bf16[2,4,4,2,32,512]{5,4,3,2,1,0:T(8,128)(2,1)S(1)} %join.11.refs_4_), channel_id=1, source_target_pairs={{0,1},{1,0},{2,3},{3,2},{4,5},{5,4},{6,7},{7,6},{8,9},{9,8},{10,11... | collective-permute-start | bytes 6291464 | tf_op jit(solution)/shard_map/in1_core/ppermute | solution.py:314
  90.1 25.6 %collective-permute-start.15 = (bf16[4,4,2,32,512]{4,3,2,1,0:T(8,128)(2,1)S(1)}, bf16[4,4,2,32,512]{4,3,2,1,0:T(8,128)(2,1)S(1)}, u32[]{:S(2)}, u32[]{:S(2)}) collective-permute-start(bf16[4,4,2,32,512]{4,3,2,1,0:T(8,128)(2,1)S(1)} %join.12.refs_1_.refs_0_), channel_id=1, source_target_pairs={{0,2},{1,3},{2,0},{3,1},{4,6},{5,7},{6,4},{7,5},{8,10},{9,11},{10,... | collective-permute-start | bytes 3145736 | tf_op jit(solution)/shard_map/in2_y/ppermute | solution.py:314
  91.7 15.6 %collective-permute-start.17 = (bf16[4,2,32,512]{3,2,1,0:T(8,128)(2,1)S(1)}, bf16[4,2,32,512]{3,2,1,0:T(8,128)(2,1)S(1)}, u32[]{:S(2)}, u32[]{:S(2)}) collective-permute-start(bf16[4,2,32,512]{3,2,1,0:T(8,128)(2,1)S(1)} %release.8.refs_3_), channel_id=1, source_target_pairs={{0,12},{1,13},{2,14},{3,15},{4,8},{5,9},{6,10},{7,11},{8,4},{9,5},... | collective-permute-start | bytes 786440 | tf_op jit(solution)/shard_map/out0_z3/ppermute | solution.py:314
  104.0 29.9 %collective-permute-start.21 = (bf16[4,2,32,512]{3,2,1,0:T(8,128)(2,1)S(1)}, bf16[4,2,32,512]{3,2,1,0:T(8,128)(2,1)S(1)}, u32[]{:S(2)}, u32[]{:S(2)}) collective-permute-start(bf16[4,2,32,512]{3,2,1,0:T(8,128)(2,1)S(1)} %get-tuple-element.69), channel_id=1, source_target_pairs={{0,4},{1,5},{2,6},{3,7},{4,0},{5,1},{6,2},{7,3},{8,12},{9,13},{10,... | collective-permute-start | bytes 786440 | tf_op jit(solution)/shard_map/out0_z1/ppermute | solution.py:314
  104.1 22.3 %collective-permute-start.20 = (bf16[4,2,32,512]{3,2,1,0:T(8,128)(2,1)S(1)}, bf16[4,2,32,512]{3,2,1,0:T(8,128)(2,1)S(1)}, u32[]{:S(2)}, u32[]{:S(2)}) collective-permute-start(bf16[4,2,32,512]{3,2,1,0:T(8,128)(2,1)S(1)} %get-tuple-element.63.refs_1_), channel_id=1, source_target_pairs={{0,8},{1,9},{2,10},{3,11},{4,12},{5,13},{6,14},{7,15},{8,0},{9,1},... | collective-permute-start | bytes 786440 | tf_op jit(solution)/shard_map/out0_z2/ppermute | solution.py:314
  107.3 27.5 %collective-permute-start.22 = (bf16[4,2,32,512]{3,2,1,0:T(8,128)(2,1)S(1)}, bf16[4,2,32,512]{3,2,1,0:T(8,128)(2,1)S(1)}, u32[]{:S(2)}, u32[]{:S(2)}) collective-permute-start(bf16[4,2,32,512]{3,2,1,0:T(8,128)(2,1)S(1)} %release.10.refs_2_), channel_id=1, source_target_pairs={{0,12},{1,13},{2,14},{3,15},{4,8},{5,9},{6,10},{7,11},{8,4},{9,5},... | collective-permute-start | bytes 786440 | tf_op jit(solution)/shard_map/out1_z3/ppermute | solution.py:314
  115.9 10.7 %collective-permute-start.19 = (bf16[2,4,4,2,32,512]{5,4,3,2,1,0:T(8,128)(2,1)S(1)}, bf16[2,4,4,2,32,512]{5,4,3,2,1,0:T(8,128)(2,1)S(1)}, u32[]{:S(2)}, u32[]{:S(2)}) collective-permute-start(bf16[2,4,4,2,32,512]{5,4,3,2,1,0:T(8,128)(2,1)S(1)} %join.13.refs_4_), channel_id=1, source_target_pairs={{0,1},{1,0},{2,3},{3,2},{4,5},{5,4},{6,7},{7,6},{8,9},{9,8},{10,11... | collective-permute-start | bytes 6291464 | tf_op jit(solution)/shard_map/in2_core/ppermute | solution.py:314
  116.0 25.6 %collective-permute-start.18 = (bf16[4,4,2,32,512]{4,3,2,1,0:T(8,128)(2,1)S(1)}, bf16[4,4,2,32,512]{4,3,2,1,0:T(8,128)(2,1)S(1)}, u32[]{:S(2)}, u32[]{:S(2)}) collective-permute-start(bf16[4,4,2,32,512]{4,3,2,1,0:T(8,128)(2,1)S(1)} %join.14.refs_3_.refs_0_), channel_id=1, source_target_pairs={{0,2},{1,3},{2,0},{3,1},{4,6},{5,7},{6,4},{7,5},{8,10},{9,11},{10,... | collective-permute-start | bytes 3145736 | tf_op jit(solution)/shard_map/in3_y/ppermute | solution.py:314
  126.5 31.2 %collective-permute-start.25 = (bf16[4,2,32,512]{3,2,1,0:T(8,128)(2,1)S(1)}, bf16[4,2,32,512]{3,2,1,0:T(8,128)(2,1)S(1)}, u32[]{:S(2)}, u32[]{:S(2)}) collective-permute-start(bf16[4,2,32,512]{3,2,1,0:T(8,128)(2,1)S(1)} %get-tuple-element.79), channel_id=1, source_target_pairs={{0,4},{1,5},{2,6},{3,7},{4,0},{5,1},{6,2},{7,3},{8,12},{9,13},{10,... | collective-permute-start | bytes 786440 | tf_op jit(solution)/shard_map/out1_z1/ppermute | solution.py:314
  126.6 22.3 %collective-permute-start.24 = (bf16[4,2,32,512]{3,2,1,0:T(8,128)(2,1)S(1)}, bf16[4,2,32,512]{3,2,1,0:T(8,128)(2,1)S(1)}, u32[]{:S(2)}, u32[]{:S(2)}) collective-permute-start(bf16[4,2,32,512]{3,2,1,0:T(8,128)(2,1)S(1)} %get-tuple-element.66.refs_3_), channel_id=1, source_target_pairs={{0,8},{1,9},{2,10},{3,11},{4,12},{5,13},{6,14},{7,15},{8,0},{9,1},... | collective-permute-start | bytes 786440 | tf_op jit(solution)/shard_map/out1_z2/ppermute | solution.py:314
  134.9 23.7 %collective-permute-start.26 = (bf16[4,2,32,512]{3,2,1,0:T(8,128)(2,1)S(1)}, bf16[4,2,32,512]{3,2,1,0:T(8,128)(2,1)S(1)}, u32[]{:S(2)}, u32[]{:S(2)}) collective-permute-start(bf16[4,2,32,512]{3,2,1,0:T(8,128)(2,1)S(1)} %release.12.refs_2_), channel_id=1, source_target_pairs={{0,12},{1,13},{2,14},{3,15},{4,8},{5,9},{6,10},{7,11},{8,4},{9,5},... | collective-permute-start | bytes 786440 | tf_op jit(solution)/shard_map/out2_z3/ppermute | solution.py:314
  141.8 11.7 %collective-permute-start.23 = (bf16[2,4,4,2,32,512]{5,4,3,2,1,0:T(8,128)(2,1)S(1)}, bf16[2,4,4,2,32,512]{5,4,3,2,1,0:T(8,128)(2,1)S(1)}, u32[]{:S(2)}, u32[]{:S(2)}) collective-permute-start(bf16[2,4,4,2,32,512]{5,4,3,2,1,0:T(8,128)(2,1)S(1)} %join.15.refs_3_), channel_id=1, source_target_pairs={{0,1},{1,0},{2,3},{3,2},{4,5},{5,4},{6,7},{7,6},{8,9},{9,8},{10,11... | collective-permute-start | bytes 6291464 | tf_op jit(solution)/shard_map/in3_core/ppermute | solution.py:314
  148.9 25.8 %collective-permute-start.30 = (bf16[4,2,32,512]{3,2,1,0:T(8,128)(2,1)S(1)}, bf16[4,2,32,512]{3,2,1,0:T(8,128)(2,1)S(1)}, u32[]{:S(2)}, u32[]{:S(2)}) collective-permute-start(bf16[4,2,32,512]{3,2,1,0:T(8,128)(2,1)S(1)} %get-tuple-element.83), channel_id=1, source_target_pairs={{0,4},{1,5},{2,6},{3,7},{4,0},{5,1},{6,2},{7,3},{8,12},{9,13},{10,... | collective-permute-start | bytes 786440 | tf_op jit(solution)/shard_map/out2_z1/ppermute | solution.py:314
  149.5 21.3 %collective-permute-start.27 = (bf16[4,2,32,512]{3,2,1,0:T(8,128)(2,1)S(1)}, bf16[4,2,32,512]{3,2,1,0:T(8,128)(2,1)S(1)}, u32[]{:S(2)}, u32[]{:S(2)}) collective-permute-start(bf16[4,2,32,512]{3,2,1,0:T(8,128)(2,1)S(1)} %get-tuple-element.73.refs_3_), channel_id=1, source_target_pairs={{0,8},{1,9},{2,10},{3,11},{4,12},{5,13},{6,14},{7,15},{8,0},{9,1},... | collective-permute-start | bytes 786440 | tf_op jit(solution)/shard_map/out2_z2/ppermute | solution.py:314
  158.6 21.8 %collective-permute-start.29 = (bf16[4,2,32,512]{3,2,1,0:T(8,128)(2,1)S(1)}, bf16[4,2,32,512]{3,2,1,0:T(8,128)(2,1)S(1)}, u32[]{:S(2)}, u32[]{:S(2)}) collective-permute-start(bf16[4,2,32,512]{3,2,1,0:T(8,128)(2,1)S(1)} %release.14.refs_3_), channel_id=1, source_target_pairs={{0,12},{1,13},{2,14},{3,15},{4,8},{5,9},{6,10},{7,11},{8,4},{9,5},... | collective-permute-start | bytes 786440 | tf_op jit(solution)/shard_map/out3_z3/ppermute | solution.py:314
  170.9 9.5 %collective-permute-start.28 = (bf16[4,2,32,512]{3,2,1,0:T(8,128)(2,1)S(1)}, bf16[4,2,32,512]{3,2,1,0:T(8,128)(2,1)S(1)}, u32[]{:S(2)}, u32[]{:S(2)}) collective-permute-start(bf16[4,2,32,512]{3,2,1,0:T(8,128)(2,1)S(1)} %get-tuple-element.81), channel_id=1, source_target_pairs={{0,4},{1,5},{2,6},{3,7},{4,0},{5,1},{6,2},{7,3},{8,12},{9,13},{10,... | collective-permute-start | bytes 786440 | tf_op jit(solution)/shard_map/out3_z1/ppermute | solution.py:314
  171.3 15.9 %collective-permute-start.31 = (bf16[4,2,32,512]{3,2,1,0:T(8,128)(2,1)S(1)}, bf16[4,2,32,512]{3,2,1,0:T(8,128)(2,1)S(1)}, u32[]{:S(2)}, u32[]{:S(2)}) collective-permute-start(bf16[4,2,32,512]{3,2,1,0:T(8,128)(2,1)S(1)} %get-tuple-element.84.refs_3_), channel_id=1, source_target_pairs={{0,8},{1,9},{2,10},{3,11},{4,12},{5,13},{6,14},{7,15},{8,0},{9,1},... | collective-permute-start | bytes 786440 | tf_op jit(solution)/shard_map/out3_z2/ppermute | solution.py:314
  (7 other events, 29.5 us)

commit v5 on v4

--- a/solution.py
+++ b/solution.py
@@ -340,6 +340,7 @@
     made = [{} for _ in range(chunks)]
     leaving = [{} for _ in range(chunks)]
     result, merge = [None], []
+    first_chunk = lax.slice_in_dim(spectra, 0, n, axis=2)
 
     def parts(at):
         return [cross[at]] + (([0] + rest) if at == len(cross) - 1 else [])
@@ -349,7 +350,8 @@
             return
         wanted = parts(at)
         with jax.named_scope(f"in{k}_{at}"):
-            blocks = relayout(me, spectra, k, n, wanted, order())
+            own, at_chunk = (spectra, k) if k else (first_chunk, 0)
+            blocks = relayout(me, own, at_chunk, n, wanted, order())
         last.append(blocks[0])
         arrived[k].update(depart(dict(zip(wanted, blocks)), f"in{k}"))
 

time: 189 us -> 188 us (level)
    unnamed x14 -> x12, local copies, waits for them, and re-layouts: 5.19 us -> 3 us
where the time goes in v5:
time: 188 us
  waiting for transfers between devices  105 us (56%)
  starting transfers between devices  47.7 us (25%)
  Pallas kernels  29.7 us (16%)
  local copies, waits for them, and re-layouts  4.47 us (2%)
    ppermute x32, waiting for transfers between devices, send(): return lax.ppermute(block, 'shot', [(d, d ^ offset) for d in range(n)])  105 us
    ppermute x32, starting transfers between devices, send(): return lax.ppermute(block, 'shot', [(d, d ^ offset) for d in range(n)])  47.7 us
    pallas_call x4, Pallas kernels, product(): pl.pallas_call(functools.partial(product_kernel, k, n, planes), out_shape...  16 us
    pallas_call x4, Pallas kernels, assemble(): pl.pallas_call(functools.partial(assemble_kernel, n, shots, k, list(block...  5.07 us
    pallas_call x4, Pallas kernels, early(): pl.pallas_call(functools.partial(early_kernel, list(blocks)), out_shape=j...  3.82 us
  transfers between devices with their start and end apart: 32, of which 16 were waited for; matrix products, arithmetic and copies ran while one was open for 0% of the time, Pallas kernels for 15%

profile of v5, /device:TPU:0, one launch (start us, length us, event | category | flops | bytes accessed | tf_op | source)
XLA Modules:
  0.0 187.9 jit_solution(581818958652248352)
XLA Ops:
  1.7 5.1 %collective-permute-start = (bf16[4,2,32,512]{3,2,1,0:T(8,128)(2,1)S(1)}, bf16[4,2,32,512]{3,2,1,0:T(8,128)(2,1)S(1)}, u32[]{:S(2)}, u32[]{:S(2)}) collective-permute-start(bf16[4,2,32,512]{3,2,1,0:T(8,128)(2,1)S(1)} %relayout.8.refs_0_), channel_id=1, source_target_pairs={{0,12},{1,13},{2,14},{3,15},{4,8},{5,9},{6,10},{7,11},{8,4},{9,5},... | collective-permute-start | bytes 786440 | tf_op jit(solution)/shard_map/in0_z3/ppermute | solution.py:314
  8.2 5.8 %collective-permute-done.refs_1_.refs_3_ = bf16[4,2,32,512]{3,2,1,0:T(8,128)(2,1)S(1)} collective-permute-done((bf16[4,2,32,512]{3,2,1,0:T(8,128)(2,1)S(1)}, bf16[4,2,32,512]{3,2,1,0:T(8,128)(2,1)S(1)}, u32[]{:S(2)}, u32[]{:S(2)}) %collective-permute-start) | collective-permute-done | bytes 262176 | tf_op jit(solution)/shard_map/in0_z3/ppermute | solution.py:314
  14.0 2.2 %copy-done.2 = bf16[32,2,64,512]{3,2,1,0:T(8,128)(2,1)S(1)} copy-done((bf16[32,2,64,512]{3,2,1,0:T(8,128)(2,1)S(1)}, bf16[32,2,64,512]{3,2,1,0:T(8,128)(2,1)}, u32[]{:S(2)}) %copy-start.2) | copy-done | bytes 4194328
  16.5 3.8 %collective-permute-start.4 = (bf16[4,2,32,512]{3,2,1,0:T(8,128)(2,1)S(1)}, bf16[4,2,32,512]{3,2,1,0:T(8,128)(2,1)S(1)}, u32[]{:S(2)}, u32[]{:S(2)}) collective-permute-start(bf16[4,2,32,512]{3,2,1,0:T(8,128)(2,1)S(1)} %relayout.10.refs_0_), channel_id=1, source_target_pairs={{0,12},{1,13},{2,14},{3,15},{4,8},{5,9},{6,10},{7,11},{8,4},{9,5},... | collective-permute-start | bytes 786440 | tf_op jit(solution)/shard_map/in1_z3/ppermute | solution.py:314
  20.3 15.3 %collective-permute-done.1.refs_1_.refs_2_ = bf16[4,2,32,512]{3,2,1,0:T(8,128)(2,1)S(1)} collective-permute-done((bf16[4,2,32,512]{3,2,1,0:T(8,128)(2,1)S(1)}, bf16[4,2,32,512]{3,2,1,0:T(8,128)(2,1)S(1)}, u32[]{:S(2)}, u32[]{:S(2)}) %collective-permute-start.1) | collective-permute-done | bytes 262176 | tf_op jit(solution)/shard_map/in0_z2/ppermute | solution.py:314
  36.6 3.3 %collective-permute-start.7 = (bf16[4,2,32,512]{3,2,1,0:T(8,128)(2,1)S(1)}, bf16[4,2,32,512]{3,2,1,0:T(8,128)(2,1)S(1)}, u32[]{:S(2)}, u32[]{:S(2)}) collective-permute-start(bf16[4,2,32,512]{3,2,1,0:T(8,128)(2,1)S(1)} %get-tuple-element.51), channel_id=1, source_target_pairs={{0,4},{1,5},{2,6},{3,7},{4,0},{5,1},{6,2},{7,3},{8,12},{9,13},{10,... | collective-permute-start | bytes 786440 | tf_op jit(solution)/shard_map/in1_z1/ppermute | solution.py:314
  43.8 14.4 %collective-permute-done.5.refs_1_.refs_2_ = bf16[4,2,32,512]{3,2,1,0:T(8,128)(2,1)S(1)} collective-permute-done((bf16[4,2,32,512]{3,2,1,0:T(8,128)(2,1)S(1)}, bf16[4,2,32,512]{3,2,1,0:T(8,128)(2,1)S(1)}, u32[]{:S(2)}, u32[]{:S(2)}) %collective-permute-start.5) | collective-permute-done | bytes 262176 | tf_op jit(solution)/shard_map/in1_z2/ppermute | solution.py:314
  58.8 3.2 %collective-permute-start.9 = (bf16[4,2,32,512]{3,2,1,0:T(8,128)(2,1)S(1)}, bf16[4,2,32,512]{3,2,1,0:T(8,128)(2,1)S(1)}, u32[]{:S(2)}, u32[]{:S(2)}) collective-permute-start(bf16[4,2,32,512]{3,2,1,0:T(8,128)(2,1)S(1)} %get-tuple-element.49.refs_2_), channel_id=1, source_target_pairs={{0,8},{1,9},{2,10},{3,11},{4,12},{5,13},{6,14},{7,15},{8,0},{9,1},... | collective-permute-start | bytes 786440 | tf_op jit(solution)/shard_map/in2_z2/ppermute | solution.py:314
  63.3 1.6 collective-permute-start.14
  65.2 1.6 collective-permute-start.12
  67.4 4.0 %product.4 = (bf16[4,2,32,512]{3,2,1,0:T(8,128)(2,1)S(1)}, bf16[4,2,32,512]{3,2,1,0:T(8,128)(2,1)S(1)}, bf16[4,2,32,512]{3,2,1,0:T(8,128)(2,1)S(1)}, bf16[4,2,32,512]{3,2,1,0:T(8,128)(2,1)S(1)}) custom-call(s32[1]{0:T(128)} %bitcast.me_ref, f32[2,64]{1,0:T(2,128)S(1)} %copy-done.5, s32[1,512]{1,0:T(1,128)S(1)} %bitcast.4, s32[512,1]{1,0:T(8,128)S(1)} %copy.10.fold_col_ref, ...), custom_call_target="tpu_custom_call" | custom-call | tf_op jit(solution)/shard_map/chunk0/product/pallas_call | solution.py:300
  71.4 9.2 %collective-permute-done.9.refs_1_.refs_2_ = bf16[4,2,32,512]{3,2,1,0:T(8,128)(2,1)S(1)} collective-permute-done((bf16[4,2,32,512]{3,2,1,0:T(8,128)(2,1)S(1)}, bf16[4,2,32,512]{3,2,1,0:T(8,128)(2,1)S(1)}, u32[]{:S(2)}, u32[]{:S(2)}) %collective-permute-start.9) | collective-permute-done | bytes 262176 | tf_op jit(solution)/shard_map/in2_z2/ppermute | solution.py:314
  81.3 3.2 %collective-permute-start.11 = (bf16[4,2,32,512]{3,2,1,0:T(8,128)(2,1)S(1)}, bf16[4,2,32,512]{3,2,1,0:T(8,128)(2,1)S(1)}, u32[]{:S(2)}, u32[]{:S(2)}) collective-permute-start(bf16[4,2,32,512]{3,2,1,0:T(8,128)(2,1)S(1)} %get-tuple-element.55.refs_2_), channel_id=1, source_target_pairs={{0,8},{1,9},{2,10},{3,11},{4,12},{5,13},{6,14},{7,15},{8,0},{9,1},... | collective-permute-start | bytes 786440 | tf_op jit(solution)/shard_map/in3_z2/ppermute | solution.py:314
  84.5 4.5 %collective-permute-done.14.refs_1_ = bf16[4,4,2,32,512]{4,3,2,1,0:T(8,128)(2,1)S(1)} collective-permute-done((bf16[4,4,2,32,512]{4,3,2,1,0:T(8,128)(2,1)S(1)}, bf16[4,4,2,32,512]{4,3,2,1,0:T(8,128)(2,1)S(1)}, u32[]{:S(2)}, u32[]{:S(2)}) %collective-permute-start.14) | collective-permute-done | bytes 1048608 | tf_op jit(solution)/shard_map/in1_y/ppermute | solution.py:314
  89.3 1.6 collective-permute-start.15
  90.9 1.6 collective-permute-start.17
  93.3 4.0 %product.5 = (bf16[4,2,32,512]{3,2,1,0:T(8,128)(2,1)S(1)}, bf16[4,2,32,512]{3,2,1,0:T(8,128)(2,1)S(1)}, bf16[4,2,32,512]{3,2,1,0:T(8,128)(2,1)S(1)}, bf16[4,2,32,512]{3,2,1,0:T(8,128)(2,1)S(1)}) custom-call(s32[1]{0:T(128)} %bitcast.me_ref, f32[2,64]{1,0:T(2,128)S(1)} %copy-done.5, s32[1,512]{1,0:T(1,128)S(1)} %bitcast.5, s32[512,1]{1,0:T(8,128)S(1)} %copy.10.fold_col_ref, ...), custom_call_target="tpu_custom_call" | custom-call | tf_op jit(solution)/shard_map/chunk1/product/pallas_call | solution.py:300
  97.3 5.8 %collective-permute-done.11.refs_4_.refs_2_ = bf16[4,2,32,512]{3,2,1,0:T(8,128)(2,1)S(1)} collective-permute-done((bf16[4,2,32,512]{3,2,1,0:T(8,128)(2,1)S(1)}, bf16[4,2,32,512]{3,2,1,0:T(8,128)(2,1)S(1)}, u32[]{:S(2)}, u32[]{:S(2)}) %collective-permute-start.11) | collective-permute-done | bytes 262176 | tf_op jit(solution)/shard_map/in3_z2/ppermute | solution.py:314
  103.2 3.2 %collective-permute-start.20 = (bf16[4,2,32,512]{3,2,1,0:T(8,128)(2,1)S(1)}, bf16[4,2,32,512]{3,2,1,0:T(8,128)(2,1)S(1)}, u32[]{:S(2)}, u32[]{:S(2)}) collective-permute-start(bf16[4,2,32,512]{3,2,1,0:T(8,128)(2,1)S(1)} %get-tuple-element.63.refs_1_), channel_id=1, source_target_pairs={{0,8},{1,9},{2,10},{3,11},{4,12},{5,13},{6,14},{7,15},{8,0},{9,1},... | collective-permute-start | bytes 786440 | tf_op jit(solution)/shard_map/out0_z2/ppermute | solution.py:314
  107.7 7.2 %collective-permute-done.15.refs_1_ = bf16[4,4,2,32,512]{4,3,2,1,0:T(8,128)(2,1)S(1)} collective-permute-done((bf16[4,4,2,32,512]{4,3,2,1,0:T(8,128)(2,1)S(1)}, bf16[4,4,2,32,512]{4,3,2,1,0:T(8,128)(2,1)S(1)}, u32[]{:S(2)}, u32[]{:S(2)}) %collective-permute-start.15) | collective-permute-done | bytes 1048608 | tf_op jit(solution)/shard_map/in2_y/ppermute | solution.py:314
  115.4 1.6 collective-permute-start.18
  116.9 8.6 %collective-permute-done.20.refs_4_.refs_0_ = bf16[4,2,32,512]{3,2,1,0:T(8,128)(2,1)S(1)} collective-permute-done((bf16[4,2,32,512]{3,2,1,0:T(8,128)(2,1)S(1)}, bf16[4,2,32,512]{3,2,1,0:T(8,128)(2,1)S(1)}, u32[]{:S(2)}, u32[]{:S(2)}) %collective-permute-start.20) | collective-permute-done | bytes 262176 | tf_op jit(solution)/shard_map/out0_z2/ppermute | solution.py:314
  125.7 3.2 %collective-permute-start.24 = (bf16[4,2,32,512]{3,2,1,0:T(8,128)(2,1)S(1)}, bf16[4,2,32,512]{3,2,1,0:T(8,128)(2,1)S(1)}, u32[]{:S(2)}, u32[]{:S(2)}) collective-permute-start(bf16[4,2,32,512]{3,2,1,0:T(8,128)(2,1)S(1)} %get-tuple-element.66.refs_3_), channel_id=1, source_target_pairs={{0,8},{1,9},{2,10},{3,11},{4,12},{5,13},{6,14},{7,15},{8,0},{9,1},... | collective-permute-start | bytes 786440 | tf_op jit(solution)/shard_map/out1_z2/ppermute | solution.py:314
  128.9 4.0 %product.6 = (bf16[4,2,32,512]{3,2,1,0:T(8,128)(2,1)S(1)}, bf16[4,2,32,512]{3,2,1,0:T(8,128)(2,1)S(1)}, bf16[4,2,32,512]{3,2,1,0:T(8,128)(2,1)S(1)}, bf16[4,2,32,512]{3,2,1,0:T(8,128)(2,1)S(1)}) custom-call(s32[1]{0:T(128)} %bitcast.me_ref, f32[2,64]{1,0:T(2,128)S(1)} %copy-done.5, s32[1,512]{1,0:T(1,128)S(1)} %bitcast.6, s32[512,1]{1,0:T(8,128)S(1)} %copy.10.fold_col_ref, ...), custom_call_target="tpu_custom_call" | custom-call | tf_op jit(solution)/shard_map/chunk2/product/pallas_call | solution.py:300
  135.2 5.8 %collective-permute-done.18.refs_1_ = bf16[4,4,2,32,512]{4,3,2,1,0:T(8,128)(2,1)S(1)} collective-permute-done((bf16[4,4,2,32,512]{4,3,2,1,0:T(8,128)(2,1)S(1)}, bf16[4,4,2,32,512]{4,3,2,1,0:T(8,128)(2,1)S(1)}, u32[]{:S(2)}, u32[]{:S(2)}) %collective-permute-start.18) | collective-permute-done | bytes 1048608 | tf_op jit(solution)/shard_map/in3_y/ppermute | solution.py:314
  141.2 6.8 %collective-permute-done.24.refs_4_.refs_0_ = bf16[4,2,32,512]{3,2,1,0:T(8,128)(2,1)S(1)} collective-permute-done((bf16[4,2,32,512]{3,2,1,0:T(8,128)(2,1)S(1)}, bf16[4,2,32,512]{3,2,1,0:T(8,128)(2,1)S(1)}, u32[]{:S(2)}, u32[]{:S(2)}) %collective-permute-start.24) | collective-permute-done | bytes 262176 | tf_op jit(solution)/shard_map/out1_z2/ppermute | solution.py:314
  148.8 2.6 %collective-permute-start.27 = (bf16[4,2,32,512]{3,2,1,0:T(8,128)(2,1)S(1)}, bf16[4,2,32,512]{3,2,1,0:T(8,128)(2,1)S(1)}, u32[]{:S(2)}, u32[]{:S(2)}) collective-permute-start(bf16[4,2,32,512]{3,2,1,0:T(8,128)(2,1)S(1)} %get-tuple-element.73.refs_3_), channel_id=1, source_target_pairs={{0,8},{1,9},{2,10},{3,11},{4,12},{5,13},{6,14},{7,15},{8,0},{9,1},... | collective-permute-start | bytes 786440 | tf_op jit(solution)/shard_map/out2_z2/ppermute | solution.py:314
  152.7 4.0 %product.7 = (bf16[4,2,32,512]{3,2,1,0:T(8,128)(2,1)S(1)}, bf16[4,2,32,512]{3,2,1,0:T(8,128)(2,1)S(1)}, bf16[4,2,32,512]{3,2,1,0:T(8,128)(2,1)S(1)}, bf16[4,2,32,512]{3,2,1,0:T(8,128)(2,1)S(1)}) custom-call(s32[1]{0:T(128)} %bitcast.me_ref, f32[2,64]{1,0:T(2,128)S(1)} %copy-done.5, s32[1,512]{1,0:T(1,128)S(1)} %bitcast.7, s32[512,1]{1,0:T(8,128)S(1)} %copy.10.fold_col_ref, ...), custom_call_target="tpu_custom_call" | custom-call | tf_op jit(solution)/shard_map/chunk3/product/pallas_call | solution.py:300
  158.9 11.2 %collective-permute-done.27.refs_4_.refs_0_ = bf16[4,2,32,512]{3,2,1,0:T(8,128)(2,1)S(1)} collective-permute-done((bf16[4,2,32,512]{3,2,1,0:T(8,128)(2,1)S(1)}, bf16[4,2,32,512]{3,2,1,0:T(8,128)(2,1)S(1)}, u32[]{:S(2)}, u32[]{:S(2)}) %collective-permute-start.27) | collective-permute-done | bytes 262176 | tf_op jit(solution)/shard_map/out2_z2/ppermute | solution.py:314
  170.5 3.4 %collective-permute-start.31 = (bf16[4,2,32,512]{3,2,1,0:T(8,128)(2,1)S(1)}, bf16[4,2,32,512]{3,2,1,0:T(8,128)(2,1)S(1)}, u32[]{:S(2)}, u32[]{:S(2)}) collective-permute-start(bf16[4,2,32,512]{3,2,1,0:T(8,128)(2,1)S(1)} %get-tuple-element.84.refs_3_), channel_id=1, source_target_pairs={{0,8},{1,9},{2,10},{3,11},{4,12},{5,13},{6,14},{7,15},{8,0},{9,1},... | collective-permute-start | bytes 786440 | tf_op jit(solution)/shard_map/out3_z2/ppermute | solution.py:314
  177.4 1.8 collective-permute-done.28.refs_1_
  180.2 6.3 %collective-permute-done.31.refs_0_ = bf16[4,2,32,512]{3,2,1,0:T(8,128)(2,1)S(1)} collective-permute-done((bf16[4,2,32,512]{3,2,1,0:T(8,128)(2,1)S(1)}, bf16[4,2,32,512]{3,2,1,0:T(8,128)(2,1)S(1)}, u32[]{:S(2)}, u32[]{:S(2)}) %collective-permute-start.31) | collective-permute-done | bytes 262176 | tf_op jit(solution)/shard_map/out3_z2/ppermute | solution.py:314
  (83 shorter events, 27.2 us)
Async XLA Ops:
  1.7 12.3 %collective-permute-start = (bf16[4,2,32,512]{3,2,1,0:T(8,128)(2,1)S(1)}, bf16[4,2,32,512]{3,2,1,0:T(8,128)(2,1)S(1)}, u32[]{:S(2)}, u32[]{:S(2)}) collective-permute-start(bf16[4,2,32,512]{3,2,1,0:T(8,128)(2,1)S(1)} %relayout.8.refs_0_), channel_id=1, source_target_pairs={{0,12},{1,13},{2,14},{3,15},{4,8},{5,9},{6,10},{7,11},{8,4},{9,5},... | collective-permute-start | bytes 786440 | tf_op jit(solution)/shard_map/in0_z3/ppermute | solution.py:314
  7.4 32.5 %collective-permute-start.2 = (bf16[4,2,32,512]{3,2,1,0:T(8,128)(2,1)S(1)}, bf16[4,2,32,512]{3,2,1,0:T(8,128)(2,1)S(1)}, u32[]{:S(2)}, u32[]{:S(2)}) collective-permute-start(bf16[4,2,32,512]{3,2,1,0:T(8,128)(2,1)S(1)} %get-tuple-element.48), channel_id=1, source_target_pairs={{0,4},{1,5},{2,6},{3,7},{4,0},{5,1},{6,2},{7,3},{8,12},{9,13},{10,... | collective-permute-start | bytes 786440 | tf_op jit(solution)/shard_map/in0_z1/ppermute | solution.py:314
  7.4 28.2 %collective-permute-start.1 = (bf16[4,2,32,512]{3,2,1,0:T(8,128)(2,1)S(1)}, bf16[4,2,32,512]{3,2,1,0:T(8,128)(2,1)S(1)}, u32[]{:S(2)}, u32[]{:S(2)}) collective-permute-start(bf16[4,2,32,512]{3,2,1,0:T(8,128)(2,1)S(1)} %get-tuple-element.45.refs_0_), channel_id=1, source_target_pairs={{0,8},{1,9},{2,10},{3,11},{4,12},{5,13},{6,14},{7,15},{8,0},{9,1},... | collective-permute-start | bytes 786440 | tf_op jit(solution)/shard_map/in0_z2/ppermute | solution.py:314
  16.5 25.7 %collective-permute-start.4 = (bf16[4,2,32,512]{3,2,1,0:T(8,128)(2,1)S(1)}, bf16[4,2,32,512]{3,2,1,0:T(8,128)(2,1)S(1)}, u32[]{:S(2)}, u32[]{:S(2)}) collective-permute-start(bf16[4,2,32,512]{3,2,1,0:T(8,128)(2,1)S(1)} %relayout.10.refs_0_), channel_id=1, source_target_pairs={{0,12},{1,13},{2,14},{3,15},{4,8},{5,9},{6,10},{7,11},{8,4},{9,5},... | collective-permute-start | bytes 786440 | tf_op jit(solution)/shard_map/in1_z3/ppermute | solution.py:314
  36.3 21.9 %collective-permute-start.5 = (bf16[4,2,32,512]{3,2,1,0:T(8,128)(2,1)S(1)}, bf16[4,2,32,512]{3,2,1,0:T(8,128)(2,1)S(1)}, u32[]{:S(2)}, u32[]{:S(2)}) collective-permute-start(bf16[4,2,32,512]{3,2,1,0:T(8,128)(2,1)S(1)} %get-tuple-element.46.refs_0_), channel_id=1, source_target_pairs={{0,8},{1,9},{2,10},{3,11},{4,12},{5,13},{6,14},{7,15},{8,0},{9,1},... | collective-permute-start | bytes 786440 | tf_op jit(solution)/shard_map/in1_z2/ppermute | solution.py:314
  36.6 26.7 %collective-permute-start.7 = (bf16[4,2,32,512]{3,2,1,0:T(8,128)(2,1)S(1)}, bf16[4,2,32,512]{3,2,1,0:T(8,128)(2,1)S(1)}, u32[]{:S(2)}, u32[]{:S(2)}) collective-permute-start(bf16[4,2,32,512]{3,2,1,0:T(8,128)(2,1)S(1)} %get-tuple-element.51), channel_id=1, source_target_pairs={{0,4},{1,5},{2,6},{3,7},{4,0},{5,1},{6,2},{7,3},{8,12},{9,13},{10,... | collective-permute-start | bytes 786440 | tf_op jit(solution)/shard_map/in1_z1/ppermute | solution.py:314
  40.7 22.3 %collective-permute-start.3 = (bf16[4,4,2,32,512]{4,3,2,1,0:T(8,128)(2,1)S(1)}, bf16[4,4,2,32,512]{4,3,2,1,0:T(8,128)(2,1)S(1)}, u32[]{:S(2)}, u32[]{:S(2)}) collective-permute-start(bf16[4,4,2,32,512]{4,3,2,1,0:T(8,128)(2,1)S(1)} %join.8.refs_0_), channel_id=1, source_target_pairs={{0,2},{1,3},{2,0},{3,1},{4,6},{5,7},{6,4},{7,5},{8,10},{9,11},{10,... | collective-permute-start | bytes 3145736 | tf_op jit(solution)/shard_map/in0_y/ppermute | solution.py:314
  42.5 22.4 %collective-permute-start.8 = (bf16[4,2,32,512]{3,2,1,0:T(8,128)(2,1)S(1)}, bf16[4,2,32,512]{3,2,1,0:T(8,128)(2,1)S(1)}, u32[]{:S(2)}, u32[]{:S(2)}) collective-permute-start(bf16[4,2,32,512]{3,2,1,0:T(8,128)(2,1)S(1)} %relayout.12.refs_0_), channel_id=1, source_target_pairs={{0,12},{1,13},{2,14},{3,15},{4,8},{5,9},{6,10},{7,11},{8,4},{9,5},... | collective-permute-start | bytes 786440 | tf_op jit(solution)/shard_map/in2_z3/ppermute | solution.py:314
  58.7 30.5 %collective-permute-start.13 = (bf16[4,2,32,512]{3,2,1,0:T(8,128)(2,1)S(1)}, bf16[4,2,32,512]{3,2,1,0:T(8,128)(2,1)S(1)}, u32[]{:S(2)}, u32[]{:S(2)}) collective-permute-start(bf16[4,2,32,512]{3,2,1,0:T(8,128)(2,1)S(1)} %get-tuple-element.57), channel_id=1, source_target_pairs={{0,4},{1,5},{2,6},{3,7},{4,0},{5,1},{6,2},{7,3},{8,12},{9,13},{10,... | collective-permute-start | bytes 786440 | tf_op jit(solution)/shard_map/in2_z1/ppermute | solution.py:314
  58.8 21.8 %collective-permute-start.9 = (bf16[4,2,32,512]{3,2,1,0:T(8,128)(2,1)S(1)}, bf16[4,2,32,512]{3,2,1,0:T(8,128)(2,1)S(1)}, u32[]{:S(2)}, u32[]{:S(2)}) collective-permute-start(bf16[4,2,32,512]{3,2,1,0:T(8,128)(2,1)S(1)} %get-tuple-element.49.refs_2_), channel_id=1, source_target_pairs={{0,8},{1,9},{2,10},{3,11},{4,12},{5,13},{6,14},{7,15},{8,0},{9,1},... | collective-permute-start | bytes 786440 | tf_op jit(solution)/shard_map/in2_z2/ppermute | solution.py:314
  63.2 4.2 %collective-permute-start.6 = (bf16[2,4,4,2,32,512]{5,4,3,2,1,0:T(8,128)(2,1)S(1)}, bf16[2,4,4,2,32,512]{5,4,3,2,1,0:T(8,128)(2,1)S(1)}, u32[]{:S(2)}, u32[]{:S(2)}) collective-permute-start(bf16[2,4,4,2,32,512]{5,4,3,2,1,0:T(8,128)(2,1)S(1)} %join.9.refs_4_), channel_id=1, source_target_pairs={{0,1},{1,0},{2,3},{3,2},{4,5},{5,4},{6,7},{7,6},{8,9},{9,8},{10,11... | collective-permute-start | bytes 6291464 | tf_op jit(solution)/shard_map/in0_core/ppermute | solution.py:314
  63.3 25.6 %collective-permute-start.14 = (bf16[4,4,2,32,512]{4,3,2,1,0:T(8,128)(2,1)S(1)}, bf16[4,4,2,32,512]{4,3,2,1,0:T(8,128)(2,1)S(1)}, u32[]{:S(2)}, u32[]{:S(2)}) collective-permute-start(bf16[4,4,2,32,512]{4,3,2,1,0:T(8,128)(2,1)S(1)} %join.10.refs_0_), channel_id=1, source_target_pairs={{0,2},{1,3},{2,0},{3,1},{4,6},{5,7},{6,4},{7,5},{8,10},{9,11},{10,... | collective-permute-start | bytes 3145736 | tf_op jit(solution)/shard_map/in1_y/ppermute | solution.py:314
  65.2 25.6 %collective-permute-start.12 = (bf16[4,2,32,512]{3,2,1,0:T(8,128)(2,1)S(1)}, bf16[4,2,32,512]{3,2,1,0:T(8,128)(2,1)S(1)}, u32[]{:S(2)}, u32[]{:S(2)}) collective-permute-start(bf16[4,2,32,512]{3,2,1,0:T(8,128)(2,1)S(1)} %relayout.14.refs_3_), channel_id=1, source_target_pairs={{0,12},{1,13},{2,14},{3,15},{4,8},{5,9},{6,10},{7,11},{8,4},{9,5},... | collective-permute-start | bytes 786440 | tf_op jit(solution)/shard_map/in3_z3/ppermute | solution.py:314
  81.2 33.9 %collective-permute-start.10 = (bf16[4,2,32,512]{3,2,1,0:T(8,128)(2,1)S(1)}, bf16[4,2,32,512]{3,2,1,0:T(8,128)(2,1)S(1)}, u32[]{:S(2)}, u32[]{:S(2)}) collective-permute-start(bf16[4,2,32,512]{3,2,1,0:T(8,128)(2,1)S(1)} %get-tuple-element.54), channel_id=1, source_target_pairs={{0,4},{1,5},{2,6},{3,7},{4,0},{5,1},{6,2},{7,3},{8,12},{9,13},{10,... | collective-permute-start | bytes 786440 | tf_op jit(solution)/shard_map/in3_z1/ppermute | solution.py:314
  81.3 21.8 %collective-permute-start.11 = (bf16[4,2,32,512]{3,2,1,0:T(8,128)(2,1)S(1)}, bf16[4,2,32,512]{3,2,1,0:T(8,128)(2,1)S(1)}, u32[]{:S(2)}, u32[]{:S(2)}) collective-permute-start(bf16[4,2,32,512]{3,2,1,0:T(8,128)(2,1)S(1)} %get-tuple-element.55.refs_2_), channel_id=1, source_target_pairs={{0,8},{1,9},{2,10},{3,11},{4,12},{5,13},{6,14},{7,15},{8,0},{9,1},... | collective-permute-start | bytes 786440 | tf_op jit(solution)/shard_map/in3_z2/ppermute | solution.py:314
  89.1 4.2 %collective-permute-start.16 = (bf16[2,4,4,2,32,512]{5,4,3,2,1,0:T(8,128)(2,1)S(1)}, bf16[2,4,4,2,32,512]{5,4,3,2,1,0:T(8,128)(2,1)S(1)}, u32[]{:S(2)}, u32[]{:S(2)}) collective-permute-start(bf16[2,4,4,2,32,512]{5,4,3,2,1,0:T(8,128)(2,1)S(1)} %join.11.refs_4_), channel_id=1, source_target_pairs={{0,1},{1,0},{2,3},{3,2},{4,5},{5,4},{6,7},{7,6},{8,9},{9,8},{10,11... | collective-permute-start | bytes 6291464 | tf_op jit(solution)/shard_map/in1_core/ppermute | solution.py:314
  89.3 25.6 %collective-permute-start.15 = (bf16[4,4,2,32,512]{4,3,2,1,0:T(8,128)(2,1)S(1)}, bf16[4,4,2,32,512]{4,3,2,1,0:T(8,128)(2,1)S(1)}, u32[]{:S(2)}, u32[]{:S(2)}) collective-permute-start(bf16[4,4,2,32,512]{4,3,2,1,0:T(8,128)(2,1)S(1)} %join.12.refs_1_.refs_0_), channel_id=1, source_target_pairs={{0,2},{1,3},{2,0},{3,1},{4,6},{5,7},{6,4},{7,5},{8,10},{9,11},{10,... | collective-permute-start | bytes 3145736 | tf_op jit(solution)/shard_map/in2_y/ppermute | solution.py:314
  90.9 15.6 %collective-permute-start.17 = (bf16[4,2,32,512]{3,2,1,0:T(8,128)(2,1)S(1)}, bf16[4,2,32,512]{3,2,1,0:T(8,128)(2,1)S(1)}, u32[]{:S(2)}, u32[]{:S(2)}) collective-permute-start(bf16[4,2,32,512]{3,2,1,0:T(8,128)(2,1)S(1)} %release.8.refs_3_), channel_id=1, source_target_pairs={{0,12},{1,13},{2,14},{3,15},{4,8},{5,9},{6,10},{7,11},{8,4},{9,5},... | collective-permute-start | bytes 786440 | tf_op jit(solution)/shard_map/out0_z3/ppermute | solution.py:314
  103.1 29.8 %collective-permute-start.21 = (bf16[4,2,32,512]{3,2,1,0:T(8,128)(2,1)S(1)}, bf16[4,2,32,512]{3,2,1,0:T(8,128)(2,1)S(1)}, u32[]{:S(2)}, u32[]{:S(2)}) collective-permute-start(bf16[4,2,32,512]{3,2,1,0:T(8,128)(2,1)S(1)} %get-tuple-element.69), channel_id=1, source_target_pairs={{0,4},{1,5},{2,6},{3,7},{4,0},{5,1},{6,2},{7,3},{8,12},{9,13},{10,... | collective-permute-start | bytes 786440 | tf_op jit(solution)/shard_map/out0_z1/ppermute | solution.py:314
  103.2 22.3 %collective-permute-start.20 = (bf16[4,2,32,512]{3,2,1,0:T(8,128)(2,1)S(1)}, bf16[4,2,32,512]{3,2,1,0:T(8,128)(2,1)S(1)}, u32[]{:S(2)}, u32[]{:S(2)}) collective-permute-start(bf16[4,2,32,512]{3,2,1,0:T(8,128)(2,1)S(1)} %get-tuple-element.63.refs_1_), channel_id=1, source_target_pairs={{0,8},{1,9},{2,10},{3,11},{4,12},{5,13},{6,14},{7,15},{8,0},{9,1},... | collective-permute-start | bytes 786440 | tf_op jit(solution)/shard_map/out0_z2/ppermute | solution.py:314
  106.5 27.4 %collective-permute-start.22 = (bf16[4,2,32,512]{3,2,1,0:T(8,128)(2,1)S(1)}, bf16[4,2,32,512]{3,2,1,0:T(8,128)(2,1)S(1)}, u32[]{:S(2)}, u32[]{:S(2)}) collective-permute-start(bf16[4,2,32,512]{3,2,1,0:T(8,128)(2,1)S(1)} %release.10.refs_2_), channel_id=1, source_target_pairs={{0,12},{1,13},{2,14},{3,15},{4,8},{5,9},{6,10},{7,11},{8,4},{9,5},... | collective-permute-start | bytes 786440 | tf_op jit(solution)/shard_map/out1_z3/ppermute | solution.py:314
  115.0 10.7 %collective-permute-start.19 = (bf16[2,4,4,2,32,512]{5,4,3,2,1,0:T(8,128)(2,1)S(1)}, bf16[2,4,4,2,32,512]{5,4,3,2,1,0:T(8,128)(2,1)S(1)}, u32[]{:S(2)}, u32[]{:S(2)}) collective-permute-start(bf16[2,4,4,2,32,512]{5,4,3,2,1,0:T(8,128)(2,1)S(1)} %join.13.refs_4_), channel_id=1, source_target_pairs={{0,1},{1,0},{2,3},{3,2},{4,5},{5,4},{6,7},{7,6},{8,9},{9,8},{10,11... | collective-permute-start | bytes 6291464 | tf_op jit(solution)/shard_map/in2_core/ppermute | solution.py:314
  115.4 25.6 %collective-permute-start.18 = (bf16[4,4,2,32,512]{4,3,2,1,0:T(8,128)(2,1)S(1)}, bf16[4,4,2,32,512]{4,3,2,1,0:T(8,128)(2,1)S(1)}, u32[]{:S(2)}, u32[]{:S(2)}) collective-permute-start(bf16[4,4,2,32,512]{4,3,2,1,0:T(8,128)(2,1)S(1)} %join.14.refs_3_.refs_0_), channel_id=1, source_target_pairs={{0,2},{1,3},{2,0},{3,1},{4,6},{5,7},{6,4},{7,5},{8,10},{9,11},{10,... | collective-permute-start | bytes 3145736 | tf_op jit(solution)/shard_map/in3_y/ppermute | solution.py:314
  125.6 31.1 %collective-permute-start.25 = (bf16[4,2,32,512]{3,2,1,0:T(8,128)(2,1)S(1)}, bf16[4,2,32,512]{3,2,1,0:T(8,128)(2,1)S(1)}, u32[]{:S(2)}, u32[]{:S(2)}) collective-permute-start(bf16[4,2,32,512]{3,2,1,0:T(8,128)(2,1)S(1)} %get-tuple-element.79), channel_id=1, source_target_pairs={{0,4},{1,5},{2,6},{3,7},{4,0},{5,1},{6,2},{7,3},{8,12},{9,13},{10,... | collective-permute-start | bytes 786440 | tf_op jit(solution)/shard_map/out1_z1/ppermute | solution.py:314
  125.7 22.3 %collective-permute-start.24 = (bf16[4,2,32,512]{3,2,1,0:T(8,128)(2,1)S(1)}, bf16[4,2,32,512]{3,2,1,0:T(8,128)(2,1)S(1)}, u32[]{:S(2)}, u32[]{:S(2)}) collective-permute-start(bf16[4,2,32,512]{3,2,1,0:T(8,128)(2,1)S(1)} %get-tuple-element.66.refs_3_), channel_id=1, source_target_pairs={{0,8},{1,9},{2,10},{3,11},{4,12},{5,13},{6,14},{7,15},{8,0},{9,1},... | collective-permute-start | bytes 786440 | tf_op jit(solution)/shard_map/out1_z2/ppermute | solution.py:314
  133.9 23.7 %collective-permute-start.26 = (bf16[4,2,32,512]{3,2,1,0:T(8,128)(2,1)S(1)}, bf16[4,2,32,512]{3,2,1,0:T(8,128)(2,1)S(1)}, u32[]{:S(2)}, u32[]{:S(2)}) collective-permute-start(bf16[4,2,32,512]{3,2,1,0:T(8,128)(2,1)S(1)} %release.12.refs_2_), channel_id=1, source_target_pairs={{0,12},{1,13},{2,14},{3,15},{4,8},{5,9},{6,10},{7,11},{8,4},{9,5},... | collective-permute-start | bytes 786440 | tf_op jit(solution)/shard_map/out2_z3/ppermute | solution.py:314
  141.1 11.5 %collective-permute-start.23 = (bf16[2,4,4,2,32,512]{5,4,3,2,1,0:T(8,128)(2,1)S(1)}, bf16[2,4,4,2,32,512]{5,4,3,2,1,0:T(8,128)(2,1)S(1)}, u32[]{:S(2)}, u32[]{:S(2)}) collective-permute-start(bf16[2,4,4,2,32,512]{5,4,3,2,1,0:T(8,128)(2,1)S(1)} %join.15.refs_3_), channel_id=1, source_target_pairs={{0,1},{1,0},{2,3},{3,2},{4,5},{5,4},{6,7},{7,6},{8,9},{9,8},{10,11... | collective-permute-start | bytes 6291464 | tf_op jit(solution)/shard_map/in3_core/ppermute | solution.py:314
  148.1 25.8 %collective-permute-start.30 = (bf16[4,2,32,512]{3,2,1,0:T(8,128)(2,1)S(1)}, bf16[4,2,32,512]{3,2,1,0:T(8,128)(2,1)S(1)}, u32[]{:S(2)}, u32[]{:S(2)}) collective-permute-start(bf16[4,2,32,512]{3,2,1,0:T(8,128)(2,1)S(1)} %get-tuple-element.83), channel_id=1, source_target_pairs={{0,4},{1,5},{2,6},{3,7},{4,0},{5,1},{6,2},{7,3},{8,12},{9,13},{10,... | collective-permute-start | bytes 786440 | tf_op jit(solution)/shard_map/out2_z1/ppermute | solution.py:314
  148.8 21.3 %collective-permute-start.27 = (bf16[4,2,32,512]{3,2,1,0:T(8,128)(2,1)S(1)}, bf16[4,2,32,512]{3,2,1,0:T(8,128)(2,1)S(1)}, u32[]{:S(2)}, u32[]{:S(2)}) collective-permute-start(bf16[4,2,32,512]{3,2,1,0:T(8,128)(2,1)S(1)} %get-tuple-element.73.refs_3_), channel_id=1, source_target_pairs={{0,8},{1,9},{2,10},{3,11},{4,12},{5,13},{6,14},{7,15},{8,0},{9,1},... | collective-permute-start | bytes 786440 | tf_op jit(solution)/shard_map/out2_z2/ppermute | solution.py:314
  157.7 21.5 %collective-permute-start.29 = (bf16[4,2,32,512]{3,2,1,0:T(8,128)(2,1)S(1)}, bf16[4,2,32,512]{3,2,1,0:T(8,128)(2,1)S(1)}, u32[]{:S(2)}, u32[]{:S(2)}) collective-permute-start(bf16[4,2,32,512]{3,2,1,0:T(8,128)(2,1)S(1)} %release.14.refs_3_), channel_id=1, source_target_pairs={{0,12},{1,13},{2,14},{3,15},{4,8},{5,9},{6,10},{7,11},{8,4},{9,5},... | collective-permute-start | bytes 786440 | tf_op jit(solution)/shard_map/out3_z3/ppermute | solution.py:314
  170.2 9.0 %collective-permute-start.28 = (bf16[4,2,32,512]{3,2,1,0:T(8,128)(2,1)S(1)}, bf16[4,2,32,512]{3,2,1,0:T(8,128)(2,1)S(1)}, u32[]{:S(2)}, u32[]{:S(2)}) collective-permute-start(bf16[4,2,32,512]{3,2,1,0:T(8,128)(2,1)S(1)} %get-tuple-element.81), channel_id=1, source_target_pairs={{0,4},{1,5},{2,6},{3,7},{4,0},{5,1},{6,2},{7,3},{8,12},{9,13},{10,... | collective-permute-start | bytes 786440 | tf_op jit(solution)/shard_map/out3_z1/ppermute | solution.py:314
  170.5 15.9 %collective-permute-start.31 = (bf16[4,2,32,512]{3,2,1,0:T(8,128)(2,1)S(1)}, bf16[4,2,32,512]{3,2,1,0:T(8,128)(2,1)S(1)}, u32[]{:S(2)}, u32[]{:S(2)}) collective-permute-start(bf16[4,2,32,512]{3,2,1,0:T(8,128)(2,1)S(1)} %get-tuple-element.84.refs_3_), channel_id=1, source_target_pairs={{0,8},{1,9},{2,10},{3,11},{4,12},{5,13},{6,14},{7,15},{8,0},{9,1},... | collective-permute-start | bytes 786440 | tf_op jit(solution)/shard_map/out3_z2/ppermute | solution.py:314
  (6 other events, 40.1 us)

commit v6 on v4

--- a/solution.py
+++ b/solution.py
@@ -206,6 +206,37 @@
         cost_estimate=PACE,
         name="relayout",
     )(me, spectra, *after)
+
+
+def first_kernel(shots, wanted, me_ref, x_ref, out):
+    width, points = x_ref.shape[2:]
+    rows, count = shots * width, PLANE * shots
+    source = lax.broadcasted_iota(jnp.int32, (count, rows), 1)
+    target = lax.broadcasted_iota(jnp.int32, (count, rows), 0)
+    plane = (me_ref[0] // PLANE) ^ wanted
+    bins = (plane * PLANE) % width + target // shots
+    hit = (target % shots) * width + bins == source
+    order = jnp.where(hit, 1.0, 0.0).astype(jnp.bfloat16)
+    for c in range(2):
+        block = x_ref[:, c].reshape(rows, points)
+        moved = jnp.dot(order, block, preferred_element_type=jnp.float32)
+        out[:, c] = moved.astype(jnp.bfloat16).reshape(PLANE, shots, points)
+
+
+def first(me, spectra, wanted):
+    shots, _, _, points = spectra.shape
+    width = 2 * PLANE
+    start = (((me[0] // PLANE) ^ wanted) * PLANE) // width * width
+    few = lax.dynamic_slice_in_dim(spectra, start, width, axis=2)
+    return pl.pallas_call(
+        functools.partial(first_kernel, shots, wanted),
+        out_shape=jax.ShapeDtypeStruct((PLANE, 2, shots, points), spectra.dtype),
+        in_specs=[smem_spec(), vmem_spec()],
+        out_specs=vmem_spec(),
+        compiler_params=params(),
+        cost_estimate=PACE,
+        name="first",
+    )(me, few)
 
 
 def join_kernel(count_in, *refs):
@@ -349,7 +380,11 @@
             return
         wanted = parts(at)
         with jax.named_scope(f"in{k}_{at}"):
-            blocks = relayout(me, spectra, k, n, wanted, order())
+            own, at_chunk = spectra, k
+            if k == 0 and at == 0:
+                blocks = [first(me, spectra, wanted[0])]
+            else:
+                blocks = relayout(me, own, at_chunk, n, wanted, order())
         last.append(blocks[0])
         arrived[k].update(depart(dict(zip(wanted, blocks)), f"in{k}"))
 

time: 189 us -> 188 us (level)
  waiting for transfers between devices: 105 us -> 103 us
  starting transfers between devices: 47.9 us -> 49.8 us
    unnamed x14, local copies, waits for them, and re-layouts: 5.19 us -> 3 us
where the time goes in v6:
time: 188 us
  waiting for transfers between devices  103 us (55%)
  starting transfers between devices  49.8 us (26%)
  Pallas kernels  29.6 us (16%)
  local copies, waits for them, and re-layouts  4.22 us (2%)
    ppermute x32, waiting for transfers between devices, send(): return lax.ppermute(block, 'shot', [(d, d ^ offset) for d in range(n)])  103 us
    ppermute x32, starting transfers between devices, send(): return lax.ppermute(block, 'shot', [(d, d ^ offset) for d in range(n)])  49.8 us
    pallas_call x4, Pallas kernels, product(): pl.pallas_call(functools.partial(product_kernel, k, n, planes), out_shape...  16 us
    pallas_call x4, Pallas kernels, assemble(): pl.pallas_call(functools.partial(assemble_kernel, n, shots, k, list(block...  5.07 us
    pallas_call x4, Pallas kernels, early(): pl.pallas_call(functools.partial(early_kernel, list(blocks)), out_shape=j...  3.82 us
  transfers between devices with their start and end apart: 32, of which 16 were waited for; matrix products, arithmetic and copies ran while one was open for 0% of the time, Pallas kernels for 15%

profile of v6, /device:TPU:0, one launch (start us, length us, event | category | flops | bytes accessed | tf_op | source)
XLA Modules:
  0.0 187.5 jit_solution(10984437980280549895)
XLA Ops:
  1.3 5.1 %collective-permute-start = (bf16[4,2,32,512]{3,2,1,0:T(8,128)(2,1)S(1)}, bf16[4,2,32,512]{3,2,1,0:T(8,128)(2,1)S(1)}, u32[]{:S(2)}, u32[]{:S(2)}) collective-permute-start(bf16[4,2,32,512]{3,2,1,0:T(8,128)(2,1)S(1)} %first.1.refs_0_), channel_id=1, source_target_pairs={{0,12},{1,13},{2,14},{3,15},{4,8},{5,9},{6,10},{7,11},{8,4},{9,5},... | collective-permute-start | bytes 786440 | tf_op jit(solution)/shard_map/in0_z3/ppermute | solution.py:345
  7.1 2.4 %collective-permute-start.1 = (bf16[4,2,32,512]{3,2,1,0:T(8,128)(2,1)S(1)}, bf16[4,2,32,512]{3,2,1,0:T(8,128)(2,1)S(1)}, u32[]{:S(2)}, u32[]{:S(2)}) collective-permute-start(bf16[4,2,32,512]{3,2,1,0:T(8,128)(2,1)S(1)} %get-tuple-element.45.refs_0_), channel_id=1, source_target_pairs={{0,8},{1,9},{2,10},{3,11},{4,12},{5,13},{6,14},{7,15},{8,0},{9,1},... | collective-permute-start | bytes 786440 | tf_op jit(solution)/shard_map/in0_z2/ppermute | solution.py:345
  9.7 4.0 %collective-permute-done.refs_1_.refs_3_ = bf16[4,2,32,512]{3,2,1,0:T(8,128)(2,1)S(1)} collective-permute-done((bf16[4,2,32,512]{3,2,1,0:T(8,128)(2,1)S(1)}, bf16[4,2,32,512]{3,2,1,0:T(8,128)(2,1)S(1)}, u32[]{:S(2)}, u32[]{:S(2)}) %collective-permute-start) | collective-permute-done | bytes 262176 | tf_op jit(solution)/shard_map/in0_z3/ppermute | solution.py:345
  13.7 2.2 %copy-done.3 = bf16[32,2,64,512]{3,2,1,0:T(8,128)(2,1)S(1)} copy-done((bf16[32,2,64,512]{3,2,1,0:T(8,128)(2,1)S(1)}, bf16[32,2,64,512]{3,2,1,0:T(8,128)(2,1)}, u32[]{:S(2)}) %copy-start.3) | copy-done | bytes 4194328
  16.2 3.9 %collective-permute-start.4 = (bf16[4,2,32,512]{3,2,1,0:T(8,128)(2,1)S(1)}, bf16[4,2,32,512]{3,2,1,0:T(8,128)(2,1)S(1)}, u32[]{:S(2)}, u32[]{:S(2)}) collective-permute-start(bf16[4,2,32,512]{3,2,1,0:T(8,128)(2,1)S(1)} %relayout.8.refs_0_), channel_id=1, source_target_pairs={{0,12},{1,13},{2,14},{3,15},{4,8},{5,9},{6,10},{7,11},{8,4},{9,5},... | collective-permute-start | bytes 786440 | tf_op jit(solution)/shard_map/in1_z3/ppermute | solution.py:345
  20.1 15.3 %collective-permute-done.1.refs_1_.refs_2_ = bf16[4,2,32,512]{3,2,1,0:T(8,128)(2,1)S(1)} collective-permute-done((bf16[4,2,32,512]{3,2,1,0:T(8,128)(2,1)S(1)}, bf16[4,2,32,512]{3,2,1,0:T(8,128)(2,1)S(1)}, u32[]{:S(2)}, u32[]{:S(2)}) %collective-permute-start.1) | collective-permute-done | bytes 262176 | tf_op jit(solution)/shard_map/in0_z2/ppermute | solution.py:345
  36.2 3.3 %collective-permute-start.7 = (bf16[4,2,32,512]{3,2,1,0:T(8,128)(2,1)S(1)}, bf16[4,2,32,512]{3,2,1,0:T(8,128)(2,1)S(1)}, u32[]{:S(2)}, u32[]{:S(2)}) collective-permute-start(bf16[4,2,32,512]{3,2,1,0:T(8,128)(2,1)S(1)} %get-tuple-element.51), channel_id=1, source_target_pairs={{0,4},{1,5},{2,6},{3,7},{4,0},{5,1},{6,2},{7,3},{8,12},{9,13},{10,... | collective-permute-start | bytes 786440 | tf_op jit(solution)/shard_map/in1_z1/ppermute | solution.py:345
  43.4 14.4 %collective-permute-done.5.refs_1_.refs_2_ = bf16[4,2,32,512]{3,2,1,0:T(8,128)(2,1)S(1)} collective-permute-done((bf16[4,2,32,512]{3,2,1,0:T(8,128)(2,1)S(1)}, bf16[4,2,32,512]{3,2,1,0:T(8,128)(2,1)S(1)}, u32[]{:S(2)}, u32[]{:S(2)}) %collective-permute-start.5) | collective-permute-done | bytes 262176 | tf_op jit(solution)/shard_map/in1_z2/ppermute | solution.py:345
  58.5 3.2 %collective-permute-start.9 = (bf16[4,2,32,512]{3,2,1,0:T(8,128)(2,1)S(1)}, bf16[4,2,32,512]{3,2,1,0:T(8,128)(2,1)S(1)}, u32[]{:S(2)}, u32[]{:S(2)}) collective-permute-start(bf16[4,2,32,512]{3,2,1,0:T(8,128)(2,1)S(1)} %get-tuple-element.49.refs_2_), channel_id=1, source_target_pairs={{0,8},{1,9},{2,10},{3,11},{4,12},{5,13},{6,14},{7,15},{8,0},{9,1},... | collective-permute-start | bytes 786440 | tf_op jit(solution)/shard_map/in2_z2/ppermute | solution.py:345
  63.0 1.6 collective-permute-start.14
  64.9 1.6 collective-permute-start.12
  67.1 4.0 %product.4 = (bf16[4,2,32,512]{3,2,1,0:T(8,128)(2,1)S(1)}, bf16[4,2,32,512]{3,2,1,0:T(8,128)(2,1)S(1)}, bf16[4,2,32,512]{3,2,1,0:T(8,128)(2,1)S(1)}, bf16[4,2,32,512]{3,2,1,0:T(8,128)(2,1)S(1)}) custom-call(s32[1]{0:T(128)} %bitcast.me_ref, f32[2,64]{1,0:T(2,128)S(1)} %copy-done.6, s32[1,512]{1,0:T(1,128)S(1)} %bitcast.4, s32[512,1]{1,0:T(8,128)S(1)} %copy.10.fold_col_ref, ...), custom_call_target="tpu_custom_call" | custom-call | tf_op jit(solution)/shard_map/chunk0/product/pallas_call | solution.py:331
  71.1 9.2 %collective-permute-done.9.refs_1_.refs_2_ = bf16[4,2,32,512]{3,2,1,0:T(8,128)(2,1)S(1)} collective-permute-done((bf16[4,2,32,512]{3,2,1,0:T(8,128)(2,1)S(1)}, bf16[4,2,32,512]{3,2,1,0:T(8,128)(2,1)S(1)}, u32[]{:S(2)}, u32[]{:S(2)}) %collective-permute-start.9) | collective-permute-done | bytes 262176 | tf_op jit(solution)/shard_map/in2_z2/ppermute | solution.py:345
  80.9 3.2 %collective-permute-start.11 = (bf16[4,2,32,512]{3,2,1,0:T(8,128)(2,1)S(1)}, bf16[4,2,32,512]{3,2,1,0:T(8,128)(2,1)S(1)}, u32[]{:S(2)}, u32[]{:S(2)}) collective-permute-start(bf16[4,2,32,512]{3,2,1,0:T(8,128)(2,1)S(1)} %get-tuple-element.55.refs_2_), channel_id=1, source_target_pairs={{0,8},{1,9},{2,10},{3,11},{4,12},{5,13},{6,14},{7,15},{8,0},{9,1},... | collective-permute-start | bytes 786440 | tf_op jit(solution)/shard_map/in3_z2/ppermute | solution.py:345
  84.2 4.5 %collective-permute-done.14.refs_1_ = bf16[4,4,2,32,512]{4,3,2,1,0:T(8,128)(2,1)S(1)} collective-permute-done((bf16[4,4,2,32,512]{4,3,2,1,0:T(8,128)(2,1)S(1)}, bf16[4,4,2,32,512]{4,3,2,1,0:T(8,128)(2,1)S(1)}, u32[]{:S(2)}, u32[]{:S(2)}) %collective-permute-start.14) | collective-permute-done | bytes 1048608 | tf_op jit(solution)/shard_map/in1_y/ppermute | solution.py:345
  90.5 1.6 collective-permute-start.17
  93.0 4.0 %product.5 = (bf16[4,2,32,512]{3,2,1,0:T(8,128)(2,1)S(1)}, bf16[4,2,32,512]{3,2,1,0:T(8,128)(2,1)S(1)}, bf16[4,2,32,512]{3,2,1,0:T(8,128)(2,1)S(1)}, bf16[4,2,32,512]{3,2,1,0:T(8,128)(2,1)S(1)}) custom-call(s32[1]{0:T(128)} %bitcast.me_ref, f32[2,64]{1,0:T(2,128)S(1)} %copy-done.6, s32[1,512]{1,0:T(1,128)S(1)} %bitcast.5, s32[512,1]{1,0:T(8,128)S(1)} %copy.10.fold_col_ref, ...), custom_call_target="tpu_custom_call" | custom-call | tf_op jit(solution)/shard_map/chunk1/product/pallas_call | solution.py:331
  97.0 5.8 %collective-permute-done.11.refs_4_.refs_2_ = bf16[4,2,32,512]{3,2,1,0:T(8,128)(2,1)S(1)} collective-permute-done((bf16[4,2,32,512]{3,2,1,0:T(8,128)(2,1)S(1)}, bf16[4,2,32,512]{3,2,1,0:T(8,128)(2,1)S(1)}, u32[]{:S(2)}, u32[]{:S(2)}) %collective-permute-start.11) | collective-permute-done | bytes 262176 | tf_op jit(solution)/shard_map/in3_z2/ppermute | solution.py:345
  102.9 3.2 %collective-permute-start.20 = (bf16[4,2,32,512]{3,2,1,0:T(8,128)(2,1)S(1)}, bf16[4,2,32,512]{3,2,1,0:T(8,128)(2,1)S(1)}, u32[]{:S(2)}, u32[]{:S(2)}) collective-permute-start(bf16[4,2,32,512]{3,2,1,0:T(8,128)(2,1)S(1)} %get-tuple-element.63.refs_1_), channel_id=1, source_target_pairs={{0,8},{1,9},{2,10},{3,11},{4,12},{5,13},{6,14},{7,15},{8,0},{9,1},... | collective-permute-start | bytes 786440 | tf_op jit(solution)/shard_map/out0_z2/ppermute | solution.py:345
  107.4 7.2 %collective-permute-done.15.refs_1_ = bf16[4,4,2,32,512]{4,3,2,1,0:T(8,128)(2,1)S(1)} collective-permute-done((bf16[4,4,2,32,512]{4,3,2,1,0:T(8,128)(2,1)S(1)}, bf16[4,4,2,32,512]{4,3,2,1,0:T(8,128)(2,1)S(1)}, u32[]{:S(2)}, u32[]{:S(2)}) %collective-permute-start.15) | collective-permute-done | bytes 1048608 | tf_op jit(solution)/shard_map/in2_y/ppermute | solution.py:345
  114.9 1.8 collective-permute-start.18
  116.6 8.6 %collective-permute-done.20.refs_4_.refs_0_ = bf16[4,2,32,512]{3,2,1,0:T(8,128)(2,1)S(1)} collective-permute-done((bf16[4,2,32,512]{3,2,1,0:T(8,128)(2,1)S(1)}, bf16[4,2,32,512]{3,2,1,0:T(8,128)(2,1)S(1)}, u32[]{:S(2)}, u32[]{:S(2)}) %collective-permute-start.20) | collective-permute-done | bytes 262176 | tf_op jit(solution)/shard_map/out0_z2/ppermute | solution.py:345
  125.4 3.2 %collective-permute-start.24 = (bf16[4,2,32,512]{3,2,1,0:T(8,128)(2,1)S(1)}, bf16[4,2,32,512]{3,2,1,0:T(8,128)(2,1)S(1)}, u32[]{:S(2)}, u32[]{:S(2)}) collective-permute-start(bf16[4,2,32,512]{3,2,1,0:T(8,128)(2,1)S(1)} %get-tuple-element.66.refs_3_), channel_id=1, source_target_pairs={{0,8},{1,9},{2,10},{3,11},{4,12},{5,13},{6,14},{7,15},{8,0},{9,1},... | collective-permute-start | bytes 786440 | tf_op jit(solution)/shard_map/out1_z2/ppermute | solution.py:345
  128.6 4.0 %product.6 = (bf16[4,2,32,512]{3,2,1,0:T(8,128)(2,1)S(1)}, bf16[4,2,32,512]{3,2,1,0:T(8,128)(2,1)S(1)}, bf16[4,2,32,512]{3,2,1,0:T(8,128)(2,1)S(1)}, bf16[4,2,32,512]{3,2,1,0:T(8,128)(2,1)S(1)}) custom-call(s32[1]{0:T(128)} %bitcast.me_ref, f32[2,64]{1,0:T(2,128)S(1)} %copy-done.6, s32[1,512]{1,0:T(1,128)S(1)} %bitcast.6, s32[512,1]{1,0:T(8,128)S(1)} %copy.10.fold_col_ref, ...), custom_call_target="tpu_custom_call" | custom-call | tf_op jit(solution)/shard_map/chunk2/product/pallas_call | solution.py:331
  134.8 5.8 %collective-permute-done.18.refs_1_ = bf16[4,4,2,32,512]{4,3,2,1,0:T(8,128)(2,1)S(1)} collective-permute-done((bf16[4,4,2,32,512]{4,3,2,1,0:T(8,128)(2,1)S(1)}, bf16[4,4,2,32,512]{4,3,2,1,0:T(8,128)(2,1)S(1)}, u32[]{:S(2)}, u32[]{:S(2)}) %collective-permute-start.18) | collective-permute-done | bytes 1048608 | tf_op jit(solution)/shard_map/in3_y/ppermute | solution.py:345
  140.9 6.8 %collective-permute-done.24.refs_4_.refs_0_ = bf16[4,2,32,512]{3,2,1,0:T(8,128)(2,1)S(1)} collective-permute-done((bf16[4,2,32,512]{3,2,1,0:T(8,128)(2,1)S(1)}, bf16[4,2,32,512]{3,2,1,0:T(8,128)(2,1)S(1)}, u32[]{:S(2)}, u32[]{:S(2)}) %collective-permute-start.24) | collective-permute-done | bytes 262176 | tf_op jit(solution)/shard_map/out1_z2/ppermute | solution.py:345
  148.5 2.6 %collective-permute-start.27 = (bf16[4,2,32,512]{3,2,1,0:T(8,128)(2,1)S(1)}, bf16[4,2,32,512]{3,2,1,0:T(8,128)(2,1)S(1)}, u32[]{:S(2)}, u32[]{:S(2)}) collective-permute-start(bf16[4,2,32,512]{3,2,1,0:T(8,128)(2,1)S(1)} %get-tuple-element.73.refs_3_), channel_id=1, source_target_pairs={{0,8},{1,9},{2,10},{3,11},{4,12},{5,13},{6,14},{7,15},{8,0},{9,1},... | collective-permute-start | bytes 786440 | tf_op jit(solution)/shard_map/out2_z2/ppermute | solution.py:345
  152.3 4.0 %product.7 = (bf16[4,2,32,512]{3,2,1,0:T(8,128)(2,1)S(1)}, bf16[4,2,32,512]{3,2,1,0:T(8,128)(2,1)S(1)}, bf16[4,2,32,512]{3,2,1,0:T(8,128)(2,1)S(1)}, bf16[4,2,32,512]{3,2,1,0:T(8,128)(2,1)S(1)}) custom-call(s32[1]{0:T(128)} %bitcast.me_ref, f32[2,64]{1,0:T(2,128)S(1)} %copy-done.6, s32[1,512]{1,0:T(1,128)S(1)} %bitcast.7, s32[512,1]{1,0:T(8,128)S(1)} %copy.10.fold_col_ref, ...), custom_call_target="tpu_custom_call" | custom-call | tf_op jit(solution)/shard_map/chunk3/product/pallas_call | solution.py:331
  158.6 11.2 %collective-permute-done.27.refs_4_.refs_0_ = bf16[4,2,32,512]{3,2,1,0:T(8,128)(2,1)S(1)} collective-permute-done((bf16[4,2,32,512]{3,2,1,0:T(8,128)(2,1)S(1)}, bf16[4,2,32,512]{3,2,1,0:T(8,128)(2,1)S(1)}, u32[]{:S(2)}, u32[]{:S(2)}) %collective-permute-start.27) | collective-permute-done | bytes 262176 | tf_op jit(solution)/shard_map/out2_z2/ppermute | solution.py:345
  170.2 3.4 %collective-permute-start.31 = (bf16[4,2,32,512]{3,2,1,0:T(8,128)(2,1)S(1)}, bf16[4,2,32,512]{3,2,1,0:T(8,128)(2,1)S(1)}, u32[]{:S(2)}, u32[]{:S(2)}) collective-permute-start(bf16[4,2,32,512]{3,2,1,0:T(8,128)(2,1)S(1)} %get-tuple-element.84.refs_3_), channel_id=1, source_target_pairs={{0,8},{1,9},{2,10},{3,11},{4,12},{5,13},{6,14},{7,15},{8,0},{9,1},... | collective-permute-start | bytes 786440 | tf_op jit(solution)/shard_map/out3_z2/ppermute | solution.py:345
  177.1 1.8 collective-permute-done.28.refs_1_
  179.8 6.3 %collective-permute-done.31.refs_0_ = bf16[4,2,32,512]{3,2,1,0:T(8,128)(2,1)S(1)} collective-permute-done((bf16[4,2,32,512]{3,2,1,0:T(8,128)(2,1)S(1)}, bf16[4,2,32,512]{3,2,1,0:T(8,128)(2,1)S(1)}, u32[]{:S(2)}, u32[]{:S(2)}) %collective-permute-start.31) | collective-permute-done | bytes 262176 | tf_op jit(solution)/shard_map/out3_z2/ppermute | solution.py:345
  (85 shorter events, 27.9 us)
Async XLA Ops:
  1.3 12.3 %collective-permute-start = (bf16[4,2,32,512]{3,2,1,0:T(8,128)(2,1)S(1)}, bf16[4,2,32,512]{3,2,1,0:T(8,128)(2,1)S(1)}, u32[]{:S(2)}, u32[]{:S(2)}) collective-permute-start(bf16[4,2,32,512]{3,2,1,0:T(8,128)(2,1)S(1)} %first.1.refs_0_), channel_id=1, source_target_pairs={{0,12},{1,13},{2,14},{3,15},{4,8},{5,9},{6,10},{7,11},{8,4},{9,5},... | collective-permute-start | bytes 786440 | tf_op jit(solution)/shard_map/in0_z3/ppermute | solution.py:345
  7.0 32.5 %collective-permute-start.2 = (bf16[4,2,32,512]{3,2,1,0:T(8,128)(2,1)S(1)}, bf16[4,2,32,512]{3,2,1,0:T(8,128)(2,1)S(1)}, u32[]{:S(2)}, u32[]{:S(2)}) collective-permute-start(bf16[4,2,32,512]{3,2,1,0:T(8,128)(2,1)S(1)} %get-tuple-element.48), channel_id=1, source_target_pairs={{0,4},{1,5},{2,6},{3,7},{4,0},{5,1},{6,2},{7,3},{8,12},{9,13},{10,... | collective-permute-start | bytes 786440 | tf_op jit(solution)/shard_map/in0_z1/ppermute | solution.py:345
  7.1 28.2 %collective-permute-start.1 = (bf16[4,2,32,512]{3,2,1,0:T(8,128)(2,1)S(1)}, bf16[4,2,32,512]{3,2,1,0:T(8,128)(2,1)S(1)}, u32[]{:S(2)}, u32[]{:S(2)}) collective-permute-start(bf16[4,2,32,512]{3,2,1,0:T(8,128)(2,1)S(1)} %get-tuple-element.45.refs_0_), channel_id=1, source_target_pairs={{0,8},{1,9},{2,10},{3,11},{4,12},{5,13},{6,14},{7,15},{8,0},{9,1},... | collective-permute-start | bytes 786440 | tf_op jit(solution)/shard_map/in0_z2/ppermute | solution.py:345
  16.2 25.7 %collective-permute-start.4 = (bf16[4,2,32,512]{3,2,1,0:T(8,128)(2,1)S(1)}, bf16[4,2,32,512]{3,2,1,0:T(8,128)(2,1)S(1)}, u32[]{:S(2)}, u32[]{:S(2)}) collective-permute-start(bf16[4,2,32,512]{3,2,1,0:T(8,128)(2,1)S(1)} %relayout.8.refs_0_), channel_id=1, source_target_pairs={{0,12},{1,13},{2,14},{3,15},{4,8},{5,9},{6,10},{7,11},{8,4},{9,5},... | collective-permute-start | bytes 786440 | tf_op jit(solution)/shard_map/in1_z3/ppermute | solution.py:345
  35.9 21.9 %collective-permute-start.5 = (bf16[4,2,32,512]{3,2,1,0:T(8,128)(2,1)S(1)}, bf16[4,2,32,512]{3,2,1,0:T(8,128)(2,1)S(1)}, u32[]{:S(2)}, u32[]{:S(2)}) collective-permute-start(bf16[4,2,32,512]{3,2,1,0:T(8,128)(2,1)S(1)} %get-tuple-element.46.refs_0_), channel_id=1, source_target_pairs={{0,8},{1,9},{2,10},{3,11},{4,12},{5,13},{6,14},{7,15},{8,0},{9,1},... | collective-permute-start | bytes 786440 | tf_op jit(solution)/shard_map/in1_z2/ppermute | solution.py:345
  36.2 26.7 %collective-permute-start.7 = (bf16[4,2,32,512]{3,2,1,0:T(8,128)(2,1)S(1)}, bf16[4,2,32,512]{3,2,1,0:T(8,128)(2,1)S(1)}, u32[]{:S(2)}, u32[]{:S(2)}) collective-permute-start(bf16[4,2,32,512]{3,2,1,0:T(8,128)(2,1)S(1)} %get-tuple-element.51), channel_id=1, source_target_pairs={{0,4},{1,5},{2,6},{3,7},{4,0},{5,1},{6,2},{7,3},{8,12},{9,13},{10,... | collective-permute-start | bytes 786440 | tf_op jit(solution)/shard_map/in1_z1/ppermute | solution.py:345
  40.4 22.3 %collective-permute-start.3 = (bf16[4,4,2,32,512]{4,3,2,1,0:T(8,128)(2,1)S(1)}, bf16[4,4,2,32,512]{4,3,2,1,0:T(8,128)(2,1)S(1)}, u32[]{:S(2)}, u32[]{:S(2)}) collective-permute-start(bf16[4,4,2,32,512]{4,3,2,1,0:T(8,128)(2,1)S(1)} %join.8.refs_0_), channel_id=1, source_target_pairs={{0,2},{1,3},{2,0},{3,1},{4,6},{5,7},{6,4},{7,5},{8,10},{9,11},{10,... | collective-permute-start | bytes 3145736 | tf_op jit(solution)/shard_map/in0_y/ppermute | solution.py:345
  42.2 22.4 %collective-permute-start.8 = (bf16[4,2,32,512]{3,2,1,0:T(8,128)(2,1)S(1)}, bf16[4,2,32,512]{3,2,1,0:T(8,128)(2,1)S(1)}, u32[]{:S(2)}, u32[]{:S(2)}) collective-permute-start(bf16[4,2,32,512]{3,2,1,0:T(8,128)(2,1)S(1)} %relayout.10.refs_0_), channel_id=1, source_target_pairs={{0,12},{1,13},{2,14},{3,15},{4,8},{5,9},{6,10},{7,11},{8,4},{9,5},... | collective-permute-start | bytes 786440 | tf_op jit(solution)/shard_map/in2_z3/ppermute | solution.py:345
  58.4 30.5 %collective-permute-start.13 = (bf16[4,2,32,512]{3,2,1,0:T(8,128)(2,1)S(1)}, bf16[4,2,32,512]{3,2,1,0:T(8,128)(2,1)S(1)}, u32[]{:S(2)}, u32[]{:S(2)}) collective-permute-start(bf16[4,2,32,512]{3,2,1,0:T(8,128)(2,1)S(1)} %get-tuple-element.57), channel_id=1, source_target_pairs={{0,4},{1,5},{2,6},{3,7},{4,0},{5,1},{6,2},{7,3},{8,12},{9,13},{10,... | collective-permute-start | bytes 786440 | tf_op jit(solution)/shard_map/in2_z1/ppermute | solution.py:345
  58.5 21.8 %collective-permute-start.9 = (bf16[4,2,32,512]{3,2,1,0:T(8,128)(2,1)S(1)}, bf16[4,2,32,512]{3,2,1,0:T(8,128)(2,1)S(1)}, u32[]{:S(2)}, u32[]{:S(2)}) collective-permute-start(bf16[4,2,32,512]{3,2,1,0:T(8,128)(2,1)S(1)} %get-tuple-element.49.refs_2_), channel_id=1, source_target_pairs={{0,8},{1,9},{2,10},{3,11},{4,12},{5,13},{6,14},{7,15},{8,0},{9,1},... | collective-permute-start | bytes 786440 | tf_op jit(solution)/shard_map/in2_z2/ppermute | solution.py:345
  62.8 4.2 %collective-permute-start.6 = (bf16[2,4,4,2,32,512]{5,4,3,2,1,0:T(8,128)(2,1)S(1)}, bf16[2,4,4,2,32,512]{5,4,3,2,1,0:T(8,128)(2,1)S(1)}, u32[]{:S(2)}, u32[]{:S(2)}) collective-permute-start(bf16[2,4,4,2,32,512]{5,4,3,2,1,0:T(8,128)(2,1)S(1)} %join.9.refs_4_), channel_id=1, source_target_pairs={{0,1},{1,0},{2,3},{3,2},{4,5},{5,4},{6,7},{7,6},{8,9},{9,8},{10,11... | collective-permute-start | bytes 6291464 | tf_op jit(solution)/shard_map/in0_core/ppermute | solution.py:345
  63.0 25.6 %collective-permute-start.14 = (bf16[4,4,2,32,512]{4,3,2,1,0:T(8,128)(2,1)S(1)}, bf16[4,4,2,32,512]{4,3,2,1,0:T(8,128)(2,1)S(1)}, u32[]{:S(2)}, u32[]{:S(2)}) collective-permute-start(bf16[4,4,2,32,512]{4,3,2,1,0:T(8,128)(2,1)S(1)} %join.10.refs_0_), channel_id=1, source_target_pairs={{0,2},{1,3},{2,0},{3,1},{4,6},{5,7},{6,4},{7,5},{8,10},{9,11},{10,... | collective-permute-start | bytes 3145736 | tf_op jit(solution)/shard_map/in1_y/ppermute | solution.py:345
  64.9 25.6 %collective-permute-start.12 = (bf16[4,2,32,512]{3,2,1,0:T(8,128)(2,1)S(1)}, bf16[4,2,32,512]{3,2,1,0:T(8,128)(2,1)S(1)}, u32[]{:S(2)}, u32[]{:S(2)}) collective-permute-start(bf16[4,2,32,512]{3,2,1,0:T(8,128)(2,1)S(1)} %relayout.12.refs_3_), channel_id=1, source_target_pairs={{0,12},{1,13},{2,14},{3,15},{4,8},{5,9},{6,10},{7,11},{8,4},{9,5},... | collective-permute-start | bytes 786440 | tf_op jit(solution)/shard_map/in3_z3/ppermute | solution.py:345
  80.9 33.9 %collective-permute-start.10 = (bf16[4,2,32,512]{3,2,1,0:T(8,128)(2,1)S(1)}, bf16[4,2,32,512]{3,2,1,0:T(8,128)(2,1)S(1)}, u32[]{:S(2)}, u32[]{:S(2)}) collective-permute-start(bf16[4,2,32,512]{3,2,1,0:T(8,128)(2,1)S(1)} %get-tuple-element.54), channel_id=1, source_target_pairs={{0,4},{1,5},{2,6},{3,7},{4,0},{5,1},{6,2},{7,3},{8,12},{9,13},{10,... | collective-permute-start | bytes 786440 | tf_op jit(solution)/shard_map/in3_z1/ppermute | solution.py:345
  80.9 21.8 %collective-permute-start.11 = (bf16[4,2,32,512]{3,2,1,0:T(8,128)(2,1)S(1)}, bf16[4,2,32,512]{3,2,1,0:T(8,128)(2,1)S(1)}, u32[]{:S(2)}, u32[]{:S(2)}) collective-permute-start(bf16[4,2,32,512]{3,2,1,0:T(8,128)(2,1)S(1)} %get-tuple-element.55.refs_2_), channel_id=1, source_target_pairs={{0,8},{1,9},{2,10},{3,11},{4,12},{5,13},{6,14},{7,15},{8,0},{9,1},... | collective-permute-start | bytes 786440 | tf_op jit(solution)/shard_map/in3_z2/ppermute | solution.py:345
  88.8 4.2 %collective-permute-start.16 = (bf16[2,4,4,2,32,512]{5,4,3,2,1,0:T(8,128)(2,1)S(1)}, bf16[2,4,4,2,32,512]{5,4,3,2,1,0:T(8,128)(2,1)S(1)}, u32[]{:S(2)}, u32[]{:S(2)}) collective-permute-start(bf16[2,4,4,2,32,512]{5,4,3,2,1,0:T(8,128)(2,1)S(1)} %join.11.refs_4_), channel_id=1, source_target_pairs={{0,1},{1,0},{2,3},{3,2},{4,5},{5,4},{6,7},{7,6},{8,9},{9,8},{10,11... | collective-permute-start | bytes 6291464 | tf_op jit(solution)/shard_map/in1_core/ppermute | solution.py:345
  88.9 25.6 %collective-permute-start.15 = (bf16[4,4,2,32,512]{4,3,2,1,0:T(8,128)(2,1)S(1)}, bf16[4,4,2,32,512]{4,3,2,1,0:T(8,128)(2,1)S(1)}, u32[]{:S(2)}, u32[]{:S(2)}) collective-permute-start(bf16[4,4,2,32,512]{4,3,2,1,0:T(8,128)(2,1)S(1)} %join.12.refs_1_.refs_0_), channel_id=1, source_target_pairs={{0,2},{1,3},{2,0},{3,1},{4,6},{5,7},{6,4},{7,5},{8,10},{9,11},{10,... | collective-permute-start | bytes 3145736 | tf_op jit(solution)/shard_map/in2_y/ppermute | solution.py:345
  90.5 15.6 %collective-permute-start.17 = (bf16[4,2,32,512]{3,2,1,0:T(8,128)(2,1)S(1)}, bf16[4,2,32,512]{3,2,1,0:T(8,128)(2,1)S(1)}, u32[]{:S(2)}, u32[]{:S(2)}) collective-permute-start(bf16[4,2,32,512]{3,2,1,0:T(8,128)(2,1)S(1)} %release.8.refs_3_), channel_id=1, source_target_pairs={{0,12},{1,13},{2,14},{3,15},{4,8},{5,9},{6,10},{7,11},{8,4},{9,5},... | collective-permute-start | bytes 786440 | tf_op jit(solution)/shard_map/out0_z3/ppermute | solution.py:345
  102.8 29.8 %collective-permute-start.21 = (bf16[4,2,32,512]{3,2,1,0:T(8,128)(2,1)S(1)}, bf16[4,2,32,512]{3,2,1,0:T(8,128)(2,1)S(1)}, u32[]{:S(2)}, u32[]{:S(2)}) collective-permute-start(bf16[4,2,32,512]{3,2,1,0:T(8,128)(2,1)S(1)} %get-tuple-element.69), channel_id=1, source_target_pairs={{0,4},{1,5},{2,6},{3,7},{4,0},{5,1},{6,2},{7,3},{8,12},{9,13},{10,... | collective-permute-start | bytes 786440 | tf_op jit(solution)/shard_map/out0_z1/ppermute | solution.py:345
  102.9 22.3 %collective-permute-start.20 = (bf16[4,2,32,512]{3,2,1,0:T(8,128)(2,1)S(1)}, bf16[4,2,32,512]{3,2,1,0:T(8,128)(2,1)S(1)}, u32[]{:S(2)}, u32[]{:S(2)}) collective-permute-start(bf16[4,2,32,512]{3,2,1,0:T(8,128)(2,1)S(1)} %get-tuple-element.63.refs_1_), channel_id=1, source_target_pairs={{0,8},{1,9},{2,10},{3,11},{4,12},{5,13},{6,14},{7,15},{8,0},{9,1},... | collective-permute-start | bytes 786440 | tf_op jit(solution)/shard_map/out0_z2/ppermute | solution.py:345
  106.1 27.4 %collective-permute-start.22 = (bf16[4,2,32,512]{3,2,1,0:T(8,128)(2,1)S(1)}, bf16[4,2,32,512]{3,2,1,0:T(8,128)(2,1)S(1)}, u32[]{:S(2)}, u32[]{:S(2)}) collective-permute-start(bf16[4,2,32,512]{3,2,1,0:T(8,128)(2,1)S(1)} %release.10.refs_2_), channel_id=1, source_target_pairs={{0,12},{1,13},{2,14},{3,15},{4,8},{5,9},{6,10},{7,11},{8,4},{9,5},... | collective-permute-start | bytes 786440 | tf_op jit(solution)/shard_map/out1_z3/ppermute | solution.py:345
  114.7 10.7 %collective-permute-start.19 = (bf16[2,4,4,2,32,512]{5,4,3,2,1,0:T(8,128)(2,1)S(1)}, bf16[2,4,4,2,32,512]{5,4,3,2,1,0:T(8,128)(2,1)S(1)}, u32[]{:S(2)}, u32[]{:S(2)}) collective-permute-start(bf16[2,4,4,2,32,512]{5,4,3,2,1,0:T(8,128)(2,1)S(1)} %join.13.refs_4_), channel_id=1, source_target_pairs={{0,1},{1,0},{2,3},{3,2},{4,5},{5,4},{6,7},{7,6},{8,9},{9,8},{10,11... | collective-permute-start | bytes 6291464 | tf_op jit(solution)/shard_map/in2_core/ppermute | solution.py:345
  114.9 25.8 %collective-permute-start.18 = (bf16[4,4,2,32,512]{4,3,2,1,0:T(8,128)(2,1)S(1)}, bf16[4,4,2,32,512]{4,3,2,1,0:T(8,128)(2,1)S(1)}, u32[]{:S(2)}, u32[]{:S(2)}) collective-permute-start(bf16[4,4,2,32,512]{4,3,2,1,0:T(8,128)(2,1)S(1)} %join.14.refs_3_.refs_0_), channel_id=1, source_target_pairs={{0,2},{1,3},{2,0},{3,1},{4,6},{5,7},{6,4},{7,5},{8,10},{9,11},{10,... | collective-permute-start | bytes 3145736 | tf_op jit(solution)/shard_map/in3_y/ppermute | solution.py:345
  125.3 31.1 %collective-permute-start.25 = (bf16[4,2,32,512]{3,2,1,0:T(8,128)(2,1)S(1)}, bf16[4,2,32,512]{3,2,1,0:T(8,128)(2,1)S(1)}, u32[]{:S(2)}, u32[]{:S(2)}) collective-permute-start(bf16[4,2,32,512]{3,2,1,0:T(8,128)(2,1)S(1)} %get-tuple-element.79), channel_id=1, source_target_pairs={{0,4},{1,5},{2,6},{3,7},{4,0},{5,1},{6,2},{7,3},{8,12},{9,13},{10,... | collective-permute-start | bytes 786440 | tf_op jit(solution)/shard_map/out1_z1/ppermute | solution.py:345
  125.4 22.3 %collective-permute-start.24 = (bf16[4,2,32,512]{3,2,1,0:T(8,128)(2,1)S(1)}, bf16[4,2,32,512]{3,2,1,0:T(8,128)(2,1)S(1)}, u32[]{:S(2)}, u32[]{:S(2)}) collective-permute-start(bf16[4,2,32,512]{3,2,1,0:T(8,128)(2,1)S(1)} %get-tuple-element.66.refs_3_), channel_id=1, source_target_pairs={{0,8},{1,9},{2,10},{3,11},{4,12},{5,13},{6,14},{7,15},{8,0},{9,1},... | collective-permute-start | bytes 786440 | tf_op jit(solution)/shard_map/out1_z2/ppermute | solution.py:345
  133.6 23.7 %collective-permute-start.26 = (bf16[4,2,32,512]{3,2,1,0:T(8,128)(2,1)S(1)}, bf16[4,2,32,512]{3,2,1,0:T(8,128)(2,1)S(1)}, u32[]{:S(2)}, u32[]{:S(2)}) collective-permute-start(bf16[4,2,32,512]{3,2,1,0:T(8,128)(2,1)S(1)} %release.12.refs_2_), channel_id=1, source_target_pairs={{0,12},{1,13},{2,14},{3,15},{4,8},{5,9},{6,10},{7,11},{8,4},{9,5},... | collective-permute-start | bytes 786440 | tf_op jit(solution)/shard_map/out2_z3/ppermute | solution.py:345
  140.8 11.5 %collective-permute-start.23 = (bf16[2,4,4,2,32,512]{5,4,3,2,1,0:T(8,128)(2,1)S(1)}, bf16[2,4,4,2,32,512]{5,4,3,2,1,0:T(8,128)(2,1)S(1)}, u32[]{:S(2)}, u32[]{:S(2)}) collective-permute-start(bf16[2,4,4,2,32,512]{5,4,3,2,1,0:T(8,128)(2,1)S(1)} %join.15.refs_3_), channel_id=1, source_target_pairs={{0,1},{1,0},{2,3},{3,2},{4,5},{5,4},{6,7},{7,6},{8,9},{9,8},{10,11... | collective-permute-start | bytes 6291464 | tf_op jit(solution)/shard_map/in3_core/ppermute | solution.py:345
  147.8 25.8 %collective-permute-start.30 = (bf16[4,2,32,512]{3,2,1,0:T(8,128)(2,1)S(1)}, bf16[4,2,32,512]{3,2,1,0:T(8,128)(2,1)S(1)}, u32[]{:S(2)}, u32[]{:S(2)}) collective-permute-start(bf16[4,2,32,512]{3,2,1,0:T(8,128)(2,1)S(1)} %get-tuple-element.83), channel_id=1, source_target_pairs={{0,4},{1,5},{2,6},{3,7},{4,0},{5,1},{6,2},{7,3},{8,12},{9,13},{10,... | collective-permute-start | bytes 786440 | tf_op jit(solution)/shard_map/out2_z1/ppermute | solution.py:345
  148.5 21.3 %collective-permute-start.27 = (bf16[4,2,32,512]{3,2,1,0:T(8,128)(2,1)S(1)}, bf16[4,2,32,512]{3,2,1,0:T(8,128)(2,1)S(1)}, u32[]{:S(2)}, u32[]{:S(2)}) collective-permute-start(bf16[4,2,32,512]{3,2,1,0:T(8,128)(2,1)S(1)} %get-tuple-element.73.refs_3_), channel_id=1, source_target_pairs={{0,8},{1,9},{2,10},{3,11},{4,12},{5,13},{6,14},{7,15},{8,0},{9,1},... | collective-permute-start | bytes 786440 | tf_op jit(solution)/shard_map/out2_z2/ppermute | solution.py:345
  157.3 21.5 %collective-permute-start.29 = (bf16[4,2,32,512]{3,2,1,0:T(8,128)(2,1)S(1)}, bf16[4,2,32,512]{3,2,1,0:T(8,128)(2,1)S(1)}, u32[]{:S(2)}, u32[]{:S(2)}) collective-permute-start(bf16[4,2,32,512]{3,2,1,0:T(8,128)(2,1)S(1)} %release.14.refs_3_), channel_id=1, source_target_pairs={{0,12},{1,13},{2,14},{3,15},{4,8},{5,9},{6,10},{7,11},{8,4},{9,5},... | collective-permute-start | bytes 786440 | tf_op jit(solution)/shard_map/out3_z3/ppermute | solution.py:345
  169.9 9.0 %collective-permute-start.28 = (bf16[4,2,32,512]{3,2,1,0:T(8,128)(2,1)S(1)}, bf16[4,2,32,512]{3,2,1,0:T(8,128)(2,1)S(1)}, u32[]{:S(2)}, u32[]{:S(2)}) collective-permute-start(bf16[4,2,32,512]{3,2,1,0:T(8,128)(2,1)S(1)} %get-tuple-element.81), channel_id=1, source_target_pairs={{0,4},{1,5},{2,6},{3,7},{4,0},{5,1},{6,2},{7,3},{8,12},{9,13},{10,... | collective-permute-start | bytes 786440 | tf_op jit(solution)/shard_map/out3_z1/ppermute | solution.py:345
  170.2 15.9 %collective-permute-start.31 = (bf16[4,2,32,512]{3,2,1,0:T(8,128)(2,1)S(1)}, bf16[4,2,32,512]{3,2,1,0:T(8,128)(2,1)S(1)}, u32[]{:S(2)}, u32[]{:S(2)}) collective-permute-start(bf16[4,2,32,512]{3,2,1,0:T(8,128)(2,1)S(1)} %get-tuple-element.84.refs_3_), channel_id=1, source_target_pairs={{0,8},{1,9},{2,10},{3,11},{4,12},{5,13},{6,14},{7,15},{8,0},{9,1},... | collective-permute-start | bytes 786440 | tf_op jit(solution)/shard_map/out3_z2/ppermute | solution.py:345
  (7 other events, 47.3 us)

commit v7 on v6

--- a/solution.py
+++ b/solution.py
@@ -137,20 +137,34 @@
     )(order, *blocks.values(), *after)
 
 
+PIECES = 2
+
+
 def assemble_kernel(n, shots, k, which, order_ref, begun_ref, *refs):
     ins = refs[: len(which)]
     out, held, sems = refs[-3:]
     copies = []
+    part = shots // PIECES
     for c in range(2):
-        total = merged(order_ref, list(zip(which, ins)), c)
-        total = total + begun_ref[c].astype(jnp.float32)
-        held[c] = total.astype(jnp.bfloat16).reshape(shots, n, -1)
-        copies.append(
-            pltpu.make_async_copy(
-                held.at[c], out.at[:, c, pl.ds(k * n, n), :], sems.at[c]
+        for p in range(PIECES):
+            rows = pl.ds(p * part * n, part * n)
+            total = begun_ref[c, rows, :].astype(jnp.float32)
+            for j, block in zip(which, ins):
+                total = total + jnp.dot(
+                    order_ref[j, rows, :],
+                    block[:, c].reshape(-1, block.shape[3]),
+                    preferred_element_type=jnp.float32,
+                )
+            at = pl.ds(p * part, part)
+            held[c, at] = total.astype(jnp.bfloat16).reshape(part, n, -1)
+            copies.append(
+                pltpu.make_async_copy(
+                    held.at[c, at],
+                    out.at[at, c, pl.ds(k * n, n), :],
+                    sems.at[len(copies)],
+                )
             )
-        )
-        copies[c].start()
+            copies[-1].start()
     for copy in copies:
         copy.wait()
 
@@ -167,7 +181,7 @@
         out_specs=hbm_spec(),
         scratch_shapes=[
             pltpu.VMEM((2, shots, n, points), jnp.bfloat16),
-            pltpu.SemaphoreType.DMA((2,)),
+            pltpu.SemaphoreType.DMA((2 * PIECES,)),
         ],
         input_output_aliases={2 + len(blocks): 0} if extra else {},
         compiler_params=params(),
@@ -372,13 +386,13 @@
     leaving = [{} for _ in range(chunks)]
     result, merge = [None], []
 
-    def parts(at):
-        return [cross[at]] + (([0] + rest) if at == len(cross) - 1 else [])
+    def parts(at, over):
+        return [over[at]] + (([0] + rest) if at == len(over) - 1 else [])
 
     def go_in(k, at):
         if k >= chunks:
             return
-        wanted = parts(at)
+        wanted = parts(at, cross if k else cross[::-1])
         with jax.named_scope(f"in{k}_{at}"):
             own, at_chunk = spectra, k
             if k == 0 and at == 0:
@@ -391,7 +405,7 @@
     def go_out(k, at):
         if not 0 <= k < chunks:
             return
-        wanted = parts(at)
+        wanted = parts(at, cross)
         with jax.named_scope(f"out{k}_{at}"):
             blocks = release([made[k][j] for j in wanted], order())
         last.append(blocks[0])

time: 188 us -> 188 us (level)
  starting transfers between devices: 49.8 us -> 58.6 us
  waiting for transfers between devices: 103 us -> 94.9 us
    ppermute x32, starting transfers between devices: 49.8 us -> 58.6 us  [send(): return lax.ppermute(block, 'shot', [(d, d ^ offset) for d in range(n)])]
    ppermute x32, waiting for transfers between devices: 103 us -> 94.9 us  [send(): return lax.ppermute(block, 'shot', [(d, d ^ offset) for d in range(n)])]
  transfers between devices with their start and end apart: 32 -> 32, of which waited for: 16 -> 15; matrix products, arithmetic and copies ran while one was open for 0% -> 0% of each run, Pallas kernels for 15% -> 15%
where the time goes in v7:
time: 188 us
  waiting for transfers between devices  94.9 us (50%)
  starting transfers between devices  58.6 us (31%)
  Pallas kernels  29.4 us (16%)
  local copies, waits for them, and re-layouts  4.22 us (2%)
    ppermute x32, waiting for transfers between devices, send(): return lax.ppermute(block, 'shot', [(d, d ^ offset) for d in range(n)])  94.9 us
    ppermute x32, starting transfers between devices, send(): return lax.ppermute(block, 'shot', [(d, d ^ offset) for d in range(n)])  58.6 us
    pallas_call x4, Pallas kernels, product(): pl.pallas_call(functools.partial(product_kernel, k, n, planes), out_shape...  16 us
    pallas_call x4, Pallas kernels, assemble(): pl.pallas_call(functools.partial(assemble_kernel, n, shots, k, list(block...  4.84 us
    pallas_call x4, Pallas kernels, early(): pl.pallas_call(functools.partial(early_kernel, list(blocks)), out_shape=j...  3.83 us
  transfers between devices with their start and end apart: 32, of which 15 were waited for; matrix products, arithmetic and copies ran while one was open for 0% of the time, Pallas kernels for 15%

profile of v7, /device:TPU:0, one launch (start us, length us, event | category | flops | bytes accessed | tf_op | source)
XLA Modules:
  0.0 187.6 jit_solution(15538834410030400734)
XLA Ops:
  1.3 4.1 %collective-permute-start = (bf16[4,2,32,512]{3,2,1,0:T(8,128)(2,1)S(1)}, bf16[4,2,32,512]{3,2,1,0:T(8,128)(2,1)S(1)}, u32[]{:S(2)}, u32[]{:S(2)}) collective-permute-start(bf16[4,2,32,512]{3,2,1,0:T(8,128)(2,1)S(1)} %first.1.refs_0_), channel_id=1, source_target_pairs={{0,8},{1,9},{2,10},{3,11},{4,12},{5,13},{6,14},{7,15},{8,0},{9,1},... | collective-permute-start | bytes 786440 | tf_op jit(solution)/shard_map/in0_z2/ppermute | solution.py:359
  6.0 1.6 collective-permute-start.2
  7.7 1.7 collective-permute-start.1
  9.6 9.5 %collective-permute-done.refs_1_.refs_2_ = bf16[4,2,32,512]{3,2,1,0:T(8,128)(2,1)S(1)} collective-permute-done((bf16[4,2,32,512]{3,2,1,0:T(8,128)(2,1)S(1)}, bf16[4,2,32,512]{3,2,1,0:T(8,128)(2,1)S(1)}, u32[]{:S(2)}, u32[]{:S(2)}) %collective-permute-start) | collective-permute-done | bytes 262176 | tf_op jit(solution)/shard_map/in0_z2/ppermute | solution.py:359
  19.1 2.2 %copy-done.3 = bf16[32,2,64,512]{3,2,1,0:T(8,128)(2,1)S(1)} copy-done((bf16[32,2,64,512]{3,2,1,0:T(8,128)(2,1)S(1)}, bf16[32,2,64,512]{3,2,1,0:T(8,128)(2,1)}, u32[]{:S(2)}) %copy-start.3) | copy-done | bytes 4194328
  21.6 3.2 %collective-permute-start.4 = (bf16[4,2,32,512]{3,2,1,0:T(8,128)(2,1)S(1)}, bf16[4,2,32,512]{3,2,1,0:T(8,128)(2,1)S(1)}, u32[]{:S(2)}, u32[]{:S(2)}) collective-permute-start(bf16[4,2,32,512]{3,2,1,0:T(8,128)(2,1)S(1)} %relayout.8.refs_0_), channel_id=1, source_target_pairs={{0,12},{1,13},{2,14},{3,15},{4,8},{5,9},{6,10},{7,11},{8,4},{9,5},... | collective-permute-start | bytes 786440 | tf_op jit(solution)/shard_map/in1_z3/ppermute | solution.py:359
  25.4 12.3 %collective-permute-start.5 = (bf16[4,2,32,512]{3,2,1,0:T(8,128)(2,1)S(1)}, bf16[4,2,32,512]{3,2,1,0:T(8,128)(2,1)S(1)}, u32[]{:S(2)}, u32[]{:S(2)}) collective-permute-start(bf16[4,2,32,512]{3,2,1,0:T(8,128)(2,1)S(1)} %get-tuple-element.46.refs_0_), channel_id=1, source_target_pairs={{0,8},{1,9},{2,10},{3,11},{4,12},{5,13},{6,14},{7,15},{8,0},{9,1},... | collective-permute-start | bytes 786440 | tf_op jit(solution)/shard_map/in1_z2/ppermute | solution.py:359
  42.2 15.4 %collective-permute-done.5.refs_1_.refs_2_ = bf16[4,2,32,512]{3,2,1,0:T(8,128)(2,1)S(1)} collective-permute-done((bf16[4,2,32,512]{3,2,1,0:T(8,128)(2,1)S(1)}, bf16[4,2,32,512]{3,2,1,0:T(8,128)(2,1)S(1)}, u32[]{:S(2)}, u32[]{:S(2)}) %collective-permute-start.5) | collective-permute-done | bytes 262176 | tf_op jit(solution)/shard_map/in1_z2/ppermute | solution.py:359
  58.3 3.3 %collective-permute-start.9 = (bf16[4,2,32,512]{3,2,1,0:T(8,128)(2,1)S(1)}, bf16[4,2,32,512]{3,2,1,0:T(8,128)(2,1)S(1)}, u32[]{:S(2)}, u32[]{:S(2)}) collective-permute-start(bf16[4,2,32,512]{3,2,1,0:T(8,128)(2,1)S(1)} %get-tuple-element.49.refs_2_), channel_id=1, source_target_pairs={{0,8},{1,9},{2,10},{3,11},{4,12},{5,13},{6,14},{7,15},{8,0},{9,1},... | collective-permute-start | bytes 786440 | tf_op jit(solution)/shard_map/in2_z2/ppermute | solution.py:359
  61.6 2.0 %collective-permute-done.3.refs_1_ = bf16[4,4,2,32,512]{4,3,2,1,0:T(8,128)(2,1)S(1)} collective-permute-done((bf16[4,4,2,32,512]{4,3,2,1,0:T(8,128)(2,1)S(1)}, bf16[4,4,2,32,512]{4,3,2,1,0:T(8,128)(2,1)S(1)}, u32[]{:S(2)}, u32[]{:S(2)}) %collective-permute-start.3) | collective-permute-done | bytes 1048608 | tf_op jit(solution)/shard_map/in0_y/ppermute | solution.py:359
  63.9 1.6 collective-permute-start.14
  67.9 4.0 %product.4 = (bf16[4,2,32,512]{3,2,1,0:T(8,128)(2,1)S(1)}, bf16[4,2,32,512]{3,2,1,0:T(8,128)(2,1)S(1)}, bf16[4,2,32,512]{3,2,1,0:T(8,128)(2,1)S(1)}, bf16[4,2,32,512]{3,2,1,0:T(8,128)(2,1)S(1)}) custom-call(s32[1]{0:T(128)} %bitcast.me_ref, f32[2,64]{1,0:T(2,128)S(1)} %copy-done.6, s32[1,512]{1,0:T(1,128)S(1)} %bitcast.4, s32[512,1]{1,0:T(8,128)S(1)} %copy.10.fold_col_ref, ...), custom_call_target="tpu_custom_call" | custom-call | tf_op jit(solution)/shard_map/chunk0/product/pallas_call | solution.py:345
  71.9 7.9 %collective-permute-done.9.refs_1_.refs_2_ = bf16[4,2,32,512]{3,2,1,0:T(8,128)(2,1)S(1)} collective-permute-done((bf16[4,2,32,512]{3,2,1,0:T(8,128)(2,1)S(1)}, bf16[4,2,32,512]{3,2,1,0:T(8,128)(2,1)S(1)}, u32[]{:S(2)}, u32[]{:S(2)}) %collective-permute-start.9) | collective-permute-done | bytes 262176 | tf_op jit(solution)/shard_map/in2_z2/ppermute | solution.py:359
  80.7 3.4 %collective-permute-start.11 = (bf16[4,2,32,512]{3,2,1,0:T(8,128)(2,1)S(1)}, bf16[4,2,32,512]{3,2,1,0:T(8,128)(2,1)S(1)}, u32[]{:S(2)}, u32[]{:S(2)}) collective-permute-start(bf16[4,2,32,512]{3,2,1,0:T(8,128)(2,1)S(1)} %get-tuple-element.55.refs_2_), channel_id=1, source_target_pairs={{0,8},{1,9},{2,10},{3,11},{4,12},{5,13},{6,14},{7,15},{8,0},{9,1},... | collective-permute-start | bytes 786440 | tf_op jit(solution)/shard_map/in3_z2/ppermute | solution.py:359
  84.1 5.4 %collective-permute-done.14.refs_1_ = bf16[4,4,2,32,512]{4,3,2,1,0:T(8,128)(2,1)S(1)} collective-permute-done((bf16[4,4,2,32,512]{4,3,2,1,0:T(8,128)(2,1)S(1)}, bf16[4,4,2,32,512]{4,3,2,1,0:T(8,128)(2,1)S(1)}, u32[]{:S(2)}, u32[]{:S(2)}) %collective-permute-start.14) | collective-permute-done | bytes 1048608 | tf_op jit(solution)/shard_map/in1_y/ppermute | solution.py:359
  89.8 1.6 collective-permute-start.15
  93.8 4.0 %product.5 = (bf16[4,2,32,512]{3,2,1,0:T(8,128)(2,1)S(1)}, bf16[4,2,32,512]{3,2,1,0:T(8,128)(2,1)S(1)}, bf16[4,2,32,512]{3,2,1,0:T(8,128)(2,1)S(1)}, bf16[4,2,32,512]{3,2,1,0:T(8,128)(2,1)S(1)}) custom-call(s32[1]{0:T(128)} %bitcast.me_ref, f32[2,64]{1,0:T(2,128)S(1)} %copy-done.6, s32[1,512]{1,0:T(1,128)S(1)} %bitcast.5, s32[512,1]{1,0:T(8,128)S(1)} %copy.10.fold_col_ref, ...), custom_call_target="tpu_custom_call" | custom-call | tf_op jit(solution)/shard_map/chunk1/product/pallas_call | solution.py:345
  97.8 4.5 %collective-permute-done.11.refs_4_.refs_2_ = bf16[4,2,32,512]{3,2,1,0:T(8,128)(2,1)S(1)} collective-permute-done((bf16[4,2,32,512]{3,2,1,0:T(8,128)(2,1)S(1)}, bf16[4,2,32,512]{3,2,1,0:T(8,128)(2,1)S(1)}, u32[]{:S(2)}, u32[]{:S(2)}) %collective-permute-start.11) | collective-permute-done | bytes 262176 | tf_op jit(solution)/shard_map/in3_z2/ppermute | solution.py:359
  102.7 3.4 %collective-permute-start.20 = (bf16[4,2,32,512]{3,2,1,0:T(8,128)(2,1)S(1)}, bf16[4,2,32,512]{3,2,1,0:T(8,128)(2,1)S(1)}, u32[]{:S(2)}, u32[]{:S(2)}) collective-permute-start(bf16[4,2,32,512]{3,2,1,0:T(8,128)(2,1)S(1)} %get-tuple-element.63.refs_1_), channel_id=1, source_target_pairs={{0,8},{1,9},{2,10},{3,11},{4,12},{5,13},{6,14},{7,15},{8,0},{9,1},... | collective-permute-start | bytes 786440 | tf_op jit(solution)/shard_map/out0_z2/ppermute | solution.py:359
  106.9 8.5 %collective-permute-done.15.refs_1_ = bf16[4,4,2,32,512]{4,3,2,1,0:T(8,128)(2,1)S(1)} collective-permute-done((bf16[4,4,2,32,512]{4,3,2,1,0:T(8,128)(2,1)S(1)}, bf16[4,4,2,32,512]{4,3,2,1,0:T(8,128)(2,1)S(1)}, u32[]{:S(2)}, u32[]{:S(2)}) %collective-permute-start.15) | collective-permute-done | bytes 1048608 | tf_op jit(solution)/shard_map/in2_y/ppermute | solution.py:359
  115.7 1.8 collective-permute-start.18
  117.5 7.4 %collective-permute-done.20.refs_4_.refs_0_ = bf16[4,2,32,512]{3,2,1,0:T(8,128)(2,1)S(1)} collective-permute-done((bf16[4,2,32,512]{3,2,1,0:T(8,128)(2,1)S(1)}, bf16[4,2,32,512]{3,2,1,0:T(8,128)(2,1)S(1)}, u32[]{:S(2)}, u32[]{:S(2)}) %collective-permute-start.20) | collective-permute-done | bytes 262176 | tf_op jit(solution)/shard_map/out0_z2/ppermute | solution.py:359
  125.2 3.4 %collective-permute-start.24 = (bf16[4,2,32,512]{3,2,1,0:T(8,128)(2,1)S(1)}, bf16[4,2,32,512]{3,2,1,0:T(8,128)(2,1)S(1)}, u32[]{:S(2)}, u32[]{:S(2)}) collective-permute-start(bf16[4,2,32,512]{3,2,1,0:T(8,128)(2,1)S(1)} %get-tuple-element.66.refs_3_), channel_id=1, source_target_pairs={{0,8},{1,9},{2,10},{3,11},{4,12},{5,13},{6,14},{7,15},{8,0},{9,1},... | collective-permute-start | bytes 786440 | tf_op jit(solution)/shard_map/out1_z2/ppermute | solution.py:359
  128.6 4.0 %product.6 = (bf16[4,2,32,512]{3,2,1,0:T(8,128)(2,1)S(1)}, bf16[4,2,32,512]{3,2,1,0:T(8,128)(2,1)S(1)}, bf16[4,2,32,512]{3,2,1,0:T(8,128)(2,1)S(1)}, bf16[4,2,32,512]{3,2,1,0:T(8,128)(2,1)S(1)}) custom-call(s32[1]{0:T(128)} %bitcast.me_ref, f32[2,64]{1,0:T(2,128)S(1)} %copy-done.6, s32[1,512]{1,0:T(1,128)S(1)} %bitcast.6, s32[512,1]{1,0:T(8,128)S(1)} %copy.10.fold_col_ref, ...), custom_call_target="tpu_custom_call" | custom-call | tf_op jit(solution)/shard_map/chunk2/product/pallas_call | solution.py:345
  134.4 7.1 %collective-permute-done.18.refs_1_ = bf16[4,4,2,32,512]{4,3,2,1,0:T(8,128)(2,1)S(1)} collective-permute-done((bf16[4,4,2,32,512]{4,3,2,1,0:T(8,128)(2,1)S(1)}, bf16[4,4,2,32,512]{4,3,2,1,0:T(8,128)(2,1)S(1)}, u32[]{:S(2)}, u32[]{:S(2)}) %collective-permute-start.18) | collective-permute-done | bytes 1048608 | tf_op jit(solution)/shard_map/in3_y/ppermute | solution.py:359
  141.7 5.6 %collective-permute-done.24.refs_4_.refs_0_ = bf16[4,2,32,512]{3,2,1,0:T(8,128)(2,1)S(1)} collective-permute-done((bf16[4,2,32,512]{3,2,1,0:T(8,128)(2,1)S(1)}, bf16[4,2,32,512]{3,2,1,0:T(8,128)(2,1)S(1)}, u32[]{:S(2)}, u32[]{:S(2)}) %collective-permute-start.24) | collective-permute-done | bytes 262176 | tf_op jit(solution)/shard_map/out1_z2/ppermute | solution.py:359
  147.7 3.4 %collective-permute-start.27 = (bf16[4,2,32,512]{3,2,1,0:T(8,128)(2,1)S(1)}, bf16[4,2,32,512]{3,2,1,0:T(8,128)(2,1)S(1)}, u32[]{:S(2)}, u32[]{:S(2)}) collective-permute-start(bf16[4,2,32,512]{3,2,1,0:T(8,128)(2,1)S(1)} %get-tuple-element.73.refs_3_), channel_id=1, source_target_pairs={{0,8},{1,9},{2,10},{3,11},{4,12},{5,13},{6,14},{7,15},{8,0},{9,1},... | collective-permute-start | bytes 786440 | tf_op jit(solution)/shard_map/out2_z2/ppermute | solution.py:359
  152.3 4.0 %product.7 = (bf16[4,2,32,512]{3,2,1,0:T(8,128)(2,1)S(1)}, bf16[4,2,32,512]{3,2,1,0:T(8,128)(2,1)S(1)}, bf16[4,2,32,512]{3,2,1,0:T(8,128)(2,1)S(1)}, bf16[4,2,32,512]{3,2,1,0:T(8,128)(2,1)S(1)}) custom-call(s32[1]{0:T(128)} %bitcast.me_ref, f32[2,64]{1,0:T(2,128)S(1)} %copy-done.6, s32[1,512]{1,0:T(1,128)S(1)} %bitcast.7, s32[512,1]{1,0:T(8,128)S(1)} %copy.10.fold_col_ref, ...), custom_call_target="tpu_custom_call" | custom-call | tf_op jit(solution)/shard_map/chunk3/product/pallas_call | solution.py:345
  158.2 11.7 %collective-permute-done.27.refs_4_.refs_0_ = bf16[4,2,32,512]{3,2,1,0:T(8,128)(2,1)S(1)} collective-permute-done((bf16[4,2,32,512]{3,2,1,0:T(8,128)(2,1)S(1)}, bf16[4,2,32,512]{3,2,1,0:T(8,128)(2,1)S(1)}, u32[]{:S(2)}, u32[]{:S(2)}) %collective-permute-start.27) | collective-permute-done | bytes 262176 | tf_op jit(solution)/shard_map/out2_z2/ppermute | solution.py:359
  170.1 3.4 %collective-permute-start.31 = (bf16[4,2,32,512]{3,2,1,0:T(8,128)(2,1)S(1)}, bf16[4,2,32,512]{3,2,1,0:T(8,128)(2,1)S(1)}, u32[]{:S(2)}, u32[]{:S(2)}) collective-permute-start(bf16[4,2,32,512]{3,2,1,0:T(8,128)(2,1)S(1)} %get-tuple-element.84.refs_3_), channel_id=1, source_target_pairs={{0,8},{1,9},{2,10},{3,11},{4,12},{5,13},{6,14},{7,15},{8,0},{9,1},... | collective-permute-start | bytes 786440 | tf_op jit(solution)/shard_map/out3_z2/ppermute | solution.py:359
  176.9 4.8 %collective-permute-done.28.refs_1_ = bf16[4,2,32,512]{3,2,1,0:T(8,128)(2,1)S(1)} collective-permute-done((bf16[4,2,32,512]{3,2,1,0:T(8,128)(2,1)S(1)}, bf16[4,2,32,512]{3,2,1,0:T(8,128)(2,1)S(1)}, u32[]{:S(2)}, u32[]{:S(2)}) %collective-permute-start.28) | collective-permute-done | bytes 262176 | tf_op jit(solution)/shard_map/out3_z1/ppermute | solution.py:359
  182.7 3.6 %collective-permute-done.31.refs_0_ = bf16[4,2,32,512]{3,2,1,0:T(8,128)(2,1)S(1)} collective-permute-done((bf16[4,2,32,512]{3,2,1,0:T(8,128)(2,1)S(1)}, bf16[4,2,32,512]{3,2,1,0:T(8,128)(2,1)S(1)}, u32[]{:S(2)}, u32[]{:S(2)}) %collective-permute-start.31) | collective-permute-done | bytes 262176 | tf_op jit(solution)/shard_map/out3_z2/ppermute | solution.py:359
  (85 shorter events, 27.5 us)
Async XLA Ops:
  1.3 17.8 %collective-permute-start = (bf16[4,2,32,512]{3,2,1,0:T(8,128)(2,1)S(1)}, bf16[4,2,32,512]{3,2,1,0:T(8,128)(2,1)S(1)}, u32[]{:S(2)}, u32[]{:S(2)}) collective-permute-start(bf16[4,2,32,512]{3,2,1,0:T(8,128)(2,1)S(1)} %first.1.refs_0_), channel_id=1, source_target_pairs={{0,8},{1,9},{2,10},{3,11},{4,12},{5,13},{6,14},{7,15},{8,0},{9,1},... | collective-permute-start | bytes 786440 | tf_op jit(solution)/shard_map/in0_z2/ppermute | solution.py:359
  6.0 31.9 %collective-permute-start.2 = (bf16[4,2,32,512]{3,2,1,0:T(8,128)(2,1)S(1)}, bf16[4,2,32,512]{3,2,1,0:T(8,128)(2,1)S(1)}, u32[]{:S(2)}, u32[]{:S(2)}) collective-permute-start(bf16[4,2,32,512]{3,2,1,0:T(8,128)(2,1)S(1)} %get-tuple-element.48), channel_id=1, source_target_pairs={{0,4},{1,5},{2,6},{3,7},{4,0},{5,1},{6,2},{7,3},{8,12},{9,13},{10,... | collective-permute-start | bytes 786440 | tf_op jit(solution)/shard_map/in0_z1/ppermute | solution.py:359
  7.7 17.1 %collective-permute-start.1 = (bf16[4,2,32,512]{3,2,1,0:T(8,128)(2,1)S(1)}, bf16[4,2,32,512]{3,2,1,0:T(8,128)(2,1)S(1)}, u32[]{:S(2)}, u32[]{:S(2)}) collective-permute-start(bf16[4,2,32,512]{3,2,1,0:T(8,128)(2,1)S(1)} %get-tuple-element.45.refs_0_), channel_id=1, source_target_pairs={{0,12},{1,13},{2,14},{3,15},{4,8},{5,9},{6,10},{7,11},{8,4},{9,5},... | collective-permute-start | bytes 786440 | tf_op jit(solution)/shard_map/in0_z3/ppermute | solution.py:359
  21.6 18.7 %collective-permute-start.4 = (bf16[4,2,32,512]{3,2,1,0:T(8,128)(2,1)S(1)}, bf16[4,2,32,512]{3,2,1,0:T(8,128)(2,1)S(1)}, u32[]{:S(2)}, u32[]{:S(2)}) collective-permute-start(bf16[4,2,32,512]{3,2,1,0:T(8,128)(2,1)S(1)} %relayout.8.refs_0_), channel_id=1, source_target_pairs={{0,12},{1,13},{2,14},{3,15},{4,8},{5,9},{6,10},{7,11},{8,4},{9,5},... | collective-permute-start | bytes 786440 | tf_op jit(solution)/shard_map/in1_z3/ppermute | solution.py:359
  25.4 32.3 %collective-permute-start.5 = (bf16[4,2,32,512]{3,2,1,0:T(8,128)(2,1)S(1)}, bf16[4,2,32,512]{3,2,1,0:T(8,128)(2,1)S(1)}, u32[]{:S(2)}, u32[]{:S(2)}) collective-permute-start(bf16[4,2,32,512]{3,2,1,0:T(8,128)(2,1)S(1)} %get-tuple-element.46.refs_0_), channel_id=1, source_target_pairs={{0,8},{1,9},{2,10},{3,11},{4,12},{5,13},{6,14},{7,15},{8,0},{9,1},... | collective-permute-start | bytes 786440 | tf_op jit(solution)/shard_map/in1_z2/ppermute | solution.py:359
  37.9 25.9 %collective-permute-start.7 = (bf16[4,2,32,512]{3,2,1,0:T(8,128)(2,1)S(1)}, bf16[4,2,32,512]{3,2,1,0:T(8,128)(2,1)S(1)}, u32[]{:S(2)}, u32[]{:S(2)}) collective-permute-start(bf16[4,2,32,512]{3,2,1,0:T(8,128)(2,1)S(1)} %get-tuple-element.51), channel_id=1, source_target_pairs={{0,4},{1,5},{2,6},{3,7},{4,0},{5,1},{6,2},{7,3},{8,12},{9,13},{10,... | collective-permute-start | bytes 786440 | tf_op jit(solution)/shard_map/in1_z1/ppermute | solution.py:359
  38.8 24.7 %collective-permute-start.3 = (bf16[4,4,2,32,512]{4,3,2,1,0:T(8,128)(2,1)S(1)}, bf16[4,4,2,32,512]{4,3,2,1,0:T(8,128)(2,1)S(1)}, u32[]{:S(2)}, u32[]{:S(2)}) collective-permute-start(bf16[4,4,2,32,512]{4,3,2,1,0:T(8,128)(2,1)S(1)} %join.8.refs_0_), channel_id=1, source_target_pairs={{0,2},{1,3},{2,0},{3,1},{4,6},{5,7},{6,4},{7,5},{8,10},{9,11},{10,... | collective-permute-start | bytes 3145736 | tf_op jit(solution)/shard_map/in0_y/ppermute | solution.py:359
  40.7 24.8 %collective-permute-start.8 = (bf16[4,2,32,512]{3,2,1,0:T(8,128)(2,1)S(1)}, bf16[4,2,32,512]{3,2,1,0:T(8,128)(2,1)S(1)}, u32[]{:S(2)}, u32[]{:S(2)}) collective-permute-start(bf16[4,2,32,512]{3,2,1,0:T(8,128)(2,1)S(1)} %relayout.10.refs_0_), channel_id=1, source_target_pairs={{0,12},{1,13},{2,14},{3,15},{4,8},{5,9},{6,10},{7,11},{8,4},{9,5},... | collective-permute-start | bytes 786440 | tf_op jit(solution)/shard_map/in2_z3/ppermute | solution.py:359
  58.2 31.5 %collective-permute-start.13 = (bf16[4,2,32,512]{3,2,1,0:T(8,128)(2,1)S(1)}, bf16[4,2,32,512]{3,2,1,0:T(8,128)(2,1)S(1)}, u32[]{:S(2)}, u32[]{:S(2)}) collective-permute-start(bf16[4,2,32,512]{3,2,1,0:T(8,128)(2,1)S(1)} %get-tuple-element.57), channel_id=1, source_target_pairs={{0,4},{1,5},{2,6},{3,7},{4,0},{5,1},{6,2},{7,3},{8,12},{9,13},{10,... | collective-permute-start | bytes 786440 | tf_op jit(solution)/shard_map/in2_z1/ppermute | solution.py:359
  58.3 21.5 %collective-permute-start.9 = (bf16[4,2,32,512]{3,2,1,0:T(8,128)(2,1)S(1)}, bf16[4,2,32,512]{3,2,1,0:T(8,128)(2,1)S(1)}, u32[]{:S(2)}, u32[]{:S(2)}) collective-permute-start(bf16[4,2,32,512]{3,2,1,0:T(8,128)(2,1)S(1)} %get-tuple-element.49.refs_2_), channel_id=1, source_target_pairs={{0,8},{1,9},{2,10},{3,11},{4,12},{5,13},{6,14},{7,15},{8,0},{9,1},... | collective-permute-start | bytes 786440 | tf_op jit(solution)/shard_map/in2_z2/ppermute | solution.py:359
  63.7 4.2 %collective-permute-start.6 = (bf16[2,4,4,2,32,512]{5,4,3,2,1,0:T(8,128)(2,1)S(1)}, bf16[2,4,4,2,32,512]{5,4,3,2,1,0:T(8,128)(2,1)S(1)}, u32[]{:S(2)}, u32[]{:S(2)}) collective-permute-start(bf16[2,4,4,2,32,512]{5,4,3,2,1,0:T(8,128)(2,1)S(1)} %join.9.refs_4_), channel_id=1, source_target_pairs={{0,1},{1,0},{2,3},{3,2},{4,5},{5,4},{6,7},{7,6},{8,9},{9,8},{10,11... | collective-permute-start | bytes 6291464 | tf_op jit(solution)/shard_map/in0_core/ppermute | solution.py:359
  63.9 25.6 %collective-permute-start.14 = (bf16[4,4,2,32,512]{4,3,2,1,0:T(8,128)(2,1)S(1)}, bf16[4,4,2,32,512]{4,3,2,1,0:T(8,128)(2,1)S(1)}, u32[]{:S(2)}, u32[]{:S(2)}) collective-permute-start(bf16[4,4,2,32,512]{4,3,2,1,0:T(8,128)(2,1)S(1)} %join.10.refs_0_), channel_id=1, source_target_pairs={{0,2},{1,3},{2,0},{3,1},{4,6},{5,7},{6,4},{7,5},{8,10},{9,11},{10,... | collective-permute-start | bytes 3145736 | tf_op jit(solution)/shard_map/in1_y/ppermute | solution.py:359
  65.8 25.6 %collective-permute-start.12 = (bf16[4,2,32,512]{3,2,1,0:T(8,128)(2,1)S(1)}, bf16[4,2,32,512]{3,2,1,0:T(8,128)(2,1)S(1)}, u32[]{:S(2)}, u32[]{:S(2)}) collective-permute-start(bf16[4,2,32,512]{3,2,1,0:T(8,128)(2,1)S(1)} %relayout.12.refs_3_), channel_id=1, source_target_pairs={{0,12},{1,13},{2,14},{3,15},{4,8},{5,9},{6,10},{7,11},{8,4},{9,5},... | collective-permute-start | bytes 786440 | tf_op jit(solution)/shard_map/in3_z3/ppermute | solution.py:359
  80.4 35.2 %collective-permute-start.10 = (bf16[4,2,32,512]{3,2,1,0:T(8,128)(2,1)S(1)}, bf16[4,2,32,512]{3,2,1,0:T(8,128)(2,1)S(1)}, u32[]{:S(2)}, u32[]{:S(2)}) collective-permute-start(bf16[4,2,32,512]{3,2,1,0:T(8,128)(2,1)S(1)} %get-tuple-element.54), channel_id=1, source_target_pairs={{0,4},{1,5},{2,6},{3,7},{4,0},{5,1},{6,2},{7,3},{8,12},{9,13},{10,... | collective-permute-start | bytes 786440 | tf_op jit(solution)/shard_map/in3_z1/ppermute | solution.py:359
  80.7 21.6 %collective-permute-start.11 = (bf16[4,2,32,512]{3,2,1,0:T(8,128)(2,1)S(1)}, bf16[4,2,32,512]{3,2,1,0:T(8,128)(2,1)S(1)}, u32[]{:S(2)}, u32[]{:S(2)}) collective-permute-start(bf16[4,2,32,512]{3,2,1,0:T(8,128)(2,1)S(1)} %get-tuple-element.55.refs_2_), channel_id=1, source_target_pairs={{0,8},{1,9},{2,10},{3,11},{4,12},{5,13},{6,14},{7,15},{8,0},{9,1},... | collective-permute-start | bytes 786440 | tf_op jit(solution)/shard_map/in3_z2/ppermute | solution.py:359
  89.6 4.2 %collective-permute-start.16 = (bf16[2,4,4,2,32,512]{5,4,3,2,1,0:T(8,128)(2,1)S(1)}, bf16[2,4,4,2,32,512]{5,4,3,2,1,0:T(8,128)(2,1)S(1)}, u32[]{:S(2)}, u32[]{:S(2)}) collective-permute-start(bf16[2,4,4,2,32,512]{5,4,3,2,1,0:T(8,128)(2,1)S(1)} %join.11.refs_4_), channel_id=1, source_target_pairs={{0,1},{1,0},{2,3},{3,2},{4,5},{5,4},{6,7},{7,6},{8,9},{9,8},{10,11... | collective-permute-start | bytes 6291464 | tf_op jit(solution)/shard_map/in1_core/ppermute | solution.py:359
  89.8 25.6 %collective-permute-start.15 = (bf16[4,4,2,32,512]{4,3,2,1,0:T(8,128)(2,1)S(1)}, bf16[4,4,2,32,512]{4,3,2,1,0:T(8,128)(2,1)S(1)}, u32[]{:S(2)}, u32[]{:S(2)}) collective-permute-start(bf16[4,4,2,32,512]{4,3,2,1,0:T(8,128)(2,1)S(1)} %join.12.refs_1_.refs_0_), channel_id=1, source_target_pairs={{0,2},{1,3},{2,0},{3,1},{4,6},{5,7},{6,4},{7,5},{8,10},{9,11},{10,... | collective-permute-start | bytes 3145736 | tf_op jit(solution)/shard_map/in2_y/ppermute | solution.py:359
  91.4 14.7 %collective-permute-start.17 = (bf16[4,2,32,512]{3,2,1,0:T(8,128)(2,1)S(1)}, bf16[4,2,32,512]{3,2,1,0:T(8,128)(2,1)S(1)}, u32[]{:S(2)}, u32[]{:S(2)}) collective-permute-start(bf16[4,2,32,512]{3,2,1,0:T(8,128)(2,1)S(1)} %release.8.refs_3_), channel_id=1, source_target_pairs={{0,12},{1,13},{2,14},{3,15},{4,8},{5,9},{6,10},{7,11},{8,4},{9,5},... | collective-permute-start | bytes 786440 | tf_op jit(solution)/shard_map/out0_z3/ppermute | solution.py:359
  102.4 30.2 %collective-permute-start.21 = (bf16[4,2,32,512]{3,2,1,0:T(8,128)(2,1)S(1)}, bf16[4,2,32,512]{3,2,1,0:T(8,128)(2,1)S(1)}, u32[]{:S(2)}, u32[]{:S(2)}) collective-permute-start(bf16[4,2,32,512]{3,2,1,0:T(8,128)(2,1)S(1)} %get-tuple-element.69), channel_id=1, source_target_pairs={{0,4},{1,5},{2,6},{3,7},{4,0},{5,1},{6,2},{7,3},{8,12},{9,13},{10,... | collective-permute-start | bytes 786440 | tf_op jit(solution)/shard_map/out0_z1/ppermute | solution.py:359
  102.7 22.1 %collective-permute-start.20 = (bf16[4,2,32,512]{3,2,1,0:T(8,128)(2,1)S(1)}, bf16[4,2,32,512]{3,2,1,0:T(8,128)(2,1)S(1)}, u32[]{:S(2)}, u32[]{:S(2)}) collective-permute-start(bf16[4,2,32,512]{3,2,1,0:T(8,128)(2,1)S(1)} %get-tuple-element.63.refs_1_), channel_id=1, source_target_pairs={{0,8},{1,9},{2,10},{3,11},{4,12},{5,13},{6,14},{7,15},{8,0},{9,1},... | collective-permute-start | bytes 786440 | tf_op jit(solution)/shard_map/out0_z2/ppermute | solution.py:359
  106.1 27.4 %collective-permute-start.22 = (bf16[4,2,32,512]{3,2,1,0:T(8,128)(2,1)S(1)}, bf16[4,2,32,512]{3,2,1,0:T(8,128)(2,1)S(1)}, u32[]{:S(2)}, u32[]{:S(2)}) collective-permute-start(bf16[4,2,32,512]{3,2,1,0:T(8,128)(2,1)S(1)} %release.10.refs_2_), channel_id=1, source_target_pairs={{0,12},{1,13},{2,14},{3,15},{4,8},{5,9},{6,10},{7,11},{8,4},{9,5},... | collective-permute-start | bytes 786440 | tf_op jit(solution)/shard_map/out1_z3/ppermute | solution.py:359
  115.5 9.7 %collective-permute-start.19 = (bf16[2,4,4,2,32,512]{5,4,3,2,1,0:T(8,128)(2,1)S(1)}, bf16[2,4,4,2,32,512]{5,4,3,2,1,0:T(8,128)(2,1)S(1)}, u32[]{:S(2)}, u32[]{:S(2)}) collective-permute-start(bf16[2,4,4,2,32,512]{5,4,3,2,1,0:T(8,128)(2,1)S(1)} %join.13.refs_4_), channel_id=1, source_target_pairs={{0,1},{1,0},{2,3},{3,2},{4,5},{5,4},{6,7},{7,6},{8,9},{9,8},{10,11... | collective-permute-start | bytes 6291464 | tf_op jit(solution)/shard_map/in2_core/ppermute | solution.py:359
  115.7 25.8 %collective-permute-start.18 = (bf16[4,4,2,32,512]{4,3,2,1,0:T(8,128)(2,1)S(1)}, bf16[4,4,2,32,512]{4,3,2,1,0:T(8,128)(2,1)S(1)}, u32[]{:S(2)}, u32[]{:S(2)}) collective-permute-start(bf16[4,4,2,32,512]{4,3,2,1,0:T(8,128)(2,1)S(1)} %join.14.refs_3_.refs_0_), channel_id=1, source_target_pairs={{0,2},{1,3},{2,0},{3,1},{4,6},{5,7},{6,4},{7,5},{8,10},{9,11},{10,... | collective-permute-start | bytes 3145736 | tf_op jit(solution)/shard_map/in3_y/ppermute | solution.py:359
  124.9 31.4 %collective-permute-start.25 = (bf16[4,2,32,512]{3,2,1,0:T(8,128)(2,1)S(1)}, bf16[4,2,32,512]{3,2,1,0:T(8,128)(2,1)S(1)}, u32[]{:S(2)}, u32[]{:S(2)}) collective-permute-start(bf16[4,2,32,512]{3,2,1,0:T(8,128)(2,1)S(1)} %get-tuple-element.79), channel_id=1, source_target_pairs={{0,4},{1,5},{2,6},{3,7},{4,0},{5,1},{6,2},{7,3},{8,12},{9,13},{10,... | collective-permute-start | bytes 786440 | tf_op jit(solution)/shard_map/out1_z1/ppermute | solution.py:359
  125.2 22.2 %collective-permute-start.24 = (bf16[4,2,32,512]{3,2,1,0:T(8,128)(2,1)S(1)}, bf16[4,2,32,512]{3,2,1,0:T(8,128)(2,1)S(1)}, u32[]{:S(2)}, u32[]{:S(2)}) collective-permute-start(bf16[4,2,32,512]{3,2,1,0:T(8,128)(2,1)S(1)} %get-tuple-element.66.refs_3_), channel_id=1, source_target_pairs={{0,8},{1,9},{2,10},{3,11},{4,12},{5,13},{6,14},{7,15},{8,0},{9,1},... | collective-permute-start | bytes 786440 | tf_op jit(solution)/shard_map/out1_z2/ppermute | solution.py:359
  133.6 23.7 %collective-permute-start.26 = (bf16[4,2,32,512]{3,2,1,0:T(8,128)(2,1)S(1)}, bf16[4,2,32,512]{3,2,1,0:T(8,128)(2,1)S(1)}, u32[]{:S(2)}, u32[]{:S(2)}) collective-permute-start(bf16[4,2,32,512]{3,2,1,0:T(8,128)(2,1)S(1)} %release.12.refs_2_), channel_id=1, source_target_pairs={{0,12},{1,13},{2,14},{3,15},{4,8},{5,9},{6,10},{7,11},{8,4},{9,5},... | collective-permute-start | bytes 786440 | tf_op jit(solution)/shard_map/out2_z3/ppermute | solution.py:359
  141.6 10.6 %collective-permute-start.23 = (bf16[2,4,4,2,32,512]{5,4,3,2,1,0:T(8,128)(2,1)S(1)}, bf16[2,4,4,2,32,512]{5,4,3,2,1,0:T(8,128)(2,1)S(1)}, u32[]{:S(2)}, u32[]{:S(2)}) collective-permute-start(bf16[2,4,4,2,32,512]{5,4,3,2,1,0:T(8,128)(2,1)S(1)} %join.15.refs_3_), channel_id=1, source_target_pairs={{0,1},{1,0},{2,3},{3,2},{4,5},{5,4},{6,7},{7,6},{8,9},{9,8},{10,11... | collective-permute-start | bytes 6291464 | tf_op jit(solution)/shard_map/in3_core/ppermute | solution.py:359
  147.4 26.1 %collective-permute-start.30 = (bf16[4,2,32,512]{3,2,1,0:T(8,128)(2,1)S(1)}, bf16[4,2,32,512]{3,2,1,0:T(8,128)(2,1)S(1)}, u32[]{:S(2)}, u32[]{:S(2)}) collective-permute-start(bf16[4,2,32,512]{3,2,1,0:T(8,128)(2,1)S(1)} %get-tuple-element.83), channel_id=1, source_target_pairs={{0,4},{1,5},{2,6},{3,7},{4,0},{5,1},{6,2},{7,3},{8,12},{9,13},{10,... | collective-permute-start | bytes 786440 | tf_op jit(solution)/shard_map/out2_z1/ppermute | solution.py:359
  147.7 22.2 %collective-permute-start.27 = (bf16[4,2,32,512]{3,2,1,0:T(8,128)(2,1)S(1)}, bf16[4,2,32,512]{3,2,1,0:T(8,128)(2,1)S(1)}, u32[]{:S(2)}, u32[]{:S(2)}) collective-permute-start(bf16[4,2,32,512]{3,2,1,0:T(8,128)(2,1)S(1)} %get-tuple-element.73.refs_3_), channel_id=1, source_target_pairs={{0,8},{1,9},{2,10},{3,11},{4,12},{5,13},{6,14},{7,15},{8,0},{9,1},... | collective-permute-start | bytes 786440 | tf_op jit(solution)/shard_map/out2_z2/ppermute | solution.py:359
  157.3 24.5 %collective-permute-start.29 = (bf16[4,2,32,512]{3,2,1,0:T(8,128)(2,1)S(1)}, bf16[4,2,32,512]{3,2,1,0:T(8,128)(2,1)S(1)}, u32[]{:S(2)}, u32[]{:S(2)}) collective-permute-start(bf16[4,2,32,512]{3,2,1,0:T(8,128)(2,1)S(1)} %release.14.refs_3_), channel_id=1, source_target_pairs={{0,12},{1,13},{2,14},{3,15},{4,8},{5,9},{6,10},{7,11},{8,4},{9,5},... | collective-permute-start | bytes 786440 | tf_op jit(solution)/shard_map/out3_z3/ppermute | solution.py:359
  169.9 11.8 %collective-permute-start.28 = (bf16[4,2,32,512]{3,2,1,0:T(8,128)(2,1)S(1)}, bf16[4,2,32,512]{3,2,1,0:T(8,128)(2,1)S(1)}, u32[]{:S(2)}, u32[]{:S(2)}) collective-permute-start(bf16[4,2,32,512]{3,2,1,0:T(8,128)(2,1)S(1)} %get-tuple-element.81), channel_id=1, source_target_pairs={{0,4},{1,5},{2,6},{3,7},{4,0},{5,1},{6,2},{7,3},{8,12},{9,13},{10,... | collective-permute-start | bytes 786440 | tf_op jit(solution)/shard_map/out3_z1/ppermute | solution.py:359
  170.1 16.1 %collective-permute-start.31 = (bf16[4,2,32,512]{3,2,1,0:T(8,128)(2,1)S(1)}, bf16[4,2,32,512]{3,2,1,0:T(8,128)(2,1)S(1)}, u32[]{:S(2)}, u32[]{:S(2)}) collective-permute-start(bf16[4,2,32,512]{3,2,1,0:T(8,128)(2,1)S(1)} %get-tuple-element.84.refs_3_), channel_id=1, source_target_pairs={{0,8},{1,9},{2,10},{3,11},{4,12},{5,13},{6,14},{7,15},{8,0},{9,1},... | collective-permute-start | bytes 786440 | tf_op jit(solution)/shard_map/out3_z2/ppermute | solution.py:359
  (7 other events, 30.4 us)

commit v8 on v6

--- a/solution.py
+++ b/solution.py
@@ -372,13 +372,16 @@
     leaving = [{} for _ in range(chunks)]
     result, merge = [None], []
 
-    def parts(at):
-        return [cross[at]] + (([0] + rest) if at == len(cross) - 1 else [])
+    def crossing(k):
+        return cross[::-1] if k % 2 == 0 else cross
+
+    def parts(at, over=cross):
+        return [over[at]] + (([0] + rest) if at == len(over) - 1 else [])
 
     def go_in(k, at):
         if k >= chunks:
             return
-        wanted = parts(at)
+        wanted = parts(at, cross)
         with jax.named_scope(f"in{k}_{at}"):
             own, at_chunk = spectra, k
             if k == 0 and at == 0:
@@ -391,7 +394,7 @@
     def go_out(k, at):
         if not 0 <= k < chunks:
             return
-        wanted = parts(at)
+        wanted = parts(at, crossing(k))
         with jax.named_scope(f"out{k}_{at}"):
             blocks = release([made[k][j] for j in wanted], order())
         last.append(blocks[0])
@@ -428,7 +431,7 @@
     def begin_finish(k):
         if not 0 <= k < chunks:
             return
-        blocks = {j: leaving[k][j] for j in range(planes) if j != cross[-1]}
+        blocks = {j: leaving[k][j] for j in range(planes) if j != crossing(k)[-1]}
         with jax.named_scope(f"chunk{k}"):
             begun[k] = early(
                 merge[0], blocks, last[-1:], PACE if k == chunks - 2 else COST
@@ -438,7 +441,7 @@
     def finish(k):
         if not 0 <= k < chunks:
             return
-        blocks = {cross[-1]: leaving[k][cross[-1]]}
+        blocks = {crossing(k)[-1]: leaving[k][crossing(k)[-1]]}
         with jax.named_scope(f"chunk{k}"):
             result[0] = assemble(merge[0], begun[k], blocks, result[0], k, n, bins, [])
 

time: 188 us -> 188 us (level)
  starting transfers between devices: 49.8 us -> 63.7 us
  waiting for transfers between devices: 103 us -> 89.4 us
    ppermute x32, starting transfers between devices: 49.8 us -> 63.7 us  [send(): return lax.ppermute(block, 'shot', [(d, d ^ offset) for d in range(n)])]
    ppermute x32, waiting for transfers between devices: 103 us -> 89.4 us  [send(): return lax.ppermute(block, 'shot', [(d, d ^ offset) for d in range(n)])]
  transfers between devices with their start and end apart: 32 -> 32, of which waited for: 16 -> 17; matrix products, arithmetic and copies ran while one was open for 0% -> 0% of each run, Pallas kernels for 15% -> 15%
where the time goes in v8:
time: 188 us
  waiting for transfers between devices  89.4 us (48%)
  starting transfers between devices  63.7 us (34%)
  Pallas kernels  29.6 us (16%)
  local copies, waits for them, and re-layouts  4.22 us (2%)
    ppermute x32, waiting for transfers between devices, send(): return lax.ppermute(block, 'shot', [(d, d ^ offset) for d in range(n)])  89.4 us
    ppermute x32, starting transfers between devices, send(): return lax.ppermute(block, 'shot', [(d, d ^ offset) for d in range(n)])  63.7 us
    pallas_call x4, Pallas kernels, product(): pl.pallas_call(functools.partial(product_kernel, k, n, planes), out_shape...  16 us
    pallas_call x4, Pallas kernels, assemble(): pl.pallas_call(functools.partial(assemble_kernel, n, shots, k, list(block...  5.07 us
    pallas_call x4, Pallas kernels, early(): pl.pallas_call(functools.partial(early_kernel, list(blocks)), out_shape=j...  3.82 us
  transfers between devices with their start and end apart: 32, of which 17 were waited for; matrix products, arithmetic and copies ran while one was open for 0% of the time, Pallas kernels for 15%

profile of v8, /device:TPU:0, one launch (start us, length us, event | category | flops | bytes accessed | tf_op | source)
XLA Modules:
  0.0 187.6 jit_solution(10534629472765149580)
XLA Ops:
  1.3 5.1 %collective-permute-start = (bf16[4,2,32,512]{3,2,1,0:T(8,128)(2,1)S(1)}, bf16[4,2,32,512]{3,2,1,0:T(8,128)(2,1)S(1)}, u32[]{:S(2)}, u32[]{:S(2)}) collective-permute-start(bf16[4,2,32,512]{3,2,1,0:T(8,128)(2,1)S(1)} %first.1.refs_0_), channel_id=1, source_target_pairs={{0,12},{1,13},{2,14},{3,15},{4,8},{5,9},{6,10},{7,11},{8,4},{9,5},... | collective-permute-start | bytes 786440 | tf_op jit(solution)/shard_map/in0_z3/ppermute | solution.py:345
  7.1 2.4 %collective-permute-start.1 = (bf16[4,2,32,512]{3,2,1,0:T(8,128)(2,1)S(1)}, bf16[4,2,32,512]{3,2,1,0:T(8,128)(2,1)S(1)}, u32[]{:S(2)}, u32[]{:S(2)}) collective-permute-start(bf16[4,2,32,512]{3,2,1,0:T(8,128)(2,1)S(1)} %get-tuple-element.45.refs_0_), channel_id=1, source_target_pairs={{0,8},{1,9},{2,10},{3,11},{4,12},{5,13},{6,14},{7,15},{8,0},{9,1},... | collective-permute-start | bytes 786440 | tf_op jit(solution)/shard_map/in0_z2/ppermute | solution.py:345
  9.7 4.0 %collective-permute-done.refs_1_.refs_3_ = bf16[4,2,32,512]{3,2,1,0:T(8,128)(2,1)S(1)} collective-permute-done((bf16[4,2,32,512]{3,2,1,0:T(8,128)(2,1)S(1)}, bf16[4,2,32,512]{3,2,1,0:T(8,128)(2,1)S(1)}, u32[]{:S(2)}, u32[]{:S(2)}) %collective-permute-start) | collective-permute-done | bytes 262176 | tf_op jit(solution)/shard_map/in0_z3/ppermute | solution.py:345
  13.7 2.2 %copy-done.3 = bf16[32,2,64,512]{3,2,1,0:T(8,128)(2,1)S(1)} copy-done((bf16[32,2,64,512]{3,2,1,0:T(8,128)(2,1)S(1)}, bf16[32,2,64,512]{3,2,1,0:T(8,128)(2,1)}, u32[]{:S(2)}) %copy-start.3) | copy-done | bytes 4194328
  16.2 3.9 %collective-permute-start.4 = (bf16[4,2,32,512]{3,2,1,0:T(8,128)(2,1)S(1)}, bf16[4,2,32,512]{3,2,1,0:T(8,128)(2,1)S(1)}, u32[]{:S(2)}, u32[]{:S(2)}) collective-permute-start(bf16[4,2,32,512]{3,2,1,0:T(8,128)(2,1)S(1)} %relayout.8.refs_0_), channel_id=1, source_target_pairs={{0,12},{1,13},{2,14},{3,15},{4,8},{5,9},{6,10},{7,11},{8,4},{9,5},... | collective-permute-start | bytes 786440 | tf_op jit(solution)/shard_map/in1_z3/ppermute | solution.py:345
  20.1 15.3 %collective-permute-done.1.refs_1_.refs_2_ = bf16[4,2,32,512]{3,2,1,0:T(8,128)(2,1)S(1)} collective-permute-done((bf16[4,2,32,512]{3,2,1,0:T(8,128)(2,1)S(1)}, bf16[4,2,32,512]{3,2,1,0:T(8,128)(2,1)S(1)}, u32[]{:S(2)}, u32[]{:S(2)}) %collective-permute-start.1) | collective-permute-done | bytes 262176 | tf_op jit(solution)/shard_map/in0_z2/ppermute | solution.py:345
  36.2 3.3 %collective-permute-start.7 = (bf16[4,2,32,512]{3,2,1,0:T(8,128)(2,1)S(1)}, bf16[4,2,32,512]{3,2,1,0:T(8,128)(2,1)S(1)}, u32[]{:S(2)}, u32[]{:S(2)}) collective-permute-start(bf16[4,2,32,512]{3,2,1,0:T(8,128)(2,1)S(1)} %get-tuple-element.51), channel_id=1, source_target_pairs={{0,4},{1,5},{2,6},{3,7},{4,0},{5,1},{6,2},{7,3},{8,12},{9,13},{10,... | collective-permute-start | bytes 786440 | tf_op jit(solution)/shard_map/in1_z1/ppermute | solution.py:345
  43.4 14.4 %collective-permute-done.5.refs_1_.refs_2_ = bf16[4,2,32,512]{3,2,1,0:T(8,128)(2,1)S(1)} collective-permute-done((bf16[4,2,32,512]{3,2,1,0:T(8,128)(2,1)S(1)}, bf16[4,2,32,512]{3,2,1,0:T(8,128)(2,1)S(1)}, u32[]{:S(2)}, u32[]{:S(2)}) %collective-permute-start.5) | collective-permute-done | bytes 262176 | tf_op jit(solution)/shard_map/in1_z2/ppermute | solution.py:345
  58.5 3.2 %collective-permute-start.9 = (bf16[4,2,32,512]{3,2,1,0:T(8,128)(2,1)S(1)}, bf16[4,2,32,512]{3,2,1,0:T(8,128)(2,1)S(1)}, u32[]{:S(2)}, u32[]{:S(2)}) collective-permute-start(bf16[4,2,32,512]{3,2,1,0:T(8,128)(2,1)S(1)} %get-tuple-element.49.refs_2_), channel_id=1, source_target_pairs={{0,8},{1,9},{2,10},{3,11},{4,12},{5,13},{6,14},{7,15},{8,0},{9,1},... | collective-permute-start | bytes 786440 | tf_op jit(solution)/shard_map/in2_z2/ppermute | solution.py:345
  67.1 4.0 %product.4 = (bf16[4,2,32,512]{3,2,1,0:T(8,128)(2,1)S(1)}, bf16[4,2,32,512]{3,2,1,0:T(8,128)(2,1)S(1)}, bf16[4,2,32,512]{3,2,1,0:T(8,128)(2,1)S(1)}, bf16[4,2,32,512]{3,2,1,0:T(8,128)(2,1)S(1)}) custom-call(s32[1]{0:T(128)} %bitcast.me_ref, f32[2,64]{1,0:T(2,128)S(1)} %copy-done.6, s32[1,512]{1,0:T(1,128)S(1)} %bitcast.4, s32[512,1]{1,0:T(8,128)S(1)} %copy.10.fold_col_ref, ...), custom_call_target="tpu_custom_call" | custom-call | tf_op jit(solution)/shard_map/chunk0/product/pallas_call | solution.py:331
  71.1 9.2 %collective-permute-done.9.refs_1_.refs_2_ = bf16[4,2,32,512]{3,2,1,0:T(8,128)(2,1)S(1)} collective-permute-done((bf16[4,2,32,512]{3,2,1,0:T(8,128)(2,1)S(1)}, bf16[4,2,32,512]{3,2,1,0:T(8,128)(2,1)S(1)}, u32[]{:S(2)}, u32[]{:S(2)}) %collective-permute-start.9) | collective-permute-done | bytes 262176 | tf_op jit(solution)/shard_map/in2_z2/ppermute | solution.py:345
  80.9 3.2 %collective-permute-start.11 = (bf16[4,2,32,512]{3,2,1,0:T(8,128)(2,1)S(1)}, bf16[4,2,32,512]{3,2,1,0:T(8,128)(2,1)S(1)}, u32[]{:S(2)}, u32[]{:S(2)}) collective-permute-start(bf16[4,2,32,512]{3,2,1,0:T(8,128)(2,1)S(1)} %get-tuple-element.55.refs_2_), channel_id=1, source_target_pairs={{0,8},{1,9},{2,10},{3,11},{4,12},{5,13},{6,14},{7,15},{8,0},{9,1},... | collective-permute-start | bytes 786440 | tf_op jit(solution)/shard_map/in3_z2/ppermute | solution.py:345
  84.2 4.5 %collective-permute-done.14.refs_1_ = bf16[4,4,2,32,512]{4,3,2,1,0:T(8,128)(2,1)S(1)} collective-permute-done((bf16[4,4,2,32,512]{4,3,2,1,0:T(8,128)(2,1)S(1)}, bf16[4,4,2,32,512]{4,3,2,1,0:T(8,128)(2,1)S(1)}, u32[]{:S(2)}, u32[]{:S(2)}) %collective-permute-start.14) | collective-permute-done | bytes 1048608 | tf_op jit(solution)/shard_map/in1_y/ppermute | solution.py:345
  91.0 2.0 %collective-permute-done.16.refs_2_ = bf16[2,4,4,2,32,512]{5,4,3,2,1,0:T(8,128)(2,1)S(1)} collective-permute-done((bf16[2,4,4,2,32,512]{5,4,3,2,1,0:T(8,128)(2,1)S(1)}, bf16[2,4,4,2,32,512]{5,4,3,2,1,0:T(8,128)(2,1)S(1)}, u32[]{:S(2)}, u32[]{:S(2)}) %collective-permute-start.16) | collective-permute-done | bytes 2097184 | tf_op jit(solution)/shard_map/in1_core/ppermute | solution.py:345
  93.0 4.0 %product.5 = (bf16[4,2,32,512]{3,2,1,0:T(8,128)(2,1)S(1)}, bf16[4,2,32,512]{3,2,1,0:T(8,128)(2,1)S(1)}, bf16[4,2,32,512]{3,2,1,0:T(8,128)(2,1)S(1)}, bf16[4,2,32,512]{3,2,1,0:T(8,128)(2,1)S(1)}) custom-call(s32[1]{0:T(128)} %bitcast.me_ref, f32[2,64]{1,0:T(2,128)S(1)} %copy-done.6, s32[1,512]{1,0:T(1,128)S(1)} %bitcast.5, s32[512,1]{1,0:T(8,128)S(1)} %copy.10.fold_col_ref, ...), custom_call_target="tpu_custom_call" | custom-call | tf_op jit(solution)/shard_map/chunk1/product/pallas_call | solution.py:331
  97.0 5.8 %collective-permute-done.11.refs_4_.refs_2_ = bf16[4,2,32,512]{3,2,1,0:T(8,128)(2,1)S(1)} collective-permute-done((bf16[4,2,32,512]{3,2,1,0:T(8,128)(2,1)S(1)}, bf16[4,2,32,512]{3,2,1,0:T(8,128)(2,1)S(1)}, u32[]{:S(2)}, u32[]{:S(2)}) %collective-permute-start.11) | collective-permute-done | bytes 262176 | tf_op jit(solution)/shard_map/in3_z2/ppermute | solution.py:345
  102.9 2.7 %collective-permute-start.20 = (bf16[4,2,32,512]{3,2,1,0:T(8,128)(2,1)S(1)}, bf16[4,2,32,512]{3,2,1,0:T(8,128)(2,1)S(1)}, u32[]{:S(2)}, u32[]{:S(2)}) collective-permute-start(bf16[4,2,32,512]{3,2,1,0:T(8,128)(2,1)S(1)} %get-tuple-element.63.refs_1_), channel_id=1, source_target_pairs={{0,12},{1,13},{2,14},{3,15},{4,8},{5,9},{6,10},{7,11},{8,4},{9,5},... | collective-permute-start | bytes 786440 | tf_op jit(solution)/shard_map/out0_z3/ppermute | solution.py:345
  105.6 4.3 %collective-permute-done.17.refs_2_ = bf16[4,2,32,512]{3,2,1,0:T(8,128)(2,1)S(1)} collective-permute-done((bf16[4,2,32,512]{3,2,1,0:T(8,128)(2,1)S(1)}, bf16[4,2,32,512]{3,2,1,0:T(8,128)(2,1)S(1)}, u32[]{:S(2)}, u32[]{:S(2)}) %collective-permute-start.17) | collective-permute-done | bytes 262176 | tf_op jit(solution)/shard_map/out0_z2/ppermute | solution.py:345
  110.0 3.5 %collective-permute-start.22 = (bf16[4,2,32,512]{3,2,1,0:T(8,128)(2,1)S(1)}, bf16[4,2,32,512]{3,2,1,0:T(8,128)(2,1)S(1)}, u32[]{:S(2)}, u32[]{:S(2)}) collective-permute-start(bf16[4,2,32,512]{3,2,1,0:T(8,128)(2,1)S(1)} %release.10.refs_2_), channel_id=1, source_target_pairs={{0,12},{1,13},{2,14},{3,15},{4,8},{5,9},{6,10},{7,11},{8,4},{9,5},... | collective-permute-start | bytes 786440 | tf_op jit(solution)/shard_map/out1_z3/ppermute | solution.py:345
  114.9 1.8 collective-permute-start.18
  116.6 1.7 collective-permute-done.20.refs_4_.refs_0_
  118.4 7.5 %collective-permute-start.25 = (bf16[4,2,32,512]{3,2,1,0:T(8,128)(2,1)S(1)}, bf16[4,2,32,512]{3,2,1,0:T(8,128)(2,1)S(1)}, u32[]{:S(2)}, u32[]{:S(2)}) collective-permute-start(bf16[4,2,32,512]{3,2,1,0:T(8,128)(2,1)S(1)} %get-tuple-element.79), channel_id=1, source_target_pairs={{0,4},{1,5},{2,6},{3,7},{4,0},{5,1},{6,2},{7,3},{8,12},{9,13},{10,... | collective-permute-start | bytes 786440 | tf_op jit(solution)/shard_map/out1_z1/ppermute | solution.py:345
  127.3 4.0 %product.6 = (bf16[4,2,32,512]{3,2,1,0:T(8,128)(2,1)S(1)}, bf16[4,2,32,512]{3,2,1,0:T(8,128)(2,1)S(1)}, bf16[4,2,32,512]{3,2,1,0:T(8,128)(2,1)S(1)}, bf16[4,2,32,512]{3,2,1,0:T(8,128)(2,1)S(1)}) custom-call(s32[1]{0:T(128)} %bitcast.me_ref, f32[2,64]{1,0:T(2,128)S(1)} %copy-done.6, s32[1,512]{1,0:T(1,128)S(1)} %bitcast.6, s32[512,1]{1,0:T(8,128)S(1)} %copy.10.fold_col_ref, ...), custom_call_target="tpu_custom_call" | custom-call | tf_op jit(solution)/shard_map/chunk2/product/pallas_call | solution.py:331
  132.3 2.7 %collective-permute-start.26 = (bf16[4,2,32,512]{3,2,1,0:T(8,128)(2,1)S(1)}, bf16[4,2,32,512]{3,2,1,0:T(8,128)(2,1)S(1)}, u32[]{:S(2)}, u32[]{:S(2)}) collective-permute-start(bf16[4,2,32,512]{3,2,1,0:T(8,128)(2,1)S(1)} %release.12.refs_2_), channel_id=1, source_target_pairs={{0,8},{1,9},{2,10},{3,11},{4,12},{5,13},{6,14},{7,15},{8,0},{9,1},... | collective-permute-start | bytes 786440 | tf_op jit(solution)/shard_map/out2_z2/ppermute | solution.py:345
  135.0 5.7 %collective-permute-done.18.refs_1_ = bf16[4,4,2,32,512]{4,3,2,1,0:T(8,128)(2,1)S(1)} collective-permute-done((bf16[4,4,2,32,512]{4,3,2,1,0:T(8,128)(2,1)S(1)}, bf16[4,4,2,32,512]{4,3,2,1,0:T(8,128)(2,1)S(1)}, u32[]{:S(2)}, u32[]{:S(2)}) %collective-permute-start.18) | collective-permute-done | bytes 1048608 | tf_op jit(solution)/shard_map/in3_y/ppermute | solution.py:345
  140.9 6.9 %collective-permute-done.24.refs_4_.refs_0_ = bf16[4,2,32,512]{3,2,1,0:T(8,128)(2,1)S(1)} collective-permute-done((bf16[4,2,32,512]{3,2,1,0:T(8,128)(2,1)S(1)}, bf16[4,2,32,512]{3,2,1,0:T(8,128)(2,1)S(1)}, u32[]{:S(2)}, u32[]{:S(2)}) %collective-permute-start.24) | collective-permute-done | bytes 262176 | tf_op jit(solution)/shard_map/out1_z2/ppermute | solution.py:345
  147.9 2.7 %collective-permute-start.27 = (bf16[4,2,32,512]{3,2,1,0:T(8,128)(2,1)S(1)}, bf16[4,2,32,512]{3,2,1,0:T(8,128)(2,1)S(1)}, u32[]{:S(2)}, u32[]{:S(2)}) collective-permute-start(bf16[4,2,32,512]{3,2,1,0:T(8,128)(2,1)S(1)} %get-tuple-element.73.refs_3_), channel_id=1, source_target_pairs={{0,12},{1,13},{2,14},{3,15},{4,8},{5,9},{6,10},{7,11},{8,4},{9,5},... | collective-permute-start | bytes 786440 | tf_op jit(solution)/shard_map/out2_z3/ppermute | solution.py:345
  151.9 4.0 %product.7 = (bf16[4,2,32,512]{3,2,1,0:T(8,128)(2,1)S(1)}, bf16[4,2,32,512]{3,2,1,0:T(8,128)(2,1)S(1)}, bf16[4,2,32,512]{3,2,1,0:T(8,128)(2,1)S(1)}, bf16[4,2,32,512]{3,2,1,0:T(8,128)(2,1)S(1)}) custom-call(s32[1]{0:T(128)} %bitcast.me_ref, f32[2,64]{1,0:T(2,128)S(1)} %copy-done.6, s32[1,512]{1,0:T(1,128)S(1)} %bitcast.7, s32[512,1]{1,0:T(8,128)S(1)} %copy.10.fold_col_ref, ...), custom_call_target="tpu_custom_call" | custom-call | tf_op jit(solution)/shard_map/chunk3/product/pallas_call | solution.py:331
  158.4 3.6 %collective-permute-done.27.refs_4_.refs_0_ = bf16[4,2,32,512]{3,2,1,0:T(8,128)(2,1)S(1)} collective-permute-done((bf16[4,2,32,512]{3,2,1,0:T(8,128)(2,1)S(1)}, bf16[4,2,32,512]{3,2,1,0:T(8,128)(2,1)S(1)}, u32[]{:S(2)}, u32[]{:S(2)}) %collective-permute-start.27) | collective-permute-done | bytes 262176 | tf_op jit(solution)/shard_map/out2_z3/ppermute | solution.py:345
  162.1 8.9 %collective-permute-start.28 = (bf16[4,2,32,512]{3,2,1,0:T(8,128)(2,1)S(1)}, bf16[4,2,32,512]{3,2,1,0:T(8,128)(2,1)S(1)}, u32[]{:S(2)}, u32[]{:S(2)}) collective-permute-start(bf16[4,2,32,512]{3,2,1,0:T(8,128)(2,1)S(1)} %get-tuple-element.81), channel_id=1, source_target_pairs={{0,4},{1,5},{2,6},{3,7},{4,0},{5,1},{6,2},{7,3},{8,12},{9,13},{10,... | collective-permute-start | bytes 786440 | tf_op jit(solution)/shard_map/out3_z1/ppermute | solution.py:345
  175.7 2.0 %collective-permute-done.28.refs_1_ = bf16[4,2,32,512]{3,2,1,0:T(8,128)(2,1)S(1)} collective-permute-done((bf16[4,2,32,512]{3,2,1,0:T(8,128)(2,1)S(1)}, bf16[4,2,32,512]{3,2,1,0:T(8,128)(2,1)S(1)}, u32[]{:S(2)}, u32[]{:S(2)}) %collective-permute-start.28) | collective-permute-done | bytes 262176 | tf_op jit(solution)/shard_map/out3_z1/ppermute | solution.py:345
  178.7 7.5 %collective-permute-done.31.refs_0_ = bf16[4,2,32,512]{3,2,1,0:T(8,128)(2,1)S(1)} collective-permute-done((bf16[4,2,32,512]{3,2,1,0:T(8,128)(2,1)S(1)}, bf16[4,2,32,512]{3,2,1,0:T(8,128)(2,1)S(1)}, u32[]{:S(2)}, u32[]{:S(2)}) %collective-permute-start.31) | collective-permute-done | bytes 262176 | tf_op jit(solution)/shard_map/out3_z2/ppermute | solution.py:345
  (85 shorter events, 31.1 us)
Async XLA Ops:
  1.3 12.3 %collective-permute-start = (bf16[4,2,32,512]{3,2,1,0:T(8,128)(2,1)S(1)}, bf16[4,2,32,512]{3,2,1,0:T(8,128)(2,1)S(1)}, u32[]{:S(2)}, u32[]{:S(2)}) collective-permute-start(bf16[4,2,32,512]{3,2,1,0:T(8,128)(2,1)S(1)} %first.1.refs_0_), channel_id=1, source_target_pairs={{0,12},{1,13},{2,14},{3,15},{4,8},{5,9},{6,10},{7,11},{8,4},{9,5},... | collective-permute-start | bytes 786440 | tf_op jit(solution)/shard_map/in0_z3/ppermute | solution.py:345
  7.0 32.5 %collective-permute-start.2 = (bf16[4,2,32,512]{3,2,1,0:T(8,128)(2,1)S(1)}, bf16[4,2,32,512]{3,2,1,0:T(8,128)(2,1)S(1)}, u32[]{:S(2)}, u32[]{:S(2)}) collective-permute-start(bf16[4,2,32,512]{3,2,1,0:T(8,128)(2,1)S(1)} %get-tuple-element.48), channel_id=1, source_target_pairs={{0,4},{1,5},{2,6},{3,7},{4,0},{5,1},{6,2},{7,3},{8,12},{9,13},{10,... | collective-permute-start | bytes 786440 | tf_op jit(solution)/shard_map/in0_z1/ppermute | solution.py:345
  7.1 28.2 %collective-permute-start.1 = (bf16[4,2,32,512]{3,2,1,0:T(8,128)(2,1)S(1)}, bf16[4,2,32,512]{3,2,1,0:T(8,128)(2,1)S(1)}, u32[]{:S(2)}, u32[]{:S(2)}) collective-permute-start(bf16[4,2,32,512]{3,2,1,0:T(8,128)(2,1)S(1)} %get-tuple-element.45.refs_0_), channel_id=1, source_target_pairs={{0,8},{1,9},{2,10},{3,11},{4,12},{5,13},{6,14},{7,15},{8,0},{9,1},... | collective-permute-start | bytes 786440 | tf_op jit(solution)/shard_map/in0_z2/ppermute | solution.py:345
  16.2 25.7 %collective-permute-start.4 = (bf16[4,2,32,512]{3,2,1,0:T(8,128)(2,1)S(1)}, bf16[4,2,32,512]{3,2,1,0:T(8,128)(2,1)S(1)}, u32[]{:S(2)}, u32[]{:S(2)}) collective-permute-start(bf16[4,2,32,512]{3,2,1,0:T(8,128)(2,1)S(1)} %relayout.8.refs_0_), channel_id=1, source_target_pairs={{0,12},{1,13},{2,14},{3,15},{4,8},{5,9},{6,10},{7,11},{8,4},{9,5},... | collective-permute-start | bytes 786440 | tf_op jit(solution)/shard_map/in1_z3/ppermute | solution.py:345
  35.9 21.9 %collective-permute-start.5 = (bf16[4,2,32,512]{3,2,1,0:T(8,128)(2,1)S(1)}, bf16[4,2,32,512]{3,2,1,0:T(8,128)(2,1)S(1)}, u32[]{:S(2)}, u32[]{:S(2)}) collective-permute-start(bf16[4,2,32,512]{3,2,1,0:T(8,128)(2,1)S(1)} %get-tuple-element.46.refs_0_), channel_id=1, source_target_pairs={{0,8},{1,9},{2,10},{3,11},{4,12},{5,13},{6,14},{7,15},{8,0},{9,1},... | collective-permute-start | bytes 786440 | tf_op jit(solution)/shard_map/in1_z2/ppermute | solution.py:345
  36.2 26.7 %collective-permute-start.7 = (bf16[4,2,32,512]{3,2,1,0:T(8,128)(2,1)S(1)}, bf16[4,2,32,512]{3,2,1,0:T(8,128)(2,1)S(1)}, u32[]{:S(2)}, u32[]{:S(2)}) collective-permute-start(bf16[4,2,32,512]{3,2,1,0:T(8,128)(2,1)S(1)} %get-tuple-element.51), channel_id=1, source_target_pairs={{0,4},{1,5},{2,6},{3,7},{4,0},{5,1},{6,2},{7,3},{8,12},{9,13},{10,... | collective-permute-start | bytes 786440 | tf_op jit(solution)/shard_map/in1_z1/ppermute | solution.py:345
  40.4 22.3 %collective-permute-start.3 = (bf16[4,4,2,32,512]{4,3,2,1,0:T(8,128)(2,1)S(1)}, bf16[4,4,2,32,512]{4,3,2,1,0:T(8,128)(2,1)S(1)}, u32[]{:S(2)}, u32[]{:S(2)}) collective-permute-start(bf16[4,4,2,32,512]{4,3,2,1,0:T(8,128)(2,1)S(1)} %join.8.refs_0_), channel_id=1, source_target_pairs={{0,2},{1,3},{2,0},{3,1},{4,6},{5,7},{6,4},{7,5},{8,10},{9,11},{10,... | collective-permute-start | bytes 3145736 | tf_op jit(solution)/shard_map/in0_y/ppermute | solution.py:345
  42.2 22.4 %collective-permute-start.8 = (bf16[4,2,32,512]{3,2,1,0:T(8,128)(2,1)S(1)}, bf16[4,2,32,512]{3,2,1,0:T(8,128)(2,1)S(1)}, u32[]{:S(2)}, u32[]{:S(2)}) collective-permute-start(bf16[4,2,32,512]{3,2,1,0:T(8,128)(2,1)S(1)} %relayout.10.refs_0_), channel_id=1, source_target_pairs={{0,12},{1,13},{2,14},{3,15},{4,8},{5,9},{6,10},{7,11},{8,4},{9,5},... | collective-permute-start | bytes 786440 | tf_op jit(solution)/shard_map/in2_z3/ppermute | solution.py:345
  58.4 30.5 %collective-permute-start.13 = (bf16[4,2,32,512]{3,2,1,0:T(8,128)(2,1)S(1)}, bf16[4,2,32,512]{3,2,1,0:T(8,128)(2,1)S(1)}, u32[]{:S(2)}, u32[]{:S(2)}) collective-permute-start(bf16[4,2,32,512]{3,2,1,0:T(8,128)(2,1)S(1)} %get-tuple-element.57), channel_id=1, source_target_pairs={{0,4},{1,5},{2,6},{3,7},{4,0},{5,1},{6,2},{7,3},{8,12},{9,13},{10,... | collective-permute-start | bytes 786440 | tf_op jit(solution)/shard_map/in2_z1/ppermute | solution.py:345
  58.5 21.8 %collective-permute-start.9 = (bf16[4,2,32,512]{3,2,1,0:T(8,128)(2,1)S(1)}, bf16[4,2,32,512]{3,2,1,0:T(8,128)(2,1)S(1)}, u32[]{:S(2)}, u32[]{:S(2)}) collective-permute-start(bf16[4,2,32,512]{3,2,1,0:T(8,128)(2,1)S(1)} %get-tuple-element.49.refs_2_), channel_id=1, source_target_pairs={{0,8},{1,9},{2,10},{3,11},{4,12},{5,13},{6,14},{7,15},{8,0},{9,1},... | collective-permute-start | bytes 786440 | tf_op jit(solution)/shard_map/in2_z2/ppermute | solution.py:345
  62.8 4.2 %collective-permute-start.6 = (bf16[2,4,4,2,32,512]{5,4,3,2,1,0:T(8,128)(2,1)S(1)}, bf16[2,4,4,2,32,512]{5,4,3,2,1,0:T(8,128)(2,1)S(1)}, u32[]{:S(2)}, u32[]{:S(2)}) collective-permute-start(bf16[2,4,4,2,32,512]{5,4,3,2,1,0:T(8,128)(2,1)S(1)} %join.9.refs_4_), channel_id=1, source_target_pairs={{0,1},{1,0},{2,3},{3,2},{4,5},{5,4},{6,7},{7,6},{8,9},{9,8},{10,11... | collective-permute-start | bytes 6291464 | tf_op jit(solution)/shard_map/in0_core/ppermute | solution.py:345
  63.0 25.6 %collective-permute-start.14 = (bf16[4,4,2,32,512]{4,3,2,1,0:T(8,128)(2,1)S(1)}, bf16[4,4,2,32,512]{4,3,2,1,0:T(8,128)(2,1)S(1)}, u32[]{:S(2)}, u32[]{:S(2)}) collective-permute-start(bf16[4,4,2,32,512]{4,3,2,1,0:T(8,128)(2,1)S(1)} %join.10.refs_0_), channel_id=1, source_target_pairs={{0,2},{1,3},{2,0},{3,1},{4,6},{5,7},{6,4},{7,5},{8,10},{9,11},{10,... | collective-permute-start | bytes 3145736 | tf_op jit(solution)/shard_map/in1_y/ppermute | solution.py:345
  64.9 25.6 %collective-permute-start.12 = (bf16[4,2,32,512]{3,2,1,0:T(8,128)(2,1)S(1)}, bf16[4,2,32,512]{3,2,1,0:T(8,128)(2,1)S(1)}, u32[]{:S(2)}, u32[]{:S(2)}) collective-permute-start(bf16[4,2,32,512]{3,2,1,0:T(8,128)(2,1)S(1)} %relayout.12.refs_3_), channel_id=1, source_target_pairs={{0,12},{1,13},{2,14},{3,15},{4,8},{5,9},{6,10},{7,11},{8,4},{9,5},... | collective-permute-start | bytes 786440 | tf_op jit(solution)/shard_map/in3_z3/ppermute | solution.py:345
  80.9 33.9 %collective-permute-start.10 = (bf16[4,2,32,512]{3,2,1,0:T(8,128)(2,1)S(1)}, bf16[4,2,32,512]{3,2,1,0:T(8,128)(2,1)S(1)}, u32[]{:S(2)}, u32[]{:S(2)}) collective-permute-start(bf16[4,2,32,512]{3,2,1,0:T(8,128)(2,1)S(1)} %get-tuple-element.54), channel_id=1, source_target_pairs={{0,4},{1,5},{2,6},{3,7},{4,0},{5,1},{6,2},{7,3},{8,12},{9,13},{10,... | collective-permute-start | bytes 786440 | tf_op jit(solution)/shard_map/in3_z1/ppermute | solution.py:345
  80.9 21.8 %collective-permute-start.11 = (bf16[4,2,32,512]{3,2,1,0:T(8,128)(2,1)S(1)}, bf16[4,2,32,512]{3,2,1,0:T(8,128)(2,1)S(1)}, u32[]{:S(2)}, u32[]{:S(2)}) collective-permute-start(bf16[4,2,32,512]{3,2,1,0:T(8,128)(2,1)S(1)} %get-tuple-element.55.refs_2_), channel_id=1, source_target_pairs={{0,8},{1,9},{2,10},{3,11},{4,12},{5,13},{6,14},{7,15},{8,0},{9,1},... | collective-permute-start | bytes 786440 | tf_op jit(solution)/shard_map/in3_z2/ppermute | solution.py:345
  88.8 4.2 %collective-permute-start.16 = (bf16[2,4,4,2,32,512]{5,4,3,2,1,0:T(8,128)(2,1)S(1)}, bf16[2,4,4,2,32,512]{5,4,3,2,1,0:T(8,128)(2,1)S(1)}, u32[]{:S(2)}, u32[]{:S(2)}) collective-permute-start(bf16[2,4,4,2,32,512]{5,4,3,2,1,0:T(8,128)(2,1)S(1)} %join.11.refs_4_), channel_id=1, source_target_pairs={{0,1},{1,0},{2,3},{3,2},{4,5},{5,4},{6,7},{7,6},{8,9},{9,8},{10,11... | collective-permute-start | bytes 6291464 | tf_op jit(solution)/shard_map/in1_core/ppermute | solution.py:345
  88.9 25.6 %collective-permute-start.15 = (bf16[4,4,2,32,512]{4,3,2,1,0:T(8,128)(2,1)S(1)}, bf16[4,4,2,32,512]{4,3,2,1,0:T(8,128)(2,1)S(1)}, u32[]{:S(2)}, u32[]{:S(2)}) collective-permute-start(bf16[4,4,2,32,512]{4,3,2,1,0:T(8,128)(2,1)S(1)} %join.12.refs_1_.refs_0_), channel_id=1, source_target_pairs={{0,2},{1,3},{2,0},{3,1},{4,6},{5,7},{6,4},{7,5},{8,10},{9,11},{10,... | collective-permute-start | bytes 3145736 | tf_op jit(solution)/shard_map/in2_y/ppermute | solution.py:345
  90.5 19.4 %collective-permute-start.17 = (bf16[4,2,32,512]{3,2,1,0:T(8,128)(2,1)S(1)}, bf16[4,2,32,512]{3,2,1,0:T(8,128)(2,1)S(1)}, u32[]{:S(2)}, u32[]{:S(2)}) collective-permute-start(bf16[4,2,32,512]{3,2,1,0:T(8,128)(2,1)S(1)} %release.8.refs_3_), channel_id=1, source_target_pairs={{0,8},{1,9},{2,10},{3,11},{4,12},{5,13},{6,14},{7,15},{8,0},{9,1},... | collective-permute-start | bytes 786440 | tf_op jit(solution)/shard_map/out0_z2/ppermute | solution.py:345
  102.8 28.4 %collective-permute-start.21 = (bf16[4,2,32,512]{3,2,1,0:T(8,128)(2,1)S(1)}, bf16[4,2,32,512]{3,2,1,0:T(8,128)(2,1)S(1)}, u32[]{:S(2)}, u32[]{:S(2)}) collective-permute-start(bf16[4,2,32,512]{3,2,1,0:T(8,128)(2,1)S(1)} %get-tuple-element.69), channel_id=1, source_target_pairs={{0,4},{1,5},{2,6},{3,7},{4,0},{5,1},{6,2},{7,3},{8,12},{9,13},{10,... | collective-permute-start | bytes 786440 | tf_op jit(solution)/shard_map/out0_z1/ppermute | solution.py:345
  102.9 15.5 %collective-permute-start.20 = (bf16[4,2,32,512]{3,2,1,0:T(8,128)(2,1)S(1)}, bf16[4,2,32,512]{3,2,1,0:T(8,128)(2,1)S(1)}, u32[]{:S(2)}, u32[]{:S(2)}) collective-permute-start(bf16[4,2,32,512]{3,2,1,0:T(8,128)(2,1)S(1)} %get-tuple-element.63.refs_1_), channel_id=1, source_target_pairs={{0,12},{1,13},{2,14},{3,15},{4,8},{5,9},{6,10},{7,11},{8,4},{9,5},... | collective-permute-start | bytes 786440 | tf_op jit(solution)/shard_map/out0_z3/ppermute | solution.py:345
  110.0 22.3 %collective-permute-start.22 = (bf16[4,2,32,512]{3,2,1,0:T(8,128)(2,1)S(1)}, bf16[4,2,32,512]{3,2,1,0:T(8,128)(2,1)S(1)}, u32[]{:S(2)}, u32[]{:S(2)}) collective-permute-start(bf16[4,2,32,512]{3,2,1,0:T(8,128)(2,1)S(1)} %release.10.refs_2_), channel_id=1, source_target_pairs={{0,12},{1,13},{2,14},{3,15},{4,8},{5,9},{6,10},{7,11},{8,4},{9,5},... | collective-permute-start | bytes 786440 | tf_op jit(solution)/shard_map/out1_z3/ppermute | solution.py:345
  114.7 11.3 %collective-permute-start.19 = (bf16[2,4,4,2,32,512]{5,4,3,2,1,0:T(8,128)(2,1)S(1)}, bf16[2,4,4,2,32,512]{5,4,3,2,1,0:T(8,128)(2,1)S(1)}, u32[]{:S(2)}, u32[]{:S(2)}) collective-permute-start(bf16[2,4,4,2,32,512]{5,4,3,2,1,0:T(8,128)(2,1)S(1)} %join.13.refs_4_), channel_id=1, source_target_pairs={{0,1},{1,0},{2,3},{3,2},{4,5},{5,4},{6,7},{7,6},{8,9},{9,8},{10,11... | collective-permute-start | bytes 6291464 | tf_op jit(solution)/shard_map/in2_core/ppermute | solution.py:345
  114.9 25.8 %collective-permute-start.18 = (bf16[4,4,2,32,512]{4,3,2,1,0:T(8,128)(2,1)S(1)}, bf16[4,4,2,32,512]{4,3,2,1,0:T(8,128)(2,1)S(1)}, u32[]{:S(2)}, u32[]{:S(2)}) collective-permute-start(bf16[4,4,2,32,512]{4,3,2,1,0:T(8,128)(2,1)S(1)} %join.14.refs_3_.refs_0_), channel_id=1, source_target_pairs={{0,2},{1,3},{2,0},{3,1},{4,6},{5,7},{6,4},{7,5},{8,10},{9,11},{10,... | collective-permute-start | bytes 3145736 | tf_op jit(solution)/shard_map/in3_y/ppermute | solution.py:345
  118.4 37.5 %collective-permute-start.25 = (bf16[4,2,32,512]{3,2,1,0:T(8,128)(2,1)S(1)}, bf16[4,2,32,512]{3,2,1,0:T(8,128)(2,1)S(1)}, u32[]{:S(2)}, u32[]{:S(2)}) collective-permute-start(bf16[4,2,32,512]{3,2,1,0:T(8,128)(2,1)S(1)} %get-tuple-element.79), channel_id=1, source_target_pairs={{0,4},{1,5},{2,6},{3,7},{4,0},{5,1},{6,2},{7,3},{8,12},{9,13},{10,... | collective-permute-start | bytes 786440 | tf_op jit(solution)/shard_map/out1_z1/ppermute | solution.py:345
  126.0 21.8 %collective-permute-start.24 = (bf16[4,2,32,512]{3,2,1,0:T(8,128)(2,1)S(1)}, bf16[4,2,32,512]{3,2,1,0:T(8,128)(2,1)S(1)}, u32[]{:S(2)}, u32[]{:S(2)}) collective-permute-start(bf16[4,2,32,512]{3,2,1,0:T(8,128)(2,1)S(1)} %get-tuple-element.66.refs_3_), channel_id=1, source_target_pairs={{0,8},{1,9},{2,10},{3,11},{4,12},{5,13},{6,14},{7,15},{8,0},{9,1},... | collective-permute-start | bytes 786440 | tf_op jit(solution)/shard_map/out1_z2/ppermute | solution.py:345
  132.3 24.6 %collective-permute-start.26 = (bf16[4,2,32,512]{3,2,1,0:T(8,128)(2,1)S(1)}, bf16[4,2,32,512]{3,2,1,0:T(8,128)(2,1)S(1)}, u32[]{:S(2)}, u32[]{:S(2)}) collective-permute-start(bf16[4,2,32,512]{3,2,1,0:T(8,128)(2,1)S(1)} %release.12.refs_2_), channel_id=1, source_target_pairs={{0,8},{1,9},{2,10},{3,11},{4,12},{5,13},{6,14},{7,15},{8,0},{9,1},... | collective-permute-start | bytes 786440 | tf_op jit(solution)/shard_map/out2_z2/ppermute | solution.py:345
  140.8 11.1 %collective-permute-start.23 = (bf16[2,4,4,2,32,512]{5,4,3,2,1,0:T(8,128)(2,1)S(1)}, bf16[2,4,4,2,32,512]{5,4,3,2,1,0:T(8,128)(2,1)S(1)}, u32[]{:S(2)}, u32[]{:S(2)}) collective-permute-start(bf16[2,4,4,2,32,512]{5,4,3,2,1,0:T(8,128)(2,1)S(1)} %join.15.refs_3_), channel_id=1, source_target_pairs={{0,1},{1,0},{2,3},{3,2},{4,5},{5,4},{6,7},{7,6},{8,9},{9,8},{10,11... | collective-permute-start | bytes 6291464 | tf_op jit(solution)/shard_map/in3_core/ppermute | solution.py:345
  147.8 24.4 %collective-permute-start.30 = (bf16[4,2,32,512]{3,2,1,0:T(8,128)(2,1)S(1)}, bf16[4,2,32,512]{3,2,1,0:T(8,128)(2,1)S(1)}, u32[]{:S(2)}, u32[]{:S(2)}) collective-permute-start(bf16[4,2,32,512]{3,2,1,0:T(8,128)(2,1)S(1)} %get-tuple-element.83), channel_id=1, source_target_pairs={{0,4},{1,5},{2,6},{3,7},{4,0},{5,1},{6,2},{7,3},{8,12},{9,13},{10,... | collective-permute-start | bytes 786440 | tf_op jit(solution)/shard_map/out2_z1/ppermute | solution.py:345
  147.9 14.1 %collective-permute-start.27 = (bf16[4,2,32,512]{3,2,1,0:T(8,128)(2,1)S(1)}, bf16[4,2,32,512]{3,2,1,0:T(8,128)(2,1)S(1)}, u32[]{:S(2)}, u32[]{:S(2)}) collective-permute-start(bf16[4,2,32,512]{3,2,1,0:T(8,128)(2,1)S(1)} %get-tuple-element.73.refs_3_), channel_id=1, source_target_pairs={{0,12},{1,13},{2,14},{3,15},{4,8},{5,9},{6,10},{7,11},{8,4},{9,5},... | collective-permute-start | bytes 786440 | tf_op jit(solution)/shard_map/out2_z3/ppermute | solution.py:345
  156.9 20.8 %collective-permute-start.29 = (bf16[4,2,32,512]{3,2,1,0:T(8,128)(2,1)S(1)}, bf16[4,2,32,512]{3,2,1,0:T(8,128)(2,1)S(1)}, u32[]{:S(2)}, u32[]{:S(2)}) collective-permute-start(bf16[4,2,32,512]{3,2,1,0:T(8,128)(2,1)S(1)} %release.14.refs_3_), channel_id=1, source_target_pairs={{0,12},{1,13},{2,14},{3,15},{4,8},{5,9},{6,10},{7,11},{8,4},{9,5},... | collective-permute-start | bytes 786440 | tf_op jit(solution)/shard_map/out3_z3/ppermute | solution.py:345
  162.1 15.6 %collective-permute-start.28 = (bf16[4,2,32,512]{3,2,1,0:T(8,128)(2,1)S(1)}, bf16[4,2,32,512]{3,2,1,0:T(8,128)(2,1)S(1)}, u32[]{:S(2)}, u32[]{:S(2)}) collective-permute-start(bf16[4,2,32,512]{3,2,1,0:T(8,128)(2,1)S(1)} %get-tuple-element.81), channel_id=1, source_target_pairs={{0,4},{1,5},{2,6},{3,7},{4,0},{5,1},{6,2},{7,3},{8,12},{9,13},{10,... | collective-permute-start | bytes 786440 | tf_op jit(solution)/shard_map/out3_z1/ppermute | solution.py:345
  170.9 15.2 %collective-permute-start.31 = (bf16[4,2,32,512]{3,2,1,0:T(8,128)(2,1)S(1)}, bf16[4,2,32,512]{3,2,1,0:T(8,128)(2,1)S(1)}, u32[]{:S(2)}, u32[]{:S(2)}) collective-permute-start(bf16[4,2,32,512]{3,2,1,0:T(8,128)(2,1)S(1)} %get-tuple-element.84.refs_3_), channel_id=1, source_target_pairs={{0,8},{1,9},{2,10},{3,11},{4,12},{5,13},{6,14},{7,15},{8,0},{9,1},... | collective-permute-start | bytes 786440 | tf_op jit(solution)/shard_map/out3_z2/ppermute | solution.py:345
  (7 other events, 45.4 us)
